TPU v7x, 32 devices: a whole 2x2x4 slice. The times are simulated.
32 devices in a mesh: sa: 4 (over x, core), an: 8 (over z, y).
Axes of the slice: x: 2, y: 2, z: 4, core: 2. Of those that a mesh axis runs over, the one named last changes fastest.
Arguments:
- decoder_states: bfloat16 [4096, 4096], P('sa', 'an'), may hold values from -170 to 170
- w_query: bfloat16 [4096, 4096], P(None, 'an'), may hold values from -0.09375 to 0.09375
- w_key: bfloat16 [1024, 4096], P(None, 'an'), may hold values from -0.1875 to 0.1875
- w_value: bfloat16 [1024, 4096], P(None, 'an'), may hold values from -0.1875 to 0.1875
- w_out: bfloat16 [4096, 4096], P('an'), may hold values from -0.375 to 0.375
- enc_up: bfloat16 [1024, 4096], replicated, may hold values from -0.1875 to 0.1875
- enc_down: bfloat16 [4096, 1024], replicated, may hold values from -0.09375 to 0.09375
- neighbour_inputs: bfloat16 [256, 128, 1024], P(('sa', 'an')), may hold values from -6 to 6
- requests: int32 [128], P('sa'), may hold values from 0 to 63, as said below
Outputs:
- cross_output: bfloat16 [4096, 4096], P('sa', 'an')
Inputs may be any that keep to these rules, and one draw needn't show every extreme that they name: Within each block of 32 requests (one index of sa) the owner of a request is its value // 8; no owner receives more than 8 requests of a block and no more than 4 distinct neighbours of one owner are requested in a block; in every block some owner receives exactly 8 requests, 4 of them distinct. A neighbour may be requested several times.
All inputs are finite; a program needn't handle non-finite values.
Results may differ from a plain program's by a relative error of at most 0.01.
The roundings to bfloat16 on the way count: a program that leaves them out, or rounds other values in their place, can miss the bound.
Values may be sent and summed in bfloat16 or wider, within the bound.
No kernel may reach another device: no remote copies, remote signals or barrier semaphores. Data moves between devices by JAX's collectives and lax.ppermute only.
A program may use at most 128 MiB of HBM per device.

v0:
```python
import jax
import jax.numpy as jnp
from jax import lax
from jax.sharding import PartitionSpec as P

D = 4096
HEADS = 32
GROUP = 64
NEIGH = 2


EPS = 1e-06


def encode(rows, enc_up, enc_down):
    wide = rows.astype(jnp.float32)
    square = jnp.mean(wide * wide, axis=-1, keepdims=True)
    normed = (wide * lax.rsqrt(square + EPS)).astype(jnp.bfloat16)
    hidden = jax.nn.gelu(
        jnp.dot(normed, enc_up, preferred_element_type=jnp.float32), approximate=False
    ).astype(jnp.bfloat16)
    return (wide + jnp.dot(hidden, enc_down, preferred_element_type=jnp.float32)).astype(
        jnp.bfloat16
    )


def shards(
    decoder_states, w_query, w_key, w_value, w_out, enc_up, enc_down, neighbour_inputs, requests
):
    owner_total = lax.axis_size("an")
    position = lax.axis_index("an")
    tok_rows, local_width = decoder_states.shape
    head_dim = D // HEADS
    heads_here = local_width // head_dim
    scale = float(head_dim) ** (-0.5)
    total_requests = requests.shape[0]
    per_owner = total_requests // owner_total
    nb_own = neighbour_inputs.shape[0]
    span = neighbour_inputs.shape[1]
    owner = requests // nb_own
    local_id = requests % nb_own
    owner_range = jnp.arange(owner_total, dtype=jnp.int32)
    local_range = jnp.arange(nb_own, dtype=jnp.int32)
    hits = (owner[:, None, None] == owner_range[None, :, None]) & (
        local_id[:, None, None] == local_range[None, None, :]
    )
    present = jnp.any(hits, axis=0).astype(jnp.int32)
    ranked = jnp.cumsum(present, axis=1) - present
    slot_of_request = owner * per_owner + ranked[owner, local_id]
    my_present = jnp.sum(jnp.where(owner_range[:, None] == position, present, 0), axis=0)
    my_rank = jnp.sum(jnp.where(owner_range[:, None] == position, ranked, 0), axis=0)
    chosen_mask = (my_present[:, None] == 1) & (
        my_rank[:, None] == jnp.arange(per_owner, dtype=jnp.int32)[None, :]
    )
    local_of_slot = jnp.sum(jnp.where(chosen_mask, local_range[:, None], 0), axis=0)
    queries = jnp.dot(
        lax.all_gather(decoder_states, "an", axis=1, tiled=True),
        w_query,
        preferred_element_type=jnp.float32,
    )
    chosen = neighbour_inputs[local_of_slot].reshape(per_owner * span, neighbour_inputs.shape[2])
    encoded = encode(chosen, enc_up, enc_down)
    both_weights = jnp.concatenate([w_key, w_value], axis=1)
    projected = jnp.dot(
        lax.all_gather(encoded, "an", axis=0, tiled=True),
        both_weights,
        preferred_element_type=jnp.float32,
    ).astype(jnp.bfloat16)
    projected = projected.reshape(owner_total * per_owner, span, 2 * local_width)
    groups = tok_rows // GROUP
    selected = projected[slot_of_request].reshape(groups, NEIGH * span, 2 * local_width)
    keys = selected[:, :, :local_width].reshape(groups, NEIGH * span, heads_here, head_dim)
    values = selected[:, :, local_width:].reshape(groups, NEIGH * span, heads_here, head_dim)
    queries = queries.astype(jnp.bfloat16).reshape(groups, GROUP, heads_here, head_dim)
    scores = (
        jnp.einsum("cqhd,ckhd->chqk", queries, keys, preferred_element_type=jnp.float32) * scale
    )
    top = jnp.max(scores, axis=-1, keepdims=True)
    weights = jnp.exp(scores - top)
    probs = (weights / jnp.sum(weights, axis=-1, keepdims=True)).astype(jnp.bfloat16)
    attended = jnp.einsum(
        "chqk,ckhd->cqhd", probs, values, preferred_element_type=jnp.float32
    ).astype(jnp.bfloat16)
    attended = attended.reshape(tok_rows, local_width)
    terms = jnp.dot(attended, w_out, preferred_element_type=jnp.float32)
    return lax.psum_scatter(terms, "an", scatter_dimension=1, tiled=True).astype(jnp.bfloat16)


def solution(mesh):
    placed = (
        P("sa", "an"),
        P(None, "an"),
        P(None, "an"),
        P(None, "an"),
        P("an", None),
        P(),
        P(),
        P(("sa", "an"), None, None),
        P("sa"),
    )
    return jax.shard_map(
        shards, mesh=mesh, in_specs=placed, out_specs=P("sa", "an"), check_vma=False
    )
```

profile of v0, /device:TPU:0, one launch (start us, length us, event | category | flops | bytes accessed | tf_op | source)
XLA Modules:
  0.0 623.9 jit_solution(10819456595790160008)
XLA Ops:
  6.5 0.0 copy-start
  6.5 0.0 all-gather.5.cloned.1.call-start
  6.5 0.7 all-gather.5.cloned.1.call-update
  7.3 0.0 all-gather.3.cloned.1.call-start
  7.3 0.7 fusion.41
  8.0 0.2 and_reduce_fusion
  8.2 0.2 reduce_window_sum.11
  8.4 0.1 select_reduce_fusion.1
  8.5 0.1 select_reduce_fusion.2
  8.6 0.0 copy-done
  8.6 0.6 gather_fusion
  9.3 0.3 fusion.19
  9.6 0.2 fusion.20
  9.8 30.8 %fusion.21 = bf16[512,1024]{1,0:T(8,128)(2,1)} fusion(bf16[4,128,1024]{2,1,0:T(8,128)(2,1)S(1)} %gather_fusion, bf16[4096,1024]{1,0:T(8,128)(2,1)} %param.15, bf16[512,1024]{1,0:T(8,128)(2,1)S(1)} %fusion.20, bf16[1024,4096]{1,0:T(8,128)(2,1)} %param.14), kind=kOutput, calls=%fused_computation.37 | convolution fusion | flops 8727822336 | bytes 19922944 | tf_op jit(solution)/shard_map/dot_general | solution.py:22
  40.6 0.0 all-gather.3.cloned.1.call-update
  40.6 0.3 reduce-scatter.2.cloned.1.call-start
  40.9 0.7 gather_fusion.1
  41.6 0.0 copy-start.3
  41.6 95.9 %all-gather.5.cloned.1.call-done = bf16[1024,4096]{1,0:T(8,128)(2,1)} async-done(((bf16[1024,512]{1,0:T(8,128)(2,1)}), bf16[1024,4096]{1,0:T(8,128)(2,1)}) %all-gather.5.cloned.1.call-update) | async-done | bytes 8388624 | tf_op jit(solution)/shard_map/all_gather | solution.py:57
  137.5 9.1 %convolution_convert_fusion.1 = bf16[1024,512]{1,0:T(8,128)(2,1)S(1)} fusion(bf16[1024,4096]{1,0:T(8,128)(2,1)} %all-gather.5.cloned.1.call-done, bf16[4096,512]{1,0:T(8,128)(2,1)} %param.10), kind=kOutput, calls=%fused_computation.41 | convolution fusion | flops 4295491584 | bytes 13631488 | tf_op jit(solution)/shard_map/dot_general | solution.py:56
  146.6 0.3 reshape.112
  146.9 115.9 %all-gather.3.cloned.1.call-done = bf16[4096,1024]{1,0:T(8,128)(2,1)} async-done(((bf16[512,1024]{1,0:T(8,128)(2,1)}), bf16[4096,1024]{1,0:T(8,128)(2,1)}) %all-gather.3.cloned.1.call-update) | async-done | bytes 8388624 | tf_op jit(solution)/shard_map/all_gather | solution.py:65
  262.8 0.0 copy-done.3
  262.8 13.6 %convolution_convert_fusion = bf16[4096,1024]{1,0:T(8,128)(2,1)} fusion(bf16[4096,1024]{1,0:T(8,128)(2,1)} %all-gather.3.cloned.1.call-done, bf16[1024,512]{1,0:T(8,128)(2,1)S(1)} %copy-done.3, bf16[1024,512]{1,0:T(8,128)(2,1)} %param.11), kind=kOutput, calls=%fused_computation.23 | convolution fusion | flops 8598323200 | bytes 18874368 | tf_op jit(solution)/shard_map/dot_general | solution.py:64
  276.4 8.4 %gather_fusion.2 = bf16[32,128,1024]{2,1,0:T(8,128)(2,1)} fusion(bf16[32,128,1024]{2,1,0:T(8,128)(2,1)} %bitcast.43, s32[1024]{0:T(1024)S(1)} %pad_clamp_fusion), kind=kCustom, calls=%fused_computation.2 | custom fusion | bytes 16777344 | tf_op jit(solution)/shard_map/gather | solution.py:71
  284.8 5.8 fusion.79
  290.6 6.4 %copy.22 = bf16[16,256,512]{1,2,0:T(8,128)(2,1)} copy(bf16[16,256,512]{2,1,0:T(8,128)(2,1)} %get-tuple-element.11) | data formatting | bytes 8388608 | tf_op jit(solution)/shard_map/slice | solution.py:72
  297.0 2.9 fusion.31
  299.9 0.0 copy-start.2
  299.9 2.0 copy-done.2
  301.9 1.6 fusion.80
  303.4 6.6 %copy.21 = bf16[16,256,512]{1,2,0:T(8,128)(2,1)} copy(bf16[16,256,512]{2,1,0:T(8,128)(2,1)} %get-tuple-element.12) | data formatting | bytes 8388608 | tf_op jit(solution)/shard_map/slice | solution.py:73
  310.1 11.9 %fusion.27 = bf16[16,64,4,128]{3,1,2,0:T(8,128)(2,1)S(1)} fusion(bf16[16,256,4,128]{1,3,2,0:T(8,128)(2,1)} %bitcast.44, f32[16,4,64]{2,1,0:T(4,128)S(1)} %fusion.80, f32[16,4,64,256]{3,2,1,0:T(8,128)} %copy-done.2), kind=kOutput, calls=%fused_computation.42 | convolution fusion | flops 274206976 | bytes 9453568 | tf_op jit(solution)/shard_map/chqk,ckhd->cqhd/dot_general | solution.py:81
  322.0 0.9 copy.26
  322.9 10.3 %fusion.28 = f32[1024,4096]{1,0:T(8,128)} fusion(bf16[512,4096]{1,0:T(8,128)(2,1)} %param.13, bf16[128,8,4,128]{3,2,1,0:T(4,128)(2,1)S(1)} %bitcast.45), kind=kOutput, calls=%fused_computation.43 | convolution fusion | flops 4294967296 | bytes 22020096 | tf_op jit(solution)/shard_map/dot_general | solution.py:85
  333.2 0.0 copy-start.1
  333.2 0.0 reduce-scatter.2.cloned.1.call-update
  333.2 281.0 %reduce-scatter.2.cloned.1.call-done = f32[1024,512]{1,0:T(8,128)} async-done(((f32[1024,4096]{1,0:T(8,128)}), f32[1024,512]{1,0:T(8,128)}) %reduce-scatter.2.cloned.1.call-update) | async-done | bytes 2097168 | tf_op jit(solution)/shard_map/reduce_scatter | solution.py:86
  614.2 2.7 convert_element_type.51
  616.9 0.0 copy-done.1
  (9 shorter events, 0.1 us)
Async XLA Ops:
  6.5 2.1 copy-start
  6.5 131.0 %all-gather.5.cloned.1.call-start = ((), (), s32[]{:S(2)}) async-start(), calls=%async_computation.2 | async-start | bytes 9437184 | tf_op jit(solution)/shard_map/all_gather | solution.py:57
  7.3 255.6 %all-gather.3.cloned.1.call-start = ((), (), s32[]{:S(2)}) async-start(), calls=%async_computation.1 | async-start | bytes 9437184 | tf_op jit(solution)/shard_map/all_gather | solution.py:65
  40.6 573.6 %reduce-scatter.2.cloned.1.call-start = ((), (), s32[]{:S(2)}) async-start(), calls=%async_computation.3 | async-start | bytes 18874368 | tf_op jit(solution)/shard_map/reduce_scatter | solution.py:86
  41.6 221.2 %copy-start.3 = (bf16[1024,512]{1,0:T(8,128)(2,1)S(1)}, bf16[1024,512]{1,0:T(8,128)(2,1)}, u32[]{:S(2)}) copy-start(bf16[1024,512]{1,0:T(8,128)(2,1)} %param.12) | copy-start | bytes 3145732
  299.9 2.0 copy-start.2
  333.2 283.8 %copy-start.1 = (bf16[8,128,1024]{2,1,0:T(8,128)(2,1)S(1)}, bf16[8,128,1024]{2,1,0:T(8,128)(2,1)}, u32[]{:S(2)}) copy-start(bf16[8,128,1024]{2,1,0:T(8,128)(2,1)} %param.16) | copy-start | bytes 6291460
Sparse Core Ops, SparseCore 0:
  9.4 128.0 all-gather.4
  139.7 123.1 all-gather.2
  333.3 280.8 reduce-scatter.1
where the time goes:
time: 633 us; the launch traced here: 624 us
  waiting for transfers between devices  494 us (78%)
  matrix products  78.5 us (12%)
  local copies, waits for them, and re-layouts  31.7 us (5%)
  between operations  13.7 us (2%)
    reduce_scatter x1, waiting for transfers between devices, shards(): lax.psum_scatter(terms, 'an', scatter_dimension=1, tiled=True)  281 us
    all_gather x1, waiting for transfers between devices, shards(): lax.all_gather(encoded, 'an', axis=0, tiled=True)  116 us
    all_gather x1, waiting for transfers between devices, shards(): lax.all_gather(decoder_states, 'an', axis=1, tiled=True)  95.9 us
    dot_general x1, matrix products, encode(): jnp.dot(hidden, enc_down, preferred_element_type=jnp.float32)  30.8 us
    dot_general x1, matrix products, shards(): jnp.dot(lax.all_gather(encoded, 'an', axis=0, tiled=True), both_weights,...  13.6 us
  transfers between devices with their start and end apart: 3, of which 3 were waited for; matrix products, arithmetic and copies ran while one was open for 7% of the time, Pallas kernels for 0%

commit v1 on v0

v1 whole, which is shorter than its diff:
```python
import functools

import jax
import jax.numpy as jnp
from jax import lax
from jax.experimental import pallas as pl
from jax.experimental.pallas import tpu as pltpu
from jax.sharding import PartitionSpec as P

D = 4096
HEADS = 32
GROUP = 64
NEIGH = 2
EPS = 1e-06
F32 = jnp.float32
BF16 = jnp.bfloat16
VMEM_LIMIT = 56 * 1024 * 1024


def encode_kernel(count, slots, *refs):
    rows = refs[:count]
    up, down, out, wide, normed, total = refs[count:]
    step = pl.program_id(0)
    span = rows[0].shape[1]

    @pl.when(step == 0)
    def _():
        for k in range(count):
            part = pl.ds(k * span, span)
            x = rows[k][0].astype(F32)
            square = jnp.mean(x * x, axis=-1, keepdims=True)
            normed[part, :] = (x * lax.rsqrt(square + EPS)).astype(BF16)
            wide[part, :] = rows[k][0]
        total[...] = jnp.zeros_like(total)

    h = jnp.dot(normed[...], up[...], preferred_element_type=F32)
    h = (0.5 * h * (1.0 + lax.erf(h * (0.5**0.5)))).astype(BF16)
    total[...] += jnp.dot(h, down[...], preferred_element_type=F32)

    @pl.when(step == pl.num_programs(0) - 1)
    def _():
        out[...] = (wide[...].astype(F32) + total[...]).astype(BF16)


def encode(neighbours, slots, up, down):
    count = slots.shape[0]
    _, span, width = neighbours.shape
    hidden = up.shape[1]
    tile = min(512, hidden)
    rows = count * span
    one = [
        pl.BlockSpec((1, span, width), functools.partial(lambda k, i, s: (s[k], 0, 0), k))
        for k in range(count)
    ]
    return pl.pallas_call(
        functools.partial(encode_kernel, count),
        grid_spec=pltpu.PrefetchScalarGridSpec(
            num_scalar_prefetch=1,
            grid=(hidden // tile,),
            in_specs=[
                *one,
                pl.BlockSpec((width, tile), lambda i, s: (0, i)),
                pl.BlockSpec((tile, width), lambda i, s: (i, 0)),
            ],
            out_specs=pl.BlockSpec((rows, width), lambda i, s: (0, 0)),
            scratch_shapes=[
                pltpu.VMEM((rows, width), BF16),
                pltpu.VMEM((rows, width), BF16),
                pltpu.VMEM((rows, width), F32),
            ],
        ),
        out_shape=jax.ShapeDtypeStruct((rows, width), BF16),
        compiler_params=pltpu.CompilerParams(vmem_limit_bytes=VMEM_LIMIT),
        cost_estimate=pl.CostEstimate(
            flops=4 * rows * width * hidden,
            bytes_accessed=4 * width * hidden + 4 * rows * width,
            transcendentals=rows * hidden,
        ),
        name="encode",
    )(slots, *([neighbours] * count), up, down)


def attend_kernel(head_dim, where, *refs):
    blocks = refs[:NEIGH]
    q, wk, wv, out = refs[NEIGH:]
    scale = float(head_dim) ** (-0.5)
    rows = jnp.concatenate([b[0] for b in blocks], axis=0)
    keys = jnp.dot(rows, wk[...], preferred_element_type=F32).astype(BF16)
    values = jnp.dot(rows, wv[...], preferred_element_type=F32).astype(BF16)
    for h in range(q.shape[1] // head_dim):
        cols = slice(h * head_dim, (h + 1) * head_dim)
        scores = (
            lax.dot_general(
                q[:, cols], keys[:, cols], (((1,), (1,)), ((), ())), preferred_element_type=F32
            )
            * scale
        )
        top = jnp.max(scores, axis=-1, keepdims=True)
        weights = jnp.exp(scores - top)
        probs = (weights / jnp.sum(weights, axis=-1, keepdims=True)).astype(BF16)
        out[:, cols] = jnp.dot(probs, values[:, cols], preferred_element_type=F32).astype(BF16)


def attend(where, encoded, queries, wk, wv, head_dim):
    tokens, cols = queries.shape
    groups = tokens // GROUP
    _, span, width = encoded.shape
    one = [
        pl.BlockSpec(
            (1, span, width), functools.partial(lambda k, c, s: (s[c * NEIGH + k], 0, 0), k)
        )
        for k in range(NEIGH)
    ]
    keys = groups * NEIGH * span
    return pl.pallas_call(
        functools.partial(attend_kernel, head_dim),
        grid_spec=pltpu.PrefetchScalarGridSpec(
            num_scalar_prefetch=1,
            grid=(groups,),
            in_specs=[
                *one,
                pl.BlockSpec((GROUP, cols), lambda c, s: (c, 0)),
                pl.BlockSpec((width, cols), lambda c, s: (0, 0)),
                pl.BlockSpec((width, cols), lambda c, s: (0, 0)),
            ],
            out_specs=pl.BlockSpec((GROUP, cols), lambda c, s: (c, 0)),
        ),
        out_shape=jax.ShapeDtypeStruct((tokens, cols), BF16),
        compiler_params=pltpu.CompilerParams(vmem_limit_bytes=VMEM_LIMIT),
        cost_estimate=pl.CostEstimate(
            flops=4 * keys * width * cols + 4 * tokens * NEIGH * span * cols,
            bytes_accessed=2 * keys * width + 4 * width * cols + 4 * tokens * cols,
            transcendentals=tokens * NEIGH * span * (cols // head_dim),
        ),
        name="attend",
    )(where, *([encoded] * NEIGH), queries, wk, wv)


def shards(
    decoder_states, w_query, w_key, w_value, w_out, enc_up, enc_down, neighbour_inputs, requests
):
    n = lax.axis_size("an")
    s_total = lax.axis_size("sa")
    position = lax.axis_index("an")
    length = n // 2
    pair, line = position % 2, position // 2
    first = pair == 0
    tok_rows, local = decoder_states.shape
    half = tok_rows // 2
    head_dim = D // HEADS
    total_requests = requests.shape[0]
    per_owner = total_requests // n
    nb_own, span, width = neighbour_inputs.shape

    def swap_pair(a):
        return lax.ppermute(a, "an", [(i, i ^ 1) for i in range(n)])

    def on_line(a, moves):
        return lax.ppermute(a, "an", [(i * 2 + y, j * 2 + y) for i, j in moves for y in range(2)])

    def line_gather(a):
        if length == 4:
            two = on_line(a, [(i, (i + 2) % 4) for i in range(4)])
            after = on_line(a, [(i + 1, i) for i in range(3)])
            before = on_line(a, [(i, i + 1) for i in range(3)])
            ends = on_line(two, [(2, 3), (1, 0)])
            return [
                a,
                jnp.where(line == 3, ends, after),
                two,
                jnp.where(line == 0, ends, before),
            ]
        out = [a]
        for _ in range(length - 1):
            out.append(on_line(out[-1], [((i + 1) % length, i) for i in range(length)]))
        return out

    def line_sum(part):
        if length == 4:
            one, three = part(1).astype(BF16), part(3).astype(BF16)
            relay = on_line(jnp.where(line == 0, three, one), [(0, 1), (3, 2)])
            after = on_line(one, [(i, i + 1) for i in range(3)])
            before = on_line(three, [(i + 1, i) for i in range(3)])
            mine = part(0)
            two = on_line(
                (part(2) + relay.astype(F32)).astype(BF16), [(i, (i + 2) % 4) for i in range(4)]
            )
            return mine + after.astype(F32) + before.astype(F32) + two.astype(F32)
        total = part(length - 1)
        for d in range(length - 2, -1, -1):
            got = on_line(total.astype(BF16), [(i, (i + 1) % length) for i in range(length)])
            total = got.astype(F32) + part(d)
        return total

    def share(a, axis):
        size = a.shape[axis] // s_total
        piece = lax.dynamic_slice_in_dim(a, lax.axis_index("sa") * size, size, axis)
        pieces = [swap_pair(piece)]
        bit = 1
        while bit < s_total:
            pieces += [
                lax.ppermute(p, "sa", [(i, i ^ bit) for i in range(s_total)]) for p in pieces
            ]
            bit *= 2
        return pieces

    low, high = decoder_states[:half], decoder_states[half:]
    mine = jnp.where(first, low, high)
    other = swap_pair(jnp.where(first, high, low))
    mine_line = line_gather(mine)
    other_line = line_gather(other)

    owner = requests // nb_own
    local_id = requests % nb_own
    owner_range = jnp.arange(n, dtype=jnp.int32)
    local_range = jnp.arange(nb_own, dtype=jnp.int32)
    hits = (owner[:, None, None] == owner_range[None, :, None]) & (
        local_id[:, None, None] == local_range[None, None, :]
    )
    present = jnp.max(hits.astype(jnp.int32), axis=0)
    earlier = (local_range[None, :] < local_range[:, None]).astype(jnp.int32)
    ranked = jnp.sum(present[:, None, :] * earlier[None, :, :], axis=2)
    rank_of_request = jnp.sum(jnp.where(hits, ranked[None], 0), axis=(1, 2))
    is_me = owner_range[:, None] == position
    my_present = jnp.sum(jnp.where(is_me, present, 0), axis=0)
    my_rank = jnp.sum(jnp.where(is_me, ranked, 0), axis=0)
    chosen_mask = (my_present[:, None] == 1) & (
        my_rank[:, None] == jnp.arange(per_owner, dtype=jnp.int32)[None, :]
    )
    local_of_slot = jnp.sum(jnp.where(chosen_mask, local_range[:, None], 0), axis=0)
    distance = (owner // 2 - line + length) % length
    crossed = (owner % 2 != pair).astype(jnp.int32)
    where = (distance * 2 + crossed) * per_owner + rank_of_request
    where = jnp.where(first, where[: total_requests // 2], where[total_requests // 2 :])

    key_pieces, value_pieces = share(w_key, 1), share(w_value, 1)
    query_pieces = share(w_query, 1)
    out_pieces = share(w_out, 0)
    wk = jnp.concatenate([w_key, *key_pieces], axis=1)
    wv = jnp.concatenate([w_value, *value_pieces], axis=1)
    wq = jnp.concatenate([w_query, *query_pieces], axis=1)
    wo = jnp.concatenate([w_out, *out_pieces], axis=0)

    encoded = encode(neighbour_inputs, local_of_slot, enc_up, enc_down)
    blocks = []
    for block in line_gather(encoded):
        blocks += [block, swap_pair(block)]
    everything = jnp.concatenate(blocks, axis=0).reshape(n * per_owner, span, width)

    queries = 0.0
    for d in range(length):
        place = (line + d) % length
        for x, y in ((mine_line[d], pair), (other_line[d], 1 - pair)):
            rows = lax.dynamic_slice_in_dim(wq, (place * 2 + y) * local, local, 0)
            queries = queries + jnp.dot(x, rows, preferred_element_type=F32)
    queries = queries.astype(BF16)

    attended = attend(where, everything, queries, wk, wv, head_dim)

    def part(d):
        place = (line + d) % length
        cols = lax.dynamic_slice_in_dim(wo, place * 2 * local, 2 * local, 1)
        return jnp.dot(attended, cols, preferred_element_type=F32)

    summed = line_sum(part).astype(BF16)
    left, right = summed[:, :local], summed[:, local:]
    keep = jnp.where(first, left, right)
    got = swap_pair(jnp.where(first, right, left))
    return jnp.concatenate([jnp.where(first, keep, got), jnp.where(first, got, keep)], axis=0)


def solution(mesh):
    placed = (
        P("sa", "an"),
        P(None, "an"),
        P(None, "an"),
        P(None, "an"),
        P("an", None),
        P(),
        P(),
        P(("sa", "an"), None, None),
        P("sa"),
    )
    return jax.shard_map(
        shards, mesh=mesh, in_specs=placed, out_specs=P("sa", "an"), check_vma=False
    )
```

time: 633 us -> 374 us (0.59); the launches traced: 624 us -> 373 us
  waiting for transfers between devices: 494 us -> 206 us
  matrix products: 78.5 us -> 23.2 us
  starting transfers between devices: 0.29 us -> 49.7 us
  Pallas kernels: 0 us -> 48.1 us
  between operations: 13.7 us -> 0.49 us
    reduce_scatter x1 -> x0, waiting for transfers between devices: 281 us -> none  [shards(): lax.psum_scatter(terms, 'an', scatter_dimension=1, tiled=True)]
    all_gather x2 -> x0, waiting for transfers between devices: 212 us -> none  [the longest x1 116 us: shards(): lax.all_gather(encoded, 'an', axis=0, tiled=True)]
    ppermute x0 -> x38, waiting for transfers between devices: none -> 206 us  [the longest x16 119 us: on_line(): lax.ppermute(a, 'an', [(i * 2 + y, j * 2 + y) for i, j in moves for y in...]
    dot_general x6 -> x12, matrix products: 78.5 us -> 23.2 us  [the longest x4 16 us: part(): return jnp.dot(attended, cols, preferred_element_type=F32)]
    ppermute x0 -> x38, starting transfers between devices: none -> 49.7 us  [the longest x16 28.8 us: on_line(): lax.ppermute(a, 'an', [(i * 2 + y, j * 2 + y) for i, j in moves for y in...]
    pallas_call x0 -> x2, Pallas kernels: none -> 48.1 us  [the longest x1 32.4 us: attend(): pl.pallas_call(functools.partial(attend_kernel, head_dim), grid_spec=pltp...]
    unnamed x8 -> x35, local copies, waits for them, and re-layouts: 1.98 us -> 27.6 us
    slice x3 -> x0, local copies, waits for them, and re-layouts: 18.8 us -> none  [the longest x2 12.2 us: shards(): selected[:, :, :local_width]]
  transfers between devices with their start and end apart: 3 -> 38, of which waited for: 3 -> 20; matrix products, arithmetic and copies ran while one was open for 7% -> 14% of each run, Pallas kernels for 0% -> 4%
where the time goes in v1:
time: 374 us; the launch traced here: 373 us
  waiting for transfers between devices  206 us (55%)
  starting transfers between devices  49.7 us (13%)
  Pallas kernels  48.1 us (13%)
  local copies, waits for them, and re-layouts  35.1 us (9%)
  matrix products  23.2 us (6%)
  other arithmetic  9.89 us (3%)
    ppermute x16, waiting for transfers between devices, on_line(): lax.ppermute(a, 'an', [(i * 2 + y, j * 2 + y) for i, j in moves for y in...  119 us
    ppermute x12, waiting for transfers between devices, share(): lax.ppermute(p, 'sa', [(i, i ^ bit) for i in range(s_total)])  49.5 us
    ppermute x10, waiting for transfers between devices, swap_pair(): return lax.ppermute(a, 'an', [(i, i ^ 1) for i in range(n)])  37.3 us
    pallas_call x1, Pallas kernels, attend(): pl.pallas_call(functools.partial(attend_kernel, head_dim), grid_spec=pltp...  32.4 us
    ppermute x16, starting transfers between devices, on_line(): lax.ppermute(a, 'an', [(i * 2 + y, j * 2 + y) for i, j in moves for y in...  28.8 us
    unnamed x35, local copies, waits for them, and re-layouts  27.6 us
    dot_general x4, matrix products, part(): return jnp.dot(attended, cols, preferred_element_type=F32)  16 us
    pallas_call x1, Pallas kernels, encode(): pl.pallas_call(functools.partial(encode_kernel, count), grid_spec=pltpu.P...  15.7 us
  transfers between devices with their start and end apart: 38, of which 20 were waited for; matrix products, arithmetic and copies ran while one was open for 14% of the time, Pallas kernels for 4%

profile of v1, /device:TPU:0, one launch (start us, length us, event | category | flops | bytes accessed | tf_op | source)
XLA Modules:
  0.0 372.6 jit_solution(3359390871251957617)
XLA Ops:
  0.0 2.3 constant_dynamic-slice_fusion.3
  2.3 3.0 collective-permute-start.8
  7.1 15.7 %encode.1 = bf16[512,1024]{1,0:T(8,128)(2,1)} custom-call(s32[4]{0:T(128)} %select_reduce_fusion.2.slots, bf16[8,128,1024]{2,1,0:T(8,128)(2,1)} %refs_3_.1, bf16[8,128,1024]{2,1,0:T(8,128)(2,1)} %refs_3_.1, bf16[8,128,1024]{2,1,0:T(8,128)(2,1)} %refs_3_.1, bf16[8,128,1024]{2,1,0:T(8,128)(2,1)} %refs_3_.1, bf16[1024,4096]{1,0:T(8,128)(2,1)} %refs_4_.1, ...), custom_call_target="tpu_custom_call" | custom-call | flops 8589934592 | bytes 18874368 | tf_op jit(solution)/shard_map/encode/pallas_call | solution.py:55
  22.8 3.2 collective-permute-start.1
  27.1 1.7 collective-permute-start.25
  28.8 4.8 %constant_dynamic-update-slice_fusion.12 = bf16[4096,1024]{1,0:T(8,128)(2,1)} fusion(bf16[4096,512]{1,0:T(8,128)(2,1)} %param.10), kind=kLoop, calls=%fused_computation.58 | loop fusion | bytes 8388608
  34.8 2.3 constant_dynamic-update-slice_fusion.27
  39.0 2.3 constant_dynamic-update-slice_fusion.7
  42.6 1.6 collective-permute-start.23
  44.3 1.7 constant_dynamic-update-slice_fusion.16
  47.6 1.7 constant_dynamic-update-slice_fusion.15
  49.3 2.7 collective-permute-done.23
  54.0 3.6 collective-permute-done.27
  57.7 1.5 collective-permute-start.28
  60.0 3.2 collective-permute-done.24
  64.4 3.9 %collective-permute-done.28 = bf16[1024,128]{1,0:T(8,128)(2,1)S(1)} collective-permute-done((bf16[1024,128]{1,0:T(8,128)(2,1)S(1)}, bf16[1024,128]{1,0:T(8,128)(2,1)S(1)}, u32[]{:S(2)}, u32[]{:S(2)}) %collective-permute-start.28) | collective-permute-done | bytes 262176 | tf_op jit(solution)/shard_map/ppermute | solution.py:202
  69.8 1.9 collective-permute-done.1
  73.0 2.3 constant_dynamic-update-slice_fusion.11
  75.3 3.0 collective-permute-done.29
  78.3 1.5 collective-permute-start.10
  80.9 18.0 %collective-permute-done = bf16[512,1024]{1,0:T(8,128)(2,1)S(1)} collective-permute-done((bf16[512,1024]{1,0:T(8,128)(2,1)S(1)}, bf16[512,1024]{1,0:T(8,128)(2,1)S(1)}, u32[]{:S(2)}, u32[]{:S(2)}) %collective-permute-start) | collective-permute-done | bytes 1048608 | tf_op jit(solution)/shard_map/ppermute | solution.py:156
  100.0 28.7 %collective-permute-done.2 = bf16[512,1024]{1,0:T(8,128)(2,1)S(1)} collective-permute-done((bf16[512,1024]{1,0:T(8,128)(2,1)}, bf16[512,1024]{1,0:T(8,128)(2,1)S(1)}, u32[]{:S(2)}, u32[]{:S(2)}) %collective-permute-start.2) | collective-permute-done | bytes 1048608 | tf_op jit(solution)/shard_map/ppermute | solution.py:159
  133.3 1.6 collective-permute-start.19
  136.0 18.8 %collective-permute-done.31 = bf16[128,4096]{1,0:T(8,128)(2,1)S(1)} collective-permute-done((bf16[128,4096]{1,0:T(8,128)(2,1)S(1)}, bf16[128,4096]{1,0:T(8,128)(2,1)S(1)}, u32[]{:S(2)}, u32[]{:S(2)}) %collective-permute-start.31) | collective-permute-done | bytes 1048608 | tf_op jit(solution)/shard_map/ppermute | solution.py:202
  154.8 1.6 collective-permute-start.6
  157.8 17.1 %collective-permute-done.11 = bf16[4096,128]{1,0:T(8,128)(2,1)S(1)} collective-permute-done((bf16[4096,128]{1,0:T(8,128)(2,1)S(1)}, bf16[4096,128]{1,0:T(8,128)(2,1)S(1)}, u32[]{:S(2)}, u32[]{:S(2)}) %collective-permute-start.11) | collective-permute-done | bytes 1048608 | tf_op jit(solution)/shard_map/ppermute | solution.py:202
  179.4 4.8 %collective-permute-start.16 = (bf16[512,512]{1,0:T(8,128)(2,1)S(1)}, bf16[512,512]{1,0:T(8,128)(2,1)S(1)}, u32[]{:S(2)}, u32[]{:S(2)}) collective-permute-start(bf16[512,512]{1,0:T(8,128)(2,1)S(1)} %collective-permute-done.12), channel_id=1, source_target_pairs={{0,4},{1,5},{2,6},{3,7},{4,0},{5,1},{6,2},{7,3},{8,12},{9,13},{10,... | collective-permute-start | bytes 1572872 | tf_op jit(solution)/shard_map/ppermute | solution.py:159
  184.3 7.5 %collective-permute-done.14 = bf16[512,512]{1,0:T(8,128)(2,1)S(1)} collective-permute-done((bf16[512,512]{1,0:T(8,128)(2,1)S(1)}, bf16[512,512]{1,0:T(8,128)(2,1)S(1)}, u32[]{:S(2)}, u32[]{:S(2)}) %collective-permute-start.14) | collective-permute-done | bytes 524320 | tf_op jit(solution)/shard_map/ppermute | solution.py:159
  194.5 2.3 constant_dynamic-update-slice_fusion.3
  196.8 2.6 collective-permute-done.5
  202.0 14.9 %collective-permute-done.16 = bf16[512,512]{1,0:T(8,128)(2,1)S(1)} collective-permute-done((bf16[512,512]{1,0:T(8,128)(2,1)S(1)}, bf16[512,512]{1,0:T(8,128)(2,1)S(1)}, u32[]{:S(2)}, u32[]{:S(2)}) %collective-permute-start.16) | collective-permute-done | bytes 524320 | tf_op jit(solution)/shard_map/ppermute | solution.py:159
  221.1 1.6 collective-permute-start.7
  225.3 8.2 %collective-permute-done.17 = bf16[512,512]{1,0:T(8,128)(2,1)S(1)} collective-permute-done((bf16[512,512]{1,0:T(8,128)(2,1)S(1)}, bf16[512,512]{1,0:T(8,128)(2,1)S(1)}, u32[]{:S(2)}, u32[]{:S(2)}) %collective-permute-start.17) | collective-permute-done | bytes 524320 | tf_op jit(solution)/shard_map/ppermute | solution.py:159
  235.7 2.1 add_convert_fusion.2.refs_2_
  237.8 6.2 %collective-permute-done.7 = bf16[512,1024]{1,0:T(8,128)(2,1)S(1)} collective-permute-done((bf16[512,1024]{1,0:T(8,128)(2,1)S(1)}, bf16[512,1024]{1,0:T(8,128)(2,1)S(1)}, u32[]{:S(2)}, u32[]{:S(2)}) %collective-permute-start.7) | collective-permute-done | bytes 1048608 | tf_op jit(solution)/shard_map/ppermute | solution.py:156
  245.1 32.4 %attend.1 = bf16[512,1024]{1,0:T(8,128)(2,1)} custom-call(s32[16]{0:T(128)} %broadcast_select_fusion.9.where, bf16[32,128,1024]{2,1,0:T(8,128)(2,1)} %bitcast.9, bf16[32,128,1024]{2,1,0:T(8,128)(2,1)} %bitcast.10, bf16[512,1024]{1,0:T(8,128)(2,1)} %add_convert_fusion.2.refs_2_, bf16[1024,1024]{1,0:T(8,128)(2,1)} %constant_dynamic-update-slice_fusion.13.refs_3_, ...), custom_call_target="tpu_custom_call" | custom-call | flops 9126805504 | bytes 10485760 | tf_op jit(solution)/shard_map/attend/pallas_call | solution.py:115
  277.5 4.2 %fusion.8 = bf16[512,1024]{1,0:T(8,128)(2,1)} fusion(bf16[512,1024]{1,0:T(8,128)(2,1)} %attend.1, bf16[1024,4096]{1,0:T(8,128)(2,1)} %constant_dynamic-update-slice_fusion.23, s32[]{:T(128)S(6)} %select_n.228), kind=kOutput, calls=%fused_computation.11 | convolution fusion | flops 1074266112 | bytes 4194308 | tf_op jit(solution)/shard_map/dot_general | solution.py:263
  281.7 4.2 %broadcast_select_fusion = (bf16[512,1024]{1,0:T(8,128)(2,1)}, bf16[512,1024]{1,0:T(8,128)(2,1)}) fusion(bf16[512,1024]{1,0:T(8,128)(2,1)} %fusion.8, pred[]{:T(512)S(6)} %eq.110, bf16[512,1024]{1,0:T(8,128)(2,1)S(1)} %copy-done.6, bf16[1024,4096]{1,0:T(8,128)(2,1)} %constant_dynamic-update-slice_fusion.23, s32[]{:T(128)S(6)} %select_n.229), kind=kOutput, calls=%fused_computation.29 | convolution fusion | flops 1074790400 | bytes 6291461 | tf_op jit(solution)/shard_map/dot_general | solution.py:263
  285.9 5.6 %collective-permute-start.35 = (bf16[512,1024]{1,0:T(8,128)(2,1)}, bf16[512,1024]{1,0:T(8,128)(2,1)}, u32[]{:S(2)}, u32[]{:S(2)}) collective-permute-start(bf16[512,1024]{1,0:T(8,128)(2,1)} %get-tuple-element.17), channel_id=1, source_target_pairs={{0,2},{1,3},{6,4},{7,5},{8,10},{9,11},{14,12},{15,13},{16,18},{17,... | collective-permute-start | bytes 3145736 | tf_op jit(solution)/shard_map/ppermute | solution.py:159
  294.1 20.3 %collective-permute-done.35 = bf16[512,1024]{1,0:T(8,128)(2,1)} collective-permute-done((bf16[512,1024]{1,0:T(8,128)(2,1)}, bf16[512,1024]{1,0:T(8,128)(2,1)}, u32[]{:S(2)}, u32[]{:S(2)}) %collective-permute-start.35) | collective-permute-done | bytes 1048608 | tf_op jit(solution)/shard_map/ppermute | solution.py:159
  314.4 4.4 %add_convert_fusion.1 = bf16[512,1024]{1,0:T(8,128)(2,1)} fusion(bf16[512,1024]{1,0:T(8,128)(2,1)} %collective-permute-done.35, bf16[512,1024]{1,0:T(8,128)(2,1)} %attend.1, bf16[1024,4096]{1,0:T(8,128)(2,1)} %constant_dynamic-update-slice_fusion.23, s32[]{:T(128)S(6)} %select_n.230), kind=kOutput, calls=%fused_computation.1 | convolution fusion | flops 1075314688 | bytes 5242884 | tf_op jit(solution)/shard_map/dot_general | solution.py:263
  319.1 3.2 fusion.6
  322.3 8.4 %collective-permute-done.34 = bf16[512,1024]{1,0:T(8,128)(2,1)S(1)} collective-permute-done((bf16[512,1024]{1,0:T(8,128)(2,1)}, bf16[512,1024]{1,0:T(8,128)(2,1)S(1)}, u32[]{:S(2)}, u32[]{:S(2)}) %collective-permute-start.34) | collective-permute-done | bytes 1048608 | tf_op jit(solution)/shard_map/ppermute | solution.py:159
  330.6 6.3 %collective-permute-done.33 = bf16[512,1024]{1,0:T(8,128)(2,1)S(1)} collective-permute-done((bf16[512,1024]{1,0:T(8,128)(2,1)}, bf16[512,1024]{1,0:T(8,128)(2,1)S(1)}, u32[]{:S(2)}, u32[]{:S(2)}) %collective-permute-start.33) | collective-permute-done | bytes 1048608 | tf_op jit(solution)/shard_map/ppermute | solution.py:159
  336.9 23.2 %collective-permute-done.36 = bf16[512,1024]{1,0:T(8,128)(2,1)} collective-permute-done((bf16[512,1024]{1,0:T(8,128)(2,1)}, bf16[512,1024]{1,0:T(8,128)(2,1)}, u32[]{:S(2)}, u32[]{:S(2)}) %collective-permute-start.36) | collective-permute-done | bytes 1048608 | tf_op jit(solution)/shard_map/ppermute | solution.py:159
  360.1 2.0 add_convert_fusion
  362.2 1.7 collective-permute-start.37
  363.9 7.5 %collective-permute-done.37 = bf16[512,512]{1,0:T(8,128)(2,1)S(1)} collective-permute-done((bf16[512,512]{1,0:T(8,128)(2,1)S(1)}, bf16[512,512]{1,0:T(8,128)(2,1)S(1)}, u32[]{:S(2)}, u32[]{:S(2)}) %collective-permute-start.37) | collective-permute-done | bytes 524320 | tf_op jit(solution)/shard_map/ppermute | solution.py:156
  (105 shorter events, 48.8 us)
Async XLA Ops:
  2.3 67.5 %collective-permute-start.8 = (bf16[4096,128]{1,0:T(8,128)(2,1)}, bf16[4096,128]{1,0:T(8,128)(2,1)}, u32[]{:S(2)}, u32[]{:S(2)}) collective-permute-start(bf16[4096,128]{1,0:T(8,128)(2,1)} %constant_dynamic-slice_fusion.3), channel_id=1, source_target_pairs={{0,1},{1,0},{2,3},{3,2},{4,5},{5,4},{6,7},{7,6},{8,9},{9,8},{10,11... | collective-permute-start | bytes 3145736 | tf_op jit(solution)/shard_map/ppermute | solution.py:156
  7.1 18.9 %copy-start.2 = (bf16[1024,512]{1,0:T(8,128)(2,1)S(1)}, bf16[1024,512]{1,0:T(8,128)(2,1)}, u32[]{:S(2)}) copy-start(bf16[1024,512]{1,0:T(8,128)(2,1)} %param.11) | copy-start | bytes 3145732
  7.1 20.0 %copy-start.3 = (bf16[1024,512]{1,0:T(8,128)(2,1)S(1)}, bf16[1024,512]{1,0:T(8,128)(2,1)}, u32[]{:S(2)}) copy-start(bf16[1024,512]{1,0:T(8,128)(2,1)} %param.12) | copy-start | bytes 3145732
  22.8 48.9 %collective-permute-start.1 = (bf16[512,1024]{1,0:T(8,128)(2,1)}, bf16[512,1024]{1,0:T(8,128)(2,1)}, u32[]{:S(2)}, u32[]{:S(2)}) collective-permute-start(bf16[512,1024]{1,0:T(8,128)(2,1)} %encode.1), channel_id=1, source_target_pairs={{0,4},{1,5},{2,6},{3,7},{4,0},{5,1},{6,2},{7,3},{8,12},{9,13},{10,... | collective-permute-start | bytes 3145736 | tf_op jit(solution)/shard_map/ppermute | solution.py:159
  26.7 15.6 %collective-permute-start.21 = (bf16[1024,128]{1,0:T(8,128)(2,1)}, bf16[1024,128]{1,0:T(8,128)(2,1)}, u32[]{:S(2)}, u32[]{:S(2)}) collective-permute-start(bf16[1024,128]{1,0:T(8,128)(2,1)} %constant_dynamic-slice_fusion.2), channel_id=1, source_target_pairs={{0,1},{1,0},{2,3},{3,2},{4,5},{5,4},{6,7},{7,6},{8,9},{9,8},{10,11... | collective-permute-start | bytes 786440 | tf_op jit(solution)/shard_map/ppermute | solution.py:156
  27.1 17.1 %collective-permute-start.25 = (bf16[1024,128]{1,0:T(8,128)(2,1)S(1)}, bf16[1024,128]{1,0:T(8,128)(2,1)}, u32[]{:S(2)}, u32[]{:S(2)}) collective-permute-start(bf16[1024,128]{1,0:T(8,128)(2,1)S(1)} %constant_dynamic-slice_fusion.1), channel_id=1, source_target_pairs={{0,1},{1,0},{2,3},{3,2},{4,5},{5,4},{6,7},{7,6},{8,9},{9,8},{10,11... | collective-permute-start | bytes 786440 | tf_op jit(solution)/shard_map/ppermute | solution.py:156
  28.8 4.9 %copy-start.1 = (bf16[512,4096]{1,0:T(8,128)(2,1)S(1)}, bf16[512,4096]{1,0:T(8,128)(2,1)}, u32[]{:S(2)}) copy-start(bf16[512,4096]{1,0:T(8,128)(2,1)} %param.13) | copy-start | bytes 12582916
  42.3 20.9 %copy-start.4 = (bf16[512,1024]{1,0:T(8,128)(2,1)S(1)}, bf16[512,1024]{1,0:T(8,128)(2,1)}, u32[]{:S(2)}) copy-start(bf16[512,1024]{1,0:T(8,128)(2,1)} %encode.1) | copy-start | bytes 3145732
  42.3 3.7 collective-permute-start.22
  42.6 9.4 %collective-permute-start.23 = (bf16[1024,128]{1,0:T(8,128)(2,1)}, bf16[1024,128]{1,0:T(8,128)(2,1)S(1)}, u32[]{:S(2)}, u32[]{:S(2)}) collective-permute-start(bf16[1024,128]{1,0:T(8,128)(2,1)} %collective-permute-done.21), channel_id=1, source_target_pairs={{0,16},{8,24},{16,0},{24,8},{1,17},{9,25},{17,1},{25,9},{2,18},{10... | collective-permute-start | bytes 786440 | tf_op jit(solution)/shard_map/ppermute | solution.py:202
  44.2 8.2 %collective-permute-start.26 = (bf16[1024,128]{1,0:T(8,128)(2,1)}, bf16[1024,128]{1,0:T(8,128)(2,1)S(1)}, u32[]{:S(2)}, u32[]{:S(2)}) collective-permute-start(bf16[1024,128]{1,0:T(8,128)(2,1)} %collective-permute-done.25), channel_id=1, source_target_pairs={{0,8},{8,0},{16,24},{24,16},{1,9},{9,1},{17,25},{25,17},{2,10},{10... | collective-permute-start | bytes 786440 | tf_op jit(solution)/shard_map/ppermute | solution.py:202
  46.0 11.6 %collective-permute-start.27 = (bf16[1024,128]{1,0:T(8,128)(2,1)}, bf16[1024,128]{1,0:T(8,128)(2,1)S(1)}, u32[]{:S(2)}, u32[]{:S(2)}) collective-permute-start(bf16[1024,128]{1,0:T(8,128)(2,1)} %collective-permute-done.25), channel_id=1, source_target_pairs={{0,16},{8,24},{16,0},{24,8},{1,17},{9,25},{17,1},{25,9},{2,18},{10... | collective-permute-start | bytes 786440 | tf_op jit(solution)/shard_map/ppermute | solution.py:202
  52.0 26.3 %collective-permute-start.29 = (bf16[128,4096]{1,0:T(8,128)(2,1)}, bf16[128,4096]{1,0:T(8,128)(2,1)S(1)}, u32[]{:S(2)}, u32[]{:S(2)}) collective-permute-start(bf16[128,4096]{1,0:T(8,128)(2,1)} %constant_dynamic-slice_fusion), channel_id=1, source_target_pairs={{0,1},{1,0},{2,3},{3,2},{4,5},{5,4},{6,7},{7,6},{8,9},{9,8},{10,11... | collective-permute-start | bytes 3145736 | tf_op jit(solution)/shard_map/ppermute | solution.py:156
  52.4 10.8 %collective-permute-start.24 = (bf16[1024,128]{1,0:T(8,128)(2,1)}, bf16[1024,128]{1,0:T(8,128)(2,1)S(1)}, u32[]{:S(2)}, u32[]{:S(2)}) collective-permute-start(bf16[1024,128]{1,0:T(8,128)(2,1)} %collective-permute-done.22), channel_id=1, source_target_pairs={{0,16},{8,24},{16,0},{24,8},{1,17},{9,25},{17,1},{25,9},{2,18},{10... | collective-permute-start | bytes 786440 | tf_op jit(solution)/shard_map/ppermute | solution.py:202
  57.7 10.7 %collective-permute-start.28 = (bf16[1024,128]{1,0:T(8,128)(2,1)S(1)}, bf16[1024,128]{1,0:T(8,128)(2,1)S(1)}, u32[]{:S(2)}, u32[]{:S(2)}) collective-permute-start(bf16[1024,128]{1,0:T(8,128)(2,1)S(1)} %collective-permute-done.26), channel_id=1, source_target_pairs={{0,16},{8,24},{16,0},{24,8},{1,17},{9,25},{17,1},{25,9},{2,18},{10... | collective-permute-start | bytes 786440 | tf_op jit(solution)/shard_map/ppermute | solution.py:202
  63.3 35.6 %collective-permute-start = (bf16[512,1024]{1,0:T(8,128)(2,1)S(1)}, bf16[512,1024]{1,0:T(8,128)(2,1)S(1)}, u32[]{:S(2)}, u32[]{:S(2)}) collective-permute-start(bf16[512,1024]{1,0:T(8,128)(2,1)S(1)} %copy-done.4), channel_id=1, source_target_pairs={{0,1},{1,0},{2,3},{3,2},{4,5},{5,4},{6,7},{7,6},{8,9},{9,8},{10,11... | collective-permute-start | bytes 3145736 | tf_op jit(solution)/shard_map/ppermute | solution.py:156
  68.3 31.6 %collective-permute-start.3 = (bf16[512,1024]{1,0:T(8,128)(2,1)S(1)}, bf16[512,1024]{1,0:T(8,128)(2,1)S(1)}, u32[]{:S(2)}, u32[]{:S(2)}) collective-permute-start(bf16[512,1024]{1,0:T(8,128)(2,1)S(1)} %copy-done.4), channel_id=1, source_target_pairs={{2,0},{3,1},{4,2},{5,3},{6,4},{7,5},{10,8},{11,9},{12,10},{13,11},... | collective-permute-start | bytes 3145736 | tf_op jit(solution)/shard_map/ppermute | solution.py:159
  69.7 61.9 %copy-start.5 = (bf16[1024,1024]{1,0:T(8,128)(2,1)}, bf16[1024,1024]{1,0:T(8,128)(2,1)S(1)}, u32[]{:S(2)}) copy-start(bf16[1024,1024]{1,0:T(8,128)(2,1)S(1)} %constant_dynamic-update-slice_fusion.18.refs_4_) | copy-start | bytes 6291460
  69.7 61.9 %collective-permute-start.9 = (bf16[4096,128]{1,0:T(8,128)(2,1)}, bf16[4096,128]{1,0:T(8,128)(2,1)S(1)}, u32[]{:S(2)}, u32[]{:S(2)}) collective-permute-start(bf16[4096,128]{1,0:T(8,128)(2,1)} %collective-permute-done.8), channel_id=1, source_target_pairs={{0,8},{8,0},{16,24},{24,16},{1,9},{9,1},{17,25},{25,17},{2,10},{10... | collective-permute-start | bytes 3145736 | tf_op jit(solution)/shard_map/ppermute | solution.py:202
  71.7 56.9 %collective-permute-start.2 = (bf16[512,1024]{1,0:T(8,128)(2,1)}, bf16[512,1024]{1,0:T(8,128)(2,1)S(1)}, u32[]{:S(2)}, u32[]{:S(2)}) collective-permute-start(bf16[512,1024]{1,0:T(8,128)(2,1)} %collective-permute-done.1), channel_id=1, source_target_pairs={{4,6},{5,7},{2,0},{3,1},{12,14},{13,15},{10,8},{11,9},{20,22},{21,... | collective-permute-start | bytes 3145736 | tf_op jit(solution)/shard_map/ppermute | solution.py:159
  75.3 56.6 %copy-start = (bf16[4096,1024]{1,0:T(8,128)(2,1)S(1)}, bf16[4096,1024]{1,0:T(8,128)(2,1)}, u32[]{:S(2)}) copy-start(bf16[4096,1024]{1,0:T(8,128)(2,1)} %constant_dynamic-update-slice_fusion.11) | copy-start | bytes 25165828
  78.3 54.0 %collective-permute-start.10 = (bf16[4096,128]{1,0:T(8,128)(2,1)}, bf16[4096,128]{1,0:T(8,128)(2,1)S(1)}, u32[]{:S(2)}, u32[]{:S(2)}) collective-permute-start(bf16[4096,128]{1,0:T(8,128)(2,1)} %collective-permute-done.8), channel_id=1, source_target_pairs={{0,16},{8,24},{16,0},{24,8},{1,17},{9,25},{17,1},{25,9},{2,18},{10... | collective-permute-start | bytes 3145736 | tf_op jit(solution)/shard_map/ppermute | solution.py:202
  98.9 58.6 %collective-permute-start.13 = (bf16[512,512]{1,0:T(8,128)(2,1)S(1)}, bf16[512,512]{1,0:T(8,128)(2,1)S(1)}, u32[]{:S(2)}, u32[]{:S(2)}) collective-permute-start(bf16[512,512]{1,0:T(8,128)(2,1)S(1)} %get-tuple-element.14), channel_id=1, source_target_pairs={{0,4},{1,5},{2,6},{3,7},{4,0},{5,1},{6,2},{7,3},{8,12},{9,13},{10,... | collective-permute-start | bytes 1572872 | tf_op jit(solution)/shard_map/ppermute | solution.py:159
  100.0 33.4 %collective-permute-start.30 = (bf16[128,4096]{1,0:T(8,128)(2,1)S(1)}, bf16[128,4096]{1,0:T(8,128)(2,1)S(1)}, u32[]{:S(2)}, u32[]{:S(2)}) collective-permute-start(bf16[128,4096]{1,0:T(8,128)(2,1)S(1)} %collective-permute-done.29), channel_id=1, source_target_pairs={{0,8},{8,0},{16,24},{24,16},{1,9},{9,1},{17,25},{25,17},{2,10},{10... | collective-permute-start | bytes 3145736 | tf_op jit(solution)/shard_map/ppermute | solution.py:202
  128.7 26.1 %collective-permute-start.31 = (bf16[128,4096]{1,0:T(8,128)(2,1)S(1)}, bf16[128,4096]{1,0:T(8,128)(2,1)S(1)}, u32[]{:S(2)}, u32[]{:S(2)}) collective-permute-start(bf16[128,4096]{1,0:T(8,128)(2,1)S(1)} %collective-permute-done.29), channel_id=1, source_target_pairs={{0,16},{8,24},{16,0},{24,8},{1,17},{9,25},{17,1},{25,9},{2,18},{10... | collective-permute-start | bytes 3145736 | tf_op jit(solution)/shard_map/ppermute | solution.py:202
  131.6 44.7 %collective-permute-start.4 = (bf16[512,1024]{1,0:T(8,128)(2,1)S(1)}, bf16[512,1024]{1,0:T(8,128)(2,1)S(1)}, u32[]{:S(2)}, u32[]{:S(2)}) collective-permute-start(bf16[512,1024]{1,0:T(8,128)(2,1)S(1)} %get-tuple-element.10), channel_id=1, source_target_pairs={{0,1},{1,0},{2,3},{3,2},{4,5},{5,4},{6,7},{7,6},{8,9},{9,8},{10,11... | collective-permute-start | bytes 3145736 | tf_op jit(solution)/shard_map/ppermute | solution.py:156
  132.3 42.6 %collective-permute-start.11 = (bf16[4096,128]{1,0:T(8,128)(2,1)S(1)}, bf16[4096,128]{1,0:T(8,128)(2,1)S(1)}, u32[]{:S(2)}, u32[]{:S(2)}) collective-permute-start(bf16[4096,128]{1,0:T(8,128)(2,1)S(1)} %collective-permute-done.9), channel_id=1, source_target_pairs={{0,16},{8,24},{16,0},{24,8},{1,17},{9,25},{17,1},{25,9},{2,18},{10... | collective-permute-start | bytes 3145736 | tf_op jit(solution)/shard_map/ppermute | solution.py:202
  133.3 46.1 %collective-permute-start.19 = (bf16[512,512]{1,0:T(8,128)(2,1)S(1)}, bf16[512,512]{1,0:T(8,128)(2,1)S(1)}, u32[]{:S(2)}, u32[]{:S(2)}) collective-permute-start(bf16[512,512]{1,0:T(8,128)(2,1)S(1)} %get-tuple-element.14), channel_id=1, source_target_pairs={{0,2},{1,3},{2,4},{3,5},{4,6},{5,7},{8,10},{9,11},{10,12},{11,13},... | collective-permute-start | bytes 1572872 | tf_op jit(solution)/shard_map/ppermute | solution.py:159
  154.8 63.5 %collective-permute-start.6 = (bf16[512,1024]{1,0:T(8,128)(2,1)S(1)}, bf16[512,1024]{1,0:T(8,128)(2,1)S(1)}, u32[]{:S(2)}, u32[]{:S(2)}) collective-permute-start(bf16[512,1024]{1,0:T(8,128)(2,1)S(1)} %copy-done.4), channel_id=1, source_target_pairs={{0,2},{1,3},{2,4},{3,5},{4,6},{5,7},{8,10},{9,11},{10,12},{11,13},... | collective-permute-start | bytes 3145736 | tf_op jit(solution)/shard_map/ppermute | solution.py:159
  157.5 20.7 %collective-permute-start.12 = (bf16[512,512]{1,0:T(8,128)(2,1)S(1)}, bf16[512,512]{1,0:T(8,128)(2,1)S(1)}, u32[]{:S(2)}, u32[]{:S(2)}) collective-permute-start(bf16[512,512]{1,0:T(8,128)(2,1)S(1)} %get-tuple-element.13), channel_id=1, source_target_pairs={{0,1},{1,0},{2,3},{3,2},{4,5},{5,4},{6,7},{7,6},{8,9},{9,8},{10,11... | collective-permute-start | bytes 1572872 | tf_op jit(solution)/shard_map/ppermute | solution.py:156
  175.0 16.7 %collective-permute-start.14 = (bf16[512,512]{1,0:T(8,128)(2,1)S(1)}, bf16[512,512]{1,0:T(8,128)(2,1)S(1)}, u32[]{:S(2)}, u32[]{:S(2)}) collective-permute-start(bf16[512,512]{1,0:T(8,128)(2,1)S(1)} %collective-permute-done.13), channel_id=1, source_target_pairs={{4,6},{5,7},{2,0},{3,1},{12,14},{13,15},{10,8},{11,9},{20,22},{21,... | collective-permute-start | bytes 1572872 | tf_op jit(solution)/shard_map/ppermute | solution.py:159
  176.3 23.2 %collective-permute-start.5 = (bf16[512,1024]{1,0:T(8,128)(2,1)}, bf16[512,1024]{1,0:T(8,128)(2,1)S(1)}, u32[]{:S(2)}, u32[]{:S(2)}) collective-permute-start(bf16[512,1024]{1,0:T(8,128)(2,1)} %collective-permute-done.1), channel_id=1, source_target_pairs={{0,1},{1,0},{2,3},{3,2},{4,5},{5,4},{6,7},{7,6},{8,9},{9,8},{10,11... | collective-permute-start | bytes 3145736 | tf_op jit(solution)/shard_map/ppermute | solution.py:156
  178.1 43.0 %collective-permute-start.15 = (bf16[512,512]{1,0:T(8,128)(2,1)S(1)}, bf16[512,512]{1,0:T(8,128)(2,1)S(1)}, u32[]{:S(2)}, u32[]{:S(2)}) collective-permute-start(bf16[512,512]{1,0:T(8,128)(2,1)S(1)} %get-tuple-element.14), channel_id=1, source_target_pairs={{2,0},{3,1},{4,2},{5,3},{6,4},{7,5},{10,8},{11,9},{12,10},{13,11},... | collective-permute-start | bytes 1572872 | tf_op jit(solution)/shard_map/ppermute | solution.py:159
  179.4 37.5 %collective-permute-start.16 = (bf16[512,512]{1,0:T(8,128)(2,1)S(1)}, bf16[512,512]{1,0:T(8,128)(2,1)S(1)}, u32[]{:S(2)}, u32[]{:S(2)}) collective-permute-start(bf16[512,512]{1,0:T(8,128)(2,1)S(1)} %collective-permute-done.12), channel_id=1, source_target_pairs={{0,4},{1,5},{2,6},{3,7},{4,0},{5,1},{6,2},{7,3},{8,12},{9,13},{10,... | collective-permute-start | bytes 1572872 | tf_op jit(solution)/shard_map/ppermute | solution.py:159
  191.7 33.6 %collective-permute-start.18 = (bf16[512,512]{1,0:T(8,128)(2,1)S(1)}, bf16[512,512]{1,0:T(8,128)(2,1)S(1)}, u32[]{:S(2)}, u32[]{:S(2)}) collective-permute-start(bf16[512,512]{1,0:T(8,128)(2,1)S(1)} %collective-permute-done.12), channel_id=1, source_target_pairs={{2,0},{3,1},{4,2},{5,3},{6,4},{7,5},{10,8},{11,9},{12,10},{13,11},... | collective-permute-start | bytes 1572872 | tf_op jit(solution)/shard_map/ppermute | solution.py:159
  199.5 24.8 %collective-permute-start.32 = (bf16[128,4096]{1,0:T(8,128)(2,1)S(1)}, bf16[128,4096]{1,0:T(8,128)(2,1)S(1)}, u32[]{:S(2)}, u32[]{:S(2)}) collective-permute-start(bf16[128,4096]{1,0:T(8,128)(2,1)S(1)} %collective-permute-done.30), channel_id=1, source_target_pairs={{0,16},{8,24},{16,0},{24,8},{1,17},{9,25},{17,1},{25,9},{2,18},{10... | collective-permute-start | bytes 3145736 | tf_op jit(solution)/shard_map/ppermute | solution.py:202
  216.9 18.8 %collective-permute-start.20 = (bf16[512,512]{1,0:T(8,128)(2,1)S(1)}, bf16[512,512]{1,0:T(8,128)(2,1)S(1)}, u32[]{:S(2)}, u32[]{:S(2)}) collective-permute-start(bf16[512,512]{1,0:T(8,128)(2,1)S(1)} %collective-permute-done.12), channel_id=1, source_target_pairs={{0,2},{1,3},{2,4},{3,5},{4,6},{5,7},{8,10},{9,11},{10,12},{11,13},... | collective-permute-start | bytes 1572872 | tf_op jit(solution)/shard_map/ppermute | solution.py:159
  218.3 15.2 %collective-permute-start.17 = (bf16[512,512]{1,0:T(8,128)(2,1)S(1)}, bf16[512,512]{1,0:T(8,128)(2,1)S(1)}, u32[]{:S(2)}, u32[]{:S(2)}) collective-permute-start(bf16[512,512]{1,0:T(8,128)(2,1)S(1)} %collective-permute-done.16), channel_id=1, source_target_pairs={{4,6},{5,7},{2,0},{3,1},{12,14},{13,15},{10,8},{11,9},{20,22},{21,... | collective-permute-start | bytes 1572872 | tf_op jit(solution)/shard_map/ppermute | solution.py:159
  221.1 22.8 %collective-permute-start.7 = (bf16[512,1024]{1,0:T(8,128)(2,1)S(1)}, bf16[512,1024]{1,0:T(8,128)(2,1)S(1)}, u32[]{:S(2)}, u32[]{:S(2)}) collective-permute-start(bf16[512,1024]{1,0:T(8,128)(2,1)S(1)} %get-tuple-element.8), channel_id=1, source_target_pairs={{0,1},{1,0},{2,3},{3,2},{4,5},{5,4},{6,7},{7,6},{8,9},{9,8},{10,11... | collective-permute-start | bytes 3145736 | tf_op jit(solution)/shard_map/ppermute | solution.py:156
  277.5 4.2 %copy-start.6 = (bf16[512,1024]{1,0:T(8,128)(2,1)S(1)}, bf16[512,1024]{1,0:T(8,128)(2,1)}, u32[]{:S(2)}) copy-start(bf16[512,1024]{1,0:T(8,128)(2,1)} %attend.1) | copy-start | bytes 3145732
  285.9 28.5 %collective-permute-start.35 = (bf16[512,1024]{1,0:T(8,128)(2,1)}, bf16[512,1024]{1,0:T(8,128)(2,1)}, u32[]{:S(2)}, u32[]{:S(2)}) collective-permute-start(bf16[512,1024]{1,0:T(8,128)(2,1)} %get-tuple-element.17), channel_id=1, source_target_pairs={{0,2},{1,3},{6,4},{7,5},{8,10},{9,11},{14,12},{15,13},{16,18},{17,... | collective-permute-start | bytes 3145736 | tf_op jit(solution)/shard_map/ppermute | solution.py:159
  291.5 45.4 %collective-permute-start.33 = (bf16[512,1024]{1,0:T(8,128)(2,1)}, bf16[512,1024]{1,0:T(8,128)(2,1)S(1)}, u32[]{:S(2)}, u32[]{:S(2)}) collective-permute-start(bf16[512,1024]{1,0:T(8,128)(2,1)} %fusion.8), channel_id=1, source_target_pairs={{0,2},{1,3},{2,4},{3,5},{4,6},{5,7},{8,10},{9,11},{10,12},{11,13},... | collective-permute-start | bytes 3145736 | tf_op jit(solution)/shard_map/ppermute | solution.py:159
  292.8 37.8 %collective-permute-start.34 = (bf16[512,1024]{1,0:T(8,128)(2,1)}, bf16[512,1024]{1,0:T(8,128)(2,1)S(1)}, u32[]{:S(2)}, u32[]{:S(2)}) collective-permute-start(bf16[512,1024]{1,0:T(8,128)(2,1)} %get-tuple-element.18), channel_id=1, source_target_pairs={{2,0},{3,1},{4,2},{5,3},{6,4},{7,5},{10,8},{11,9},{12,10},{13,11},... | collective-permute-start | bytes 3145736 | tf_op jit(solution)/shard_map/ppermute | solution.py:159
  318.8 41.3 %collective-permute-start.36 = (bf16[512,1024]{1,0:T(8,128)(2,1)}, bf16[512,1024]{1,0:T(8,128)(2,1)}, u32[]{:S(2)}, u32[]{:S(2)}) collective-permute-start(bf16[512,1024]{1,0:T(8,128)(2,1)} %add_convert_fusion.1), channel_id=1, source_target_pairs={{0,4},{1,5},{2,6},{3,7},{4,0},{5,1},{6,2},{7,3},{8,12},{9,13},{10,... | collective-permute-start | bytes 3145736 | tf_op jit(solution)/shard_map/ppermute | solution.py:159
  362.2 9.2 %collective-permute-start.37 = (bf16[512,512]{1,0:T(8,128)(2,1)S(1)}, bf16[512,512]{1,0:T(8,128)(2,1)S(1)}, u32[]{:S(2)}, u32[]{:S(2)}) collective-permute-start(bf16[512,512]{1,0:T(8,128)(2,1)S(1)} %broadcast_select_fusion.5), channel_id=1, source_target_pairs={{0,1},{1,0},{2,3},{3,2},{4,5},{5,4},{6,7},{7,6},{8,9},{9,8},{10,11... | collective-permute-start | bytes 1572872 | tf_op jit(solution)/shard_map/ppermute | solution.py:156

commit v2 on v1

v2 whole, which is shorter than its diff:
```python
import functools

import jax
import jax.numpy as jnp
from jax import lax
from jax.experimental import pallas as pl
from jax.experimental.pallas import tpu as pltpu
from jax.sharding import PartitionSpec as P

D = 4096
HEADS = 32
GROUP = 64
NEIGH = 2
EPS = 1e-06
F32 = jnp.float32
BF16 = jnp.bfloat16
MIB = 1024 * 1024


def encode_kernel(count, slots, *refs):
    rows = refs[:count]
    up, down, out, wide, normed, total = refs[count:]
    step = pl.program_id(0)
    span = rows[0].shape[1]

    @pl.when(step == 0)
    def _():
        for k in range(count):
            part = pl.ds(k * span, span)
            x = rows[k][0].astype(F32)
            square = jnp.mean(x * x, axis=-1, keepdims=True)
            normed[part, :] = (x * lax.rsqrt(square + EPS)).astype(BF16)
            wide[part, :] = rows[k][0]
        total[...] = jnp.zeros_like(total)

    h = jnp.dot(normed[...], up[...], preferred_element_type=F32)
    h = (0.5 * h * (1.0 + lax.erf(h * (0.5**0.5)))).astype(BF16)
    total[...] += jnp.dot(h, down[...], preferred_element_type=F32)

    @pl.when(step == pl.num_programs(0) - 1)
    def _():
        out[...] = (wide[...].astype(F32) + total[...]).astype(BF16)


def encode(neighbours, slots, up, down):
    count = slots.shape[0]
    _, span, width = neighbours.shape
    hidden = up.shape[1]
    tile = min(512, hidden)
    rows = count * span
    one = [
        pl.BlockSpec((1, span, width), functools.partial(lambda k, i, s: (s[k], 0, 0), k))
        for k in range(count)
    ]
    return pl.pallas_call(
        functools.partial(encode_kernel, count),
        grid_spec=pltpu.PrefetchScalarGridSpec(
            num_scalar_prefetch=1,
            grid=(hidden // tile,),
            in_specs=[
                *one,
                pl.BlockSpec((width, tile), lambda i, s: (0, i)),
                pl.BlockSpec((tile, width), lambda i, s: (i, 0)),
            ],
            out_specs=pl.BlockSpec((rows, width), lambda i, s: (0, 0)),
            scratch_shapes=[
                pltpu.VMEM((rows, width), BF16),
                pltpu.VMEM((rows, width), BF16),
                pltpu.VMEM((rows, width), F32),
            ],
        ),
        out_shape=jax.ShapeDtypeStruct((rows, width), BF16),
        compiler_params=pltpu.CompilerParams(vmem_limit_bytes=56 * MIB),
        cost_estimate=pl.CostEstimate(
            flops=4 * rows * width * hidden,
            bytes_accessed=4 * width * hidden + 4 * rows * width,
            transcendentals=rows * hidden,
        ),
        name="encode",
    )(slots, *([neighbours] * count), up, down)


def attend_kernel(head_dim, count, where, *refs):
    blocks = refs[:count]
    q, *weights, out, keys, values, scores, probs = refs[count:]
    scale = float(head_dim) ** (-0.5)
    rows = jnp.concatenate([b[0] for b in blocks], axis=0)
    half = q.shape[1] // 2
    for made, (near, far) in ((keys, weights[:2]), (values, weights[2:])):
        made[:, :half] = jnp.dot(rows, near[...], preferred_element_type=F32).astype(BF16)
        made[:, half:] = jnp.dot(rows, far[...], preferred_element_type=F32).astype(BF16)
    groups, heads = count // NEIGH, q.shape[1] // head_dim
    span = rows.shape[0] // groups
    each = [(g, h) for g in range(groups) for h in range(heads)]

    def places(g, h):
        at = (g * heads + h) * GROUP
        return (
            slice(g * GROUP, (g + 1) * GROUP),
            slice(g * span, (g + 1) * span),
            slice(h * head_dim, (h + 1) * head_dim),
            slice(at, at + GROUP),
        )

    for g, h in each:
        mine, seen, cols, at = places(g, h)
        scores[at, :] = (
            lax.dot_general(
                q[mine, cols],
                keys[seen, cols],
                (((1,), (1,)), ((), ())),
                preferred_element_type=F32,
            )
            * scale
        )
    for g in range(groups):
        at = slice(g * heads * GROUP, (g + 1) * heads * GROUP)
        s = scores[at, :]
        weights = jnp.exp(s - jnp.max(s, axis=-1, keepdims=True))
        probs[at, :] = (weights / jnp.sum(weights, axis=-1, keepdims=True)).astype(BF16)
    for g, h in each:
        mine, seen, cols, at = places(g, h)
        out[mine, cols] = jnp.dot(
            probs[at, :], values[seen, cols], preferred_element_type=F32
        ).astype(BF16)


def attend(where, encoded, queries, w_key, w_value, packed, head_dim, at_once):
    tokens, cols = queries.shape
    groups = tokens // GROUP
    _, span, width = encoded.shape
    count = at_once * NEIGH
    one = [
        pl.BlockSpec((1, span, width), functools.partial(lambda k, c, s: (s[c * count + k], 0, 0), k))
        for k in range(count)
    ]
    keys = groups * NEIGH * span
    return pl.pallas_call(
        functools.partial(attend_kernel, head_dim, count),
        grid_spec=pltpu.PrefetchScalarGridSpec(
            num_scalar_prefetch=1,
            grid=(groups // at_once,),
            in_specs=[
                *one,
                pl.BlockSpec((at_once * GROUP, cols), lambda c, s: (c, 0)),
                pl.BlockSpec((width, cols // 2), lambda c, s: (0, 0)),
                pl.BlockSpec((width, cols // 2), lambda c, s: (D // width, 0)),
                pl.BlockSpec((width, cols // 2), lambda c, s: (0, 0)),
                pl.BlockSpec((width, cols // 2), lambda c, s: (D // width + 1, 0)),
            ],
            out_specs=pl.BlockSpec((at_once * GROUP, cols), lambda c, s: (c, 0)),
            scratch_shapes=[
                pltpu.VMEM((count * span, cols), BF16),
                pltpu.VMEM((count * span, cols), BF16),
                pltpu.VMEM((at_once * GROUP * (cols // head_dim), NEIGH * span), F32),
                pltpu.VMEM((at_once * GROUP * (cols // head_dim), NEIGH * span), BF16),
            ],
        ),
        out_shape=jax.ShapeDtypeStruct((tokens, cols), BF16),
        compiler_params=pltpu.CompilerParams(vmem_limit_bytes=40 * MIB),
        cost_estimate=pl.CostEstimate(
            flops=4 * keys * width * cols + 4 * tokens * NEIGH * span * cols,
            bytes_accessed=2 * keys * width + 4 * width * cols + 4 * tokens * cols,
            transcendentals=tokens * NEIGH * span * (cols // head_dim),
        ),
        name="attend",
    )(where, *([encoded] * count), queries, w_key, packed, w_value, packed)


def terms_kernel(order, a, near, far, hold, *send):
    step = pl.program_id(0)
    half = a.shape[1] // 2
    term = jnp.dot(a[:, :half], near[...], preferred_element_type=F32) + jnp.dot(
        a[:, half:], far[...], preferred_element_type=F32
    )

    @pl.when(step == 0)
    def _():
        hold[...] = term

    for k, out in enumerate(send):

        @pl.when(step == k + 1)
        def _(out=out):
            out[...] = term.astype(BF16)


def terms(order, attended, near, far):
    rows, depth = attended.shape
    count = order.shape[0]
    cols = near.shape[1] // count
    return pl.pallas_call(
        terms_kernel,
        grid_spec=pltpu.PrefetchScalarGridSpec(
            num_scalar_prefetch=1,
            grid=(count,),
            in_specs=[
                pl.BlockSpec((rows, depth), lambda k, s: (0, 0)),
                pl.BlockSpec((depth // 2, cols), lambda k, s: (0, s[k])),
                pl.BlockSpec((depth // 2, cols), lambda k, s: (0, s[k])),
            ],
            out_specs=[pl.BlockSpec((rows, cols), lambda k, s: (0, 0))] * count,
        ),
        out_shape=[
            jax.ShapeDtypeStruct((rows, cols), BF16 if k else F32) for k in range(count)
        ],
        compiler_params=pltpu.CompilerParams(vmem_limit_bytes=28 * MIB),
        cost_estimate=pl.CostEstimate(
            flops=2 * rows * depth * cols * count,
            bytes_accessed=2 * rows * depth + 2 * depth * cols * count + 2 * rows * cols * count,
            transcendentals=0,
        ),
        name="terms",
    )(order, attended, near, far)


def shards(
    decoder_states, w_query, w_key, w_value, w_out, enc_up, enc_down, neighbour_inputs, requests
):
    n = lax.axis_size("an")
    s_total = lax.axis_size("sa")
    position = lax.axis_index("an")
    length = n // 2
    pair, line = position % 2, position // 2
    first = pair == 0
    tok_rows, local = decoder_states.shape
    half = tok_rows // 2
    head_dim = D // HEADS
    total_requests = requests.shape[0]
    per_owner = total_requests // n
    nb_own, span, width = neighbour_inputs.shape

    def swap_pair(a):
        return lax.ppermute(a, "an", [(i, i ^ 1) for i in range(n)])

    def swap_sa(a, bit):
        return lax.ppermute(a, "sa", [(i, i ^ bit) for i in range(s_total)])

    def on_line(a, moves):
        return lax.ppermute(a, "an", [(i * 2 + y, j * 2 + y) for i, j in moves for y in range(2)])

    def from_place(a, d):
        return on_line(a, [((i + d) % length, i) for i in range(length)])

    def line_gather(a):
        if length != 4:
            moves = [from_place(a, d) for d in range(1, length)]
            return moves, lambda moves: [a, *moves]
        two = from_place(a, 2)
        after = on_line(a, [(i + 1, i) for i in range(3)])
        before = on_line(a, [(i, i + 1) for i in range(3)])

        def finish(moves):
            two, after, before = moves
            ends = on_line(two, [(2, 3), (1, 0)])
            after = jnp.where(line == 3, ends, after)
            return [a, after, two, jnp.where(line == 0, ends, before)]

        return [two, after, before], finish

    def line_sum(hold, send):
        if length == 4:
            one, two, three = send
            relay = on_line(jnp.where(line == 0, three, one), [(0, 1), (3, 2)])
            after = on_line(one, [(i, i + 1) for i in range(3)])
            before = on_line(three, [(i + 1, i) for i in range(3)])
            two = from_place((two.astype(F32) + relay.astype(F32)).astype(BF16), 2)
            got = [after, before, two]
        else:
            got = [from_place(a, length - 1 - i) for i, a in enumerate(send)]
        for a in got:
            hold = hold + a.astype(F32)
        return hold

    def swap_pieces(pieces, bit, axis):
        return jnp.concatenate([pieces, swap_sa(pieces, bit)], axis=axis)

    def own_piece(a, axis):
        size = a.shape[axis] // s_total
        return lax.dynamic_slice_in_dim(a, lax.axis_index("sa") * size, size, axis)

    low, high = decoder_states[:half], decoder_states[half:]
    mine = jnp.where(first, low, high)
    other = swap_pair(jnp.where(first, high, low))
    owner = requests // nb_own
    local_id = requests % nb_own
    owner_range = jnp.arange(n, dtype=jnp.int32)
    local_range = jnp.arange(nb_own, dtype=jnp.int32)
    hits = (owner[:, None, None] == owner_range[None, :, None]) & (
        local_id[:, None, None] == local_range[None, None, :]
    )
    present = jnp.max(hits.astype(jnp.int32), axis=0)
    earlier = (local_range[None, :] < local_range[:, None]).astype(jnp.int32)
    ranked = jnp.sum(present[:, None, :] * earlier[None, :, :], axis=2)
    rank_of_request = jnp.sum(jnp.where(hits, ranked[None], 0), axis=(1, 2))
    is_me = owner_range[:, None] == position
    my_present = jnp.sum(jnp.where(is_me, present, 0), axis=0)
    my_rank = jnp.sum(jnp.where(is_me, ranked, 0), axis=0)
    chosen_mask = (my_present[:, None] == 1) & (
        my_rank[:, None] == jnp.arange(per_owner, dtype=jnp.int32)[None, :]
    )
    local_of_slot = jnp.sum(jnp.where(chosen_mask, local_range[:, None], 0), axis=0)
    where = owner * per_owner + rank_of_request
    where = jnp.where(first, where[: total_requests // 2], where[total_requests // 2 :])

    tie = lax.optimization_barrier
    bits = [s_total >> k for k in range(1, s_total.bit_length())]
    packed = swap_pair(
        jnp.concatenate([own_piece(w, 1) for w in (w_query, w_key, w_value)], axis=0)
    )
    mine_near, mine_finish = line_gather(mine)
    encoded = encode(neighbour_inputs, local_of_slot, enc_up, enc_down)
    encoded, mine_near, other, packed, piece = tie(
        (encoded, mine_near, other, packed, own_piece(w_out, 0))
    )
    other_near, other_finish = line_gather(other)
    everything = lax.all_gather(
        encoded.reshape(per_owner, span, width), "an", axis=0, tiled=True
    )
    mine_line, other_line = mine_finish(mine_near), other_finish(other_near)
    piece = swap_pair(piece)
    packed = swap_pieces(packed, bits[0], 1)
    mine_line, other_line, packed, piece = tie((mine_line, other_line, packed, piece))
    for bit in bits[1:]:
        packed = swap_pieces(packed, bit, 1)
    for bit in bits:
        piece = swap_pieces(piece, bit, 0)
    order = (line + jnp.arange(length, dtype=jnp.int32)) % length
    everything, piece = tie((everything, piece))

    chunks = []
    split = 1
    rows, asked = half // split, where.shape[0] // split
    for k in range(split):
        queries = []
        for weight in (w_query, packed[:D]):
            total = 0.0
            for d in range(length):
                for x, y in ((mine_line[d], pair), (other_line[d], 1 - pair)):
                    part = lax.dynamic_slice_in_dim(
                        weight, (order[d] * 2 + y) * local, local, 0
                    )
                    total = total + jnp.dot(x, part, preferred_element_type=F32)
            queries.append(total.astype(BF16))
        queries = jnp.concatenate(queries, axis=1)
        attended = attend(
            where[k * asked : (k + 1) * asked],
            everything,
            queries,
            w_key,
            w_value,
            packed,
            head_dim,
            min(4, asked // NEIGH),
        )
        hold, *send = terms(order, attended, w_out, piece)
        summed = line_sum(hold, send).astype(BF16)
        left, right = summed[:, :local], summed[:, local:]
        chunks.append((jnp.where(first, left, right), swap_pair(jnp.where(first, right, left))))
    keep = jnp.concatenate([c[0] for c in chunks], axis=0)
    got = jnp.concatenate([c[1] for c in chunks], axis=0)
    return jnp.concatenate([jnp.where(first, keep, got), jnp.where(first, got, keep)], axis=0)


def solution(mesh):
    placed = (
        P("sa", "an"),
        P(None, "an"),
        P(None, "an"),
        P(None, "an"),
        P("an", None),
        P(),
        P(),
        P(("sa", "an"), None, None),
        P("sa"),
    )
    return jax.shard_map(
        shards, mesh=mesh, in_specs=placed, out_specs=P("sa", "an"), check_vma=False
    )
```

time: 374 us -> 340 us (0.909)
  local copies, waits for them, and re-layouts: 35.1 us -> 12.7 us
  between operations: 0.49 us -> 16.5 us
  starting transfers between devices: 49.7 us -> 36.5 us
  Pallas kernels: 48.1 us -> 37.1 us
  other arithmetic: 9.89 us -> 19.4 us
  matrix products: 23.2 us -> 14.5 us
  waiting for transfers between devices: 206 us -> 202 us
    ppermute x12 -> x4, waiting for transfers between devices: 49.5 us -> 6.82 us  [swap_sa(): return lax.ppermute(a, 'sa', [(i, i ^ bit) for i in range(s_total)])]
    ppermute x16 -> x12, waiting for transfers between devices: 119 us -> 150 us  [on_line(): lax.ppermute(a, 'an', [(i * 2 + y, j * 2 + y) for i, j in moves for y in...]
    unnamed x35 -> x33, local copies, waits for them, and re-layouts: 27.6 us -> 7.88 us
    pallas_call x1 -> x2, Pallas kernels: 32.4 us -> 21.1 us  [the longest x1 14.4 us: attend(): pl.pallas_call(functools.partial(attend_kernel, head_dim, count), grid_sp...]
    all_gather x0 -> x1, waiting for transfers between devices: none -> 10.8 us  [shards(): lax.all_gather(encoded.reshape(per_owner, span, width), 'an', axis=0, til...]
    concatenate x0 -> x5, other arithmetic: none -> 8.91 us  [the longest x3 8.66 us: swap_pieces(): return jnp.concatenate([pieces, swap_sa(pieces, bit)], axis=axis)]
    ppermute x12 -> x4, starting transfers between devices: 10.5 us -> 1.64 us  [swap_sa(): return lax.ppermute(a, 'sa', [(i, i ^ bit) for i in range(s_total)])]
    dot_general x12 -> x16, matrix products: 23.2 us -> 14.5 us  [shards(): total = total + jnp.dot(x, part, preferred_element_type=F32)]
  transfers between devices with their start and end apart: 38 -> 21, of which waited for: 20 -> 10; matrix products, arithmetic and copies ran while one was open for 14% -> 10% of each run, Pallas kernels for 4% -> 5%
where the time goes in v2:
time: 340 us; the launch traced here: 339 us
  waiting for transfers between devices  202 us (59%)
  Pallas kernels  37.1 us (11%)
  starting transfers between devices  36.5 us (11%)
  other arithmetic  19.4 us (6%)
  between operations  16.5 us (5%)
  matrix products  14.5 us (4%)
  local copies, waits for them, and re-layouts  12.7 us (4%)
    ppermute x12, waiting for transfers between devices, on_line(): lax.ppermute(a, 'an', [(i * 2 + y, j * 2 + y) for i, j in moves for y in...  150 us
    ppermute x4, waiting for transfers between devices, swap_pair(): return lax.ppermute(a, 'an', [(i, i ^ 1) for i in range(n)])  34.8 us
    ppermute x12, starting transfers between devices, on_line(): lax.ppermute(a, 'an', [(i * 2 + y, j * 2 + y) for i, j in moves for y in...  30.3 us
    pallas_call x1, Pallas kernels, encode(): pl.pallas_call(functools.partial(encode_kernel, count), grid_spec=pltpu.P...  16.1 us
    dot_general x16, matrix products, shards(): total = total + jnp.dot(x, part, preferred_element_type=F32)  14.5 us
    pallas_call x1, Pallas kernels, attend(): pl.pallas_call(functools.partial(attend_kernel, head_dim, count), grid_sp...  14.4 us
    all_gather x1, waiting for transfers between devices, shards(): lax.all_gather(encoded.reshape(per_owner, span, width), 'an', axis=0, til...  10.8 us
    concatenate x3, other arithmetic, swap_pieces(): return jnp.concatenate([pieces, swap_sa(pieces, bit)], axis=axis)  8.66 us
  transfers between devices with their start and end apart: 21, of which 10 were waited for; matrix products, arithmetic and copies ran while one was open for 10% of the time, Pallas kernels for 5%

profile of v2, /device:TPU:0, one launch (start us, length us, event | category | flops | bytes accessed | tf_op | source)
XLA Modules:
  0.0 339.1 jit_solution(11256985582971931113)
XLA Ops:
  6.5 2.2 broadcast_select_fusion.9
  8.8 4.0 %collective-permute-start = (bf16[512,512]{1,0:T(8,128)(2,1)S(1)}, bf16[512,512]{1,0:T(8,128)(2,1)S(1)}, u32[]{:S(2)}, u32[]{:S(2)}) collective-permute-start(bf16[512,512]{1,0:T(8,128)(2,1)S(1)} %get-tuple-element.37), channel_id=1, source_target_pairs={{4,0},{5,1},{6,2},{7,3},{0,4},{1,5},{2,6},{3,7},{12,8},{13,9},{14,... | collective-permute-start | bytes 1572872 | tf_op jit(solution)/shard_map/ppermute | solution.py:240
  12.8 1.3 collective-permute-start.1
  14.1 5.4 %collective-permute-start.2 = (bf16[512,512]{1,0:T(8,128)(2,1)S(1)}, bf16[512,512]{1,0:T(8,128)(2,1)}, u32[]{:S(2)}, u32[]{:S(2)}) collective-permute-start(bf16[512,512]{1,0:T(8,128)(2,1)S(1)} %get-tuple-element.37), channel_id=1, source_target_pairs={{0,2},{1,3},{2,4},{3,5},{4,6},{5,7},{8,10},{9,11},{10,12},{11,13},... | collective-permute-start | bytes 1572872 | tf_op jit(solution)/shard_map/ppermute | solution.py:240
  19.5 1.5 collective-permute-start.3
  21.0 1.3 constant_dynamic-slice_fusion.3
  24.4 16.1 %encode.1 = bf16[512,1024]{1,0:T(8,128)(2,1)} custom-call(s32[4]{0:T(128)} %select_reduce_fusion.2.slots, bf16[8,128,1024]{2,1,0:T(8,128)(2,1)} %refs_3_.1, bf16[8,128,1024]{2,1,0:T(8,128)(2,1)} %refs_3_.1, bf16[8,128,1024]{2,1,0:T(8,128)(2,1)} %refs_3_.1, bf16[8,128,1024]{2,1,0:T(8,128)(2,1)} %refs_3_.1, bf16[1024,4096]{1,0:T(8,128)(2,1)} %refs_4_.1, ...), custom_call_target="tpu_custom_call" | custom-call | flops 8589934592 | bytes 18874368 | tf_op jit(solution)/shard_map/encode/pallas_call | solution.py:55
  40.4 2.3 constant_dynamic-slice_fusion
  42.7 23.5 %collective-permute-done.4 = bf16[6144,128]{1,0:T(8,128)(2,1)S(1)} collective-permute-done((bf16[6144,128]{1,0:T(8,128)(2,1)S(1)}, bf16[6144,128]{1,0:T(8,128)(2,1)S(1)}, u32[]{:S(2)}, u32[]{:S(2)}) %collective-permute-start.4) | collective-permute-done | bytes 1572896 | tf_op jit(solution)/shard_map/ppermute | solution.py:234
  66.2 1.2 copy-done.13
  67.4 1.6 collective-permute-start.10
  69.5 1.3 collective-permute-start.5
  70.9 1.3 collective-permute-start.8
  72.2 6.8 %collective-permute-start.9 = (bf16[512,512]{1,0:T(8,128)(2,1)}, bf16[512,512]{1,0:T(8,128)(2,1)}, u32[]{:S(2)}, u32[]{:S(2)}) collective-permute-start(bf16[512,512]{1,0:T(8,128)(2,1)} %collective-permute-done.3), channel_id=1, source_target_pairs={{0,2},{1,3},{2,4},{3,5},{4,6},{5,7},{8,10},{9,11},{10,12},{11,13},... | collective-permute-start | bytes 1572872 | tf_op jit(solution)/shard_map/ppermute | solution.py:240
  79.0 37.0 %collective-permute-done.6 = bf16[512,512]{1,0:T(8,128)(2,1)} collective-permute-done((bf16[512,512]{1,0:T(8,128)(2,1)}, bf16[512,512]{1,0:T(8,128)(2,1)}, u32[]{:S(2)}, u32[]{:S(2)}) %collective-permute-start.6) | collective-permute-done | bytes 524320 | tf_op jit(solution)/shard_map/ppermute | solution.py:240
  116.0 1.3 collective-permute-start.7
  117.3 1.6 collective-permute-start.11
  118.9 2.1 broadcast_select_fusion.2
  121.0 21.2 %collective-permute-done.8 = bf16[512,512]{1,0:T(8,128)(2,1)} collective-permute-done((bf16[512,512]{1,0:T(8,128)(2,1)}, bf16[512,512]{1,0:T(8,128)(2,1)}, u32[]{:S(2)}, u32[]{:S(2)}) %collective-permute-start.8) | collective-permute-done | bytes 524320 | tf_op jit(solution)/shard_map/ppermute | solution.py:240
  142.2 24.6 %collective-permute-done.7 = bf16[512,512]{1,0:T(8,128)(2,1)} collective-permute-done((bf16[512,512]{1,0:T(8,128)(2,1)}, bf16[512,512]{1,0:T(8,128)(2,1)}, u32[]{:S(2)}, u32[]{:S(2)}) %collective-permute-start.7) | collective-permute-done | bytes 524320 | tf_op jit(solution)/shard_map/ppermute | solution.py:240
  166.8 2.2 broadcast_select_fusion.1
  169.0 3.4 %pad_maximum_fusion.1 = bf16[6144,256]{1,0:T(8,128)(2,1)} fusion(bf16[6144,128]{1,0:T(8,128)(2,1)} %collective-permute-done.10, bf16[6144,128]{1,0:T(8,128)(2,1)S(1)} %copy-done.14), kind=kLoop, calls=%fused_computation.1 | loop fusion | flops 6291456 | bytes 6291456 | tf_op jit(solution)/shard_map/concatenate | solution.py:276
  175.8 1.8 fusion.29
  177.6 1.6 fusion.33
  179.2 1.5 fusion.37
  180.7 6.8 %collective-permute-done.12 = bf16[128,4096]{1,0:T(8,128)(2,1)} collective-permute-done((bf16[128,4096]{1,0:T(8,128)(2,1)}, bf16[128,4096]{1,0:T(8,128)(2,1)}, u32[]{:S(2)}, u32[]{:S(2)}) %collective-permute-start.12) | collective-permute-done | bytes 1048608 | tf_op jit(solution)/shard_map/ppermute | solution.py:237
  187.5 1.7 pad_maximum_fusion.2
  189.3 1.5 fusion.41
  192.2 0.8 fusion.13
  193.0 1.2 copy-done.6
  194.5 3.6 %pad_maximum_fusion.far = bf16[512,4096]{1,0:T(8,128)(2,1)} fusion(bf16[256,4096]{1,0:T(8,128)(2,1)S(1)} %collective-permute-done.13, bf16[128,4096]{1,0:T(8,128)(2,1)} %collective-permute-done.12, bf16[128,4096]{1,0:T(8,128)(2,1)} %collective-permute-done.11), kind=kLoop, calls=%fused_computation | loop fusion | flops 12582912 | bytes 8388608 | tf_op jit(solution)/shard_map/concatenate | solution.py:276
  198.6 2.4 copy-done
  201.0 1.5 fusion.26
  203.9 1.5 fusion.18
  207.1 10.8 %all-gather.2.cloned.1.call-done.refs_0_.refs_1_.refs_2_.refs_3_.refs_4_.refs_5_.refs_6_.refs_7_ = bf16[32,128,1024]{2,1,0:T(8,128)(2,1)} async-done(((bf16[4,128,1024]{2,1,0:T(8,128)(2,1)}), bf16[32,128,1024]{2,1,0:T(8,128)(2,1)}) %all-gather.2.cloned.1.call-update) | async-done | bytes 8388624 | tf_op jit(solution)/shard_map/all_gather | solution.py:317
  217.9 2.8 copy-done.1
  220.7 14.4 %attend.1.a = bf16[512,1024]{1,0:T(8,128)(2,1)S(1)} custom-call(s32[16]{0:T(128)S(1)} %broadcast_select_fusion.11.where, bf16[32,128,1024]{2,1,0:T(8,128)(2,1)} %all-gather.2.cloned.1.call-done.refs_0_.refs_1_.refs_2_.refs_3_.refs_4_.refs_5_.refs_6_.refs_7_, ...), custom_call_target="tpu_custom_call" | custom-call | flops 9126805504 | bytes 10485760 | tf_op jit(solution)/shard_map/attend/pallas_call | solution.py:138
  235.1 6.7 %terms.1 = (f32[512,1024]{1,0:T(8,128)S(1)}, bf16[512,1024]{1,0:T(8,128)(2,1)S(1)}, bf16[512,1024]{1,0:T(8,128)(2,1)S(1)}, bf16[512,1024]{1,0:T(8,128)(2,1)S(1)}) custom-call(s32[4]{0:T(128)S(1)} %and_select_fusion.3.order, bf16[512,1024]{1,0:T(8,128)(2,1)S(1)} %attend.1.a, bf16[512,4096]{1,0:T(8,128)(2,1)S(1)} %copy-done.5, bf16[512,4096]{1,0:T(8,128)(2,1)S(1)} %copy-done.2), custom_call_target="tpu_custom_call" | custom-call | flops 4294967296 | bytes 13631488 | tf_op jit(solution)/shard_map/terms/pallas_call | solution.py:192
  241.9 1.4 collective-permute-start.17
  243.3 1.4 collective-permute-start.15
  244.7 1.3 collective-permute-start.16
  246.0 20.7 %collective-permute-done.17 = bf16[512,1024]{1,0:T(8,128)(2,1)S(1)} collective-permute-done((bf16[512,1024]{1,0:T(8,128)(2,1)S(1)}, bf16[512,1024]{1,0:T(8,128)(2,1)S(1)}, u32[]{:S(2)}, u32[]{:S(2)}) %collective-permute-start.17) | collective-permute-done | bytes 1048608 | tf_op jit(solution)/shard_map/ppermute | solution.py:240
  267.1 4.5 %collective-permute-start.18 = (bf16[512,1024]{1,0:T(8,128)(2,1)S(1)}, bf16[512,1024]{1,0:T(8,128)(2,1)S(1)}, u32[]{:S(2)}, u32[]{:S(2)}) collective-permute-start(bf16[512,1024]{1,0:T(8,128)(2,1)S(1)} %add_convert_fusion.1), channel_id=1, source_target_pairs={{4,0},{5,1},{6,2},{7,3},{0,4},{1,5},{2,6},{3,7},{12,8},{13,9},{14,... | collective-permute-start | bytes 3145736 | tf_op jit(solution)/shard_map/ppermute | solution.py:240
  271.5 17.6 %collective-permute-done.15 = bf16[512,1024]{1,0:T(8,128)(2,1)S(1)} collective-permute-done((bf16[512,1024]{1,0:T(8,128)(2,1)S(1)}, bf16[512,1024]{1,0:T(8,128)(2,1)S(1)}, u32[]{:S(2)}, u32[]{:S(2)}) %collective-permute-start.15) | collective-permute-done | bytes 1048608 | tf_op jit(solution)/shard_map/ppermute | solution.py:240
  289.2 28.9 %collective-permute-done.18 = bf16[512,1024]{1,0:T(8,128)(2,1)S(1)} collective-permute-done((bf16[512,1024]{1,0:T(8,128)(2,1)S(1)}, bf16[512,1024]{1,0:T(8,128)(2,1)S(1)}, u32[]{:S(2)}, u32[]{:S(2)}) %collective-permute-start.18) | collective-permute-done | bytes 1048608 | tf_op jit(solution)/shard_map/ppermute | solution.py:240
  318.9 0.8 collective-permute-start.19
  319.8 11.3 %collective-permute-done.19 = bf16[512,512]{1,0:T(8,128)(2,1)S(1)} collective-permute-done((bf16[512,512]{1,0:T(8,128)(2,1)S(1)}, bf16[512,512]{1,0:T(8,128)(2,1)S(1)}, u32[]{:S(2)}, u32[]{:S(2)}) %collective-permute-start.19) | collective-permute-done | bytes 524320 | tf_op jit(solution)/shard_map/ppermute | solution.py:234
  331.2 1.0 pad_maximum_fusion.5
  (80 shorter events, 10.2 us)
Async XLA Ops:
  6.5 15.7 %copy-start.4 = (bf16[1024,512]{1,0:T(8,128)(2,1)S(1)}, bf16[1024,512]{1,0:T(8,128)(2,1)}, u32[]{:S(2)}) copy-start(bf16[1024,512]{1,0:T(8,128)(2,1)} %refs_9_.1) | copy-start | bytes 3145732
  6.5 15.8 %copy-start.3 = (bf16[1024,512]{1,0:T(8,128)(2,1)S(1)}, bf16[1024,512]{1,0:T(8,128)(2,1)}, u32[]{:S(2)}) copy-start(bf16[1024,512]{1,0:T(8,128)(2,1)} %refs_11_.1) | copy-start | bytes 3145732
  6.5 211.4 %all-gather.2.cloned.1.call-start = ((), (), s32[]{:S(2)}) async-start(), calls=%async_computation | async-start | bytes 9437184 | tf_op jit(solution)/shard_map/all_gather | solution.py:317
  6.5 16.5 %copy-start.15 = (s32[32]{0:T(128)S(1)}, s32[32]{0:T(128)}, u32[]{:S(2)}) copy-start(s32[32]{0:T(128)} %param.17) | copy-start | bytes 388
  8.8 34.0 %collective-permute-start = (bf16[512,512]{1,0:T(8,128)(2,1)S(1)}, bf16[512,512]{1,0:T(8,128)(2,1)S(1)}, u32[]{:S(2)}, u32[]{:S(2)}) collective-permute-start(bf16[512,512]{1,0:T(8,128)(2,1)S(1)} %get-tuple-element.37), channel_id=1, source_target_pairs={{4,0},{5,1},{6,2},{7,3},{0,4},{1,5},{2,6},{3,7},{12,8},{13,9},{14,... | collective-permute-start | bytes 1572872 | tf_op jit(solution)/shard_map/ppermute | solution.py:240
  12.8 29.9 %collective-permute-start.1 = (bf16[512,512]{1,0:T(8,128)(2,1)S(1)}, bf16[512,512]{1,0:T(8,128)(2,1)}, u32[]{:S(2)}, u32[]{:S(2)}) collective-permute-start(bf16[512,512]{1,0:T(8,128)(2,1)S(1)} %get-tuple-element.37), channel_id=1, source_target_pairs={{2,0},{3,1},{4,2},{5,3},{6,4},{7,5},{10,8},{11,9},{12,10},{13,11},... | collective-permute-start | bytes 1572872 | tf_op jit(solution)/shard_map/ppermute | solution.py:240
  14.1 28.6 %collective-permute-start.2 = (bf16[512,512]{1,0:T(8,128)(2,1)S(1)}, bf16[512,512]{1,0:T(8,128)(2,1)}, u32[]{:S(2)}, u32[]{:S(2)}) collective-permute-start(bf16[512,512]{1,0:T(8,128)(2,1)S(1)} %get-tuple-element.37), channel_id=1, source_target_pairs={{0,2},{1,3},{2,4},{3,5},{4,6},{5,7},{8,10},{9,11},{10,12},{11,13},... | collective-permute-start | bytes 1572872 | tf_op jit(solution)/shard_map/ppermute | solution.py:240
  19.5 23.3 %collective-permute-start.3 = (bf16[512,512]{1,0:T(8,128)(2,1)}, bf16[512,512]{1,0:T(8,128)(2,1)}, u32[]{:S(2)}, u32[]{:S(2)}) collective-permute-start(bf16[512,512]{1,0:T(8,128)(2,1)} %get-tuple-element.55), channel_id=1, source_target_pairs={{0,1},{1,0},{2,3},{3,2},{4,5},{5,4},{6,7},{7,6},{8,9},{9,8},{10,11... | collective-permute-start | bytes 1572872 | tf_op jit(solution)/shard_map/ppermute | solution.py:234
  22.5 43.7 %collective-permute-start.4 = (bf16[6144,128]{1,0:T(8,128)(2,1)S(1)}, bf16[6144,128]{1,0:T(8,128)(2,1)S(1)}, u32[]{:S(2)}, u32[]{:S(2)}) collective-permute-start(bf16[6144,128]{1,0:T(8,128)(2,1)S(1)} %pad_maximum_fusion.3), channel_id=1, source_target_pairs={{0,1},{1,0},{2,3},{3,2},{4,5},{5,4},{6,7},{7,6},{8,9},{9,8},{10,11... | collective-permute-start | bytes 4718600 | tf_op jit(solution)/shard_map/ppermute | solution.py:234
  42.7 74.6 %copy-start.11 = (bf16[512,512]{1,0:T(8,128)(2,1)}, bf16[512,512]{1,0:T(8,128)(2,1)S(1)}, u32[]{:S(2)}) copy-start(bf16[512,512]{1,0:T(8,128)(2,1)S(1)} %collective-permute-done) | copy-start | bytes 1572868
  66.2 1.2 copy-start.13
  67.4 101.6 %collective-permute-start.10 = (bf16[6144,128]{1,0:T(8,128)(2,1)}, bf16[6144,128]{1,0:T(8,128)(2,1)}, u32[]{:S(2)}, u32[]{:S(2)}) collective-permute-start(bf16[6144,128]{1,0:T(8,128)(2,1)} %copy-done.13), channel_id=1, source_target_pairs={{0,16},{8,24},{16,0},{24,8},{1,17},{9,25},{17,1},{25,9},{2,18},{10... | collective-permute-start | bytes 4718600 | tf_op jit(solution)/shard_map/ppermute | solution.py:237
  69.0 47.0 %collective-permute-start.6 = (bf16[512,512]{1,0:T(8,128)(2,1)}, bf16[512,512]{1,0:T(8,128)(2,1)}, u32[]{:S(2)}, u32[]{:S(2)}) collective-permute-start(bf16[512,512]{1,0:T(8,128)(2,1)} %collective-permute-done.3), channel_id=1, source_target_pairs={{4,0},{5,1},{6,2},{7,3},{0,4},{1,5},{2,6},{3,7},{12,8},{13,9},{14,... | collective-permute-start | bytes 1572872 | tf_op jit(solution)/shard_map/ppermute | solution.py:240
  69.5 47.8 %collective-permute-start.5 = (bf16[512,512]{1,0:T(8,128)(2,1)S(1)}, bf16[512,512]{1,0:T(8,128)(2,1)}, u32[]{:S(2)}, u32[]{:S(2)}) collective-permute-start(bf16[512,512]{1,0:T(8,128)(2,1)S(1)} %collective-permute-done), channel_id=1, source_target_pairs={{4,6},{5,7},{2,0},{3,1},{12,14},{13,15},{10,8},{11,9},{20,22},{21,... | collective-permute-start | bytes 1572872 | tf_op jit(solution)/shard_map/ppermute | solution.py:240
  70.9 71.3 %collective-permute-start.8 = (bf16[512,512]{1,0:T(8,128)(2,1)}, bf16[512,512]{1,0:T(8,128)(2,1)}, u32[]{:S(2)}, u32[]{:S(2)}) collective-permute-start(bf16[512,512]{1,0:T(8,128)(2,1)} %collective-permute-done.3), channel_id=1, source_target_pairs={{2,0},{3,1},{4,2},{5,3},{6,4},{7,5},{10,8},{11,9},{12,10},{13,11},... | collective-permute-start | bytes 1572872 | tf_op jit(solution)/shard_map/ppermute | solution.py:240
  72.2 70.0 %collective-permute-start.9 = (bf16[512,512]{1,0:T(8,128)(2,1)}, bf16[512,512]{1,0:T(8,128)(2,1)}, u32[]{:S(2)}, u32[]{:S(2)}) collective-permute-start(bf16[512,512]{1,0:T(8,128)(2,1)} %collective-permute-done.3), channel_id=1, source_target_pairs={{0,2},{1,3},{2,4},{3,5},{4,6},{5,7},{8,10},{9,11},{10,12},{11,13},... | collective-permute-start | bytes 1572872 | tf_op jit(solution)/shard_map/ppermute | solution.py:240
  116.0 50.8 %collective-permute-start.7 = (bf16[512,512]{1,0:T(8,128)(2,1)}, bf16[512,512]{1,0:T(8,128)(2,1)}, u32[]{:S(2)}, u32[]{:S(2)}) collective-permute-start(bf16[512,512]{1,0:T(8,128)(2,1)} %collective-permute-done.6), channel_id=1, source_target_pairs={{4,6},{5,7},{2,0},{3,1},{12,14},{13,15},{10,8},{11,9},{20,22},{21,... | collective-permute-start | bytes 1572872 | tf_op jit(solution)/shard_map/ppermute | solution.py:240
  117.3 51.7 %copy-start.14 = (bf16[6144,128]{1,0:T(8,128)(2,1)S(1)}, bf16[6144,128]{1,0:T(8,128)(2,1)}, u32[]{:S(2)}) copy-start(bf16[6144,128]{1,0:T(8,128)(2,1)} %copy-done.13) | copy-start | bytes 4718596
  117.3 55.1 %collective-permute-start.11 = (bf16[128,4096]{1,0:T(8,128)(2,1)}, bf16[128,4096]{1,0:T(8,128)(2,1)}, u32[]{:S(2)}, u32[]{:S(2)}) collective-permute-start(bf16[128,4096]{1,0:T(8,128)(2,1)} %constant_dynamic-slice_fusion), channel_id=1, source_target_pairs={{0,1},{1,0},{2,3},{3,2},{4,5},{5,4},{6,7},{7,6},{8,9},{9,8},{10,11... | collective-permute-start | bytes 3145736 | tf_op jit(solution)/shard_map/ppermute | solution.py:234
  172.4 15.1 %collective-permute-start.12 = (bf16[128,4096]{1,0:T(8,128)(2,1)}, bf16[128,4096]{1,0:T(8,128)(2,1)}, u32[]{:S(2)}, u32[]{:S(2)}) collective-permute-start(bf16[128,4096]{1,0:T(8,128)(2,1)} %collective-permute-done.11), channel_id=1, source_target_pairs={{0,16},{8,24},{16,0},{24,8},{1,17},{9,25},{17,1},{25,9},{2,18},{10... | collective-permute-start | bytes 3145736 | tf_op jit(solution)/shard_map/ppermute | solution.py:237
  175.7 3.5 %copy-start.7 = (bf16[4096,512]{1,0:T(8,128)(2,1)S(1)}, bf16[4096,512]{1,0:T(8,128)(2,1)}, u32[]{:S(2)}) copy-start(bf16[4096,512]{1,0:T(8,128)(2,1)} %param.10) | copy-start | bytes 12582916
  175.8 22.3 %collective-permute-start.14 = (bf16[6144,256]{1,0:T(8,128)(2,1)}, bf16[6144,256]{1,0:T(8,128)(2,1)S(1)}, u32[]{:S(2)}, u32[]{:S(2)}) collective-permute-start(bf16[6144,256]{1,0:T(8,128)(2,1)} %pad_maximum_fusion.1), channel_id=1, source_target_pairs={{0,8},{8,0},{16,24},{24,16},{1,9},{9,1},{17,25},{25,17},{2,10},{10... | collective-permute-start | bytes 9437192 | tf_op jit(solution)/shard_map/ppermute | solution.py:237
  180.7 10.6 %copy-start.12 = (bf16[512,512]{1,0:T(8,128)(2,1)S(1)}, bf16[512,512]{1,0:T(8,128)(2,1)}, u32[]{:S(2)}) copy-start(bf16[512,512]{1,0:T(8,128)(2,1)} %copy-done.11) | copy-start | bytes 1572868
  189.2 2.5 copy-start.8
  189.2 5.2 %collective-permute-start.13 = (bf16[256,4096]{1,0:T(8,128)(2,1)S(1)}, bf16[256,4096]{1,0:T(8,128)(2,1)S(1)}, u32[]{:S(2)}, u32[]{:S(2)}) collective-permute-start(bf16[256,4096]{1,0:T(8,128)(2,1)S(1)} %pad_maximum_fusion.2), channel_id=1, source_target_pairs={{0,8},{8,0},{16,24},{24,16},{1,9},{9,1},{17,25},{25,17},{2,10},{10... | collective-permute-start | bytes 6291464 | tf_op jit(solution)/shard_map/ppermute | solution.py:237
  192.2 2.0 copy-start.6
  198.3 2.7 copy-start
  201.0 2.0 copy-start.10
  203.0 2.8 copy-start.9
  217.9 2.8 copy-start.1
  220.7 14.4 %copy-start.2 = (bf16[512,4096]{1,0:T(8,128)(2,1)S(1)}, bf16[512,4096]{1,0:T(8,128)(2,1)}, u32[]{:S(2)}) copy-start(bf16[512,4096]{1,0:T(8,128)(2,1)} %pad_maximum_fusion.far) | copy-start | bytes 12582916
  220.7 14.4 %copy-start.5 = (bf16[512,4096]{1,0:T(8,128)(2,1)S(1)}, bf16[512,4096]{1,0:T(8,128)(2,1)}, u32[]{:S(2)}) copy-start(bf16[512,4096]{1,0:T(8,128)(2,1)} %near.1) | copy-start | bytes 12582916
  241.9 24.8 %collective-permute-start.17 = (bf16[512,1024]{1,0:T(8,128)(2,1)S(1)}, bf16[512,1024]{1,0:T(8,128)(2,1)S(1)}, u32[]{:S(2)}, u32[]{:S(2)}) collective-permute-start(bf16[512,1024]{1,0:T(8,128)(2,1)S(1)} %broadcast_select_fusion), channel_id=1, source_target_pairs={{0,2},{1,3},{6,4},{7,5},{8,10},{9,11},{14,12},{15,13},{16,18},{17,... | collective-permute-start | bytes 3145736 | tf_op jit(solution)/shard_map/ppermute | solution.py:240
  243.3 45.9 %collective-permute-start.15 = (bf16[512,1024]{1,0:T(8,128)(2,1)S(1)}, bf16[512,1024]{1,0:T(8,128)(2,1)S(1)}, u32[]{:S(2)}, u32[]{:S(2)}) collective-permute-start(bf16[512,1024]{1,0:T(8,128)(2,1)S(1)} %get-tuple-element.48), channel_id=1, source_target_pairs={{0,2},{1,3},{2,4},{3,5},{4,6},{5,7},{8,10},{9,11},{10,12},{11,13},... | collective-permute-start | bytes 3145736 | tf_op jit(solution)/shard_map/ppermute | solution.py:240
  244.7 44.5 %collective-permute-start.16 = (bf16[512,1024]{1,0:T(8,128)(2,1)S(1)}, bf16[512,1024]{1,0:T(8,128)(2,1)S(1)}, u32[]{:S(2)}, u32[]{:S(2)}) collective-permute-start(bf16[512,1024]{1,0:T(8,128)(2,1)S(1)} %get-tuple-element.49), channel_id=1, source_target_pairs={{2,0},{3,1},{4,2},{5,3},{6,4},{7,5},{10,8},{11,9},{12,10},{13,11},... | collective-permute-start | bytes 3145736 | tf_op jit(solution)/shard_map/ppermute | solution.py:240
  267.1 51.0 %collective-permute-start.18 = (bf16[512,1024]{1,0:T(8,128)(2,1)S(1)}, bf16[512,1024]{1,0:T(8,128)(2,1)S(1)}, u32[]{:S(2)}, u32[]{:S(2)}) collective-permute-start(bf16[512,1024]{1,0:T(8,128)(2,1)S(1)} %add_convert_fusion.1), channel_id=1, source_target_pairs={{4,0},{5,1},{6,2},{7,3},{0,4},{1,5},{2,6},{3,7},{12,8},{13,9},{14,... | collective-permute-start | bytes 3145736 | tf_op jit(solution)/shard_map/ppermute | solution.py:240
  318.9 12.1 %collective-permute-start.19 = (bf16[512,512]{1,0:T(8,128)(2,1)S(1)}, bf16[512,512]{1,0:T(8,128)(2,1)S(1)}, u32[]{:S(2)}, u32[]{:S(2)}) collective-permute-start(bf16[512,512]{1,0:T(8,128)(2,1)S(1)} %broadcast_select_fusion.7), channel_id=1, source_target_pairs={{0,1},{1,0},{2,3},{3,2},{4,5},{5,4},{6,7},{7,6},{8,9},{9,8},{10,11... | collective-permute-start | bytes 1572872 | tf_op jit(solution)/shard_map/ppermute | solution.py:234
Sparse Core Ops, SparseCore 0:
  67.5 150.3 all-gather.1

commit v3 on v2

--- a/solution.py
+++ b/solution.py
@@ -300,33 +300,56 @@
         my_rank[:, None] == jnp.arange(per_owner, dtype=jnp.int32)[None, :]
     )
     local_of_slot = jnp.sum(jnp.where(chosen_mask, local_range[:, None], 0), axis=0)
-    where = owner * per_owner + rank_of_request
+    away = (owner // 2 - line + length) % length
+    over = (owner % 2 != pair).astype(jnp.int32)
+    where = (away * 2 + over) * per_owner + rank_of_request
     where = jnp.where(first, where[: total_requests // 2], where[total_requests // 2 :])
 
     tie = lax.optimization_barrier
     bits = [s_total >> k for k in range(1, s_total.bit_length())]
+    rows_each = per_owner * span
+    everything = jnp.zeros((n * rows_each, width), BF16)
+
+    def put(everything, a, d, over):
+        return lax.dynamic_update_slice_in_dim(everything, a, (d * 2 + over) * rows_each, 0)
+
+    mine_near, mine_finish = line_gather(mine)
+    encoded = encode(neighbour_inputs, local_of_slot, enc_up, enc_down)
+    encoded, other, mine_near = tie((encoded, other, mine_near))
+
     packed = swap_pair(
         jnp.concatenate([own_piece(w, 1) for w in (w_query, w_key, w_value)], axis=0)
     )
-    mine_near, mine_finish = line_gather(mine)
-    encoded = encode(neighbour_inputs, local_of_slot, enc_up, enc_down)
-    encoded, mine_near, other, packed, piece = tie(
-        (encoded, mine_near, other, packed, own_piece(w_out, 0))
-    )
+    near, finish = line_gather(encoded)
+    crossed = {0: swap_pair(encoded)}
+    mine_line = mine_finish(mine_near)
+    near, crossed[0], mine_line, packed, piece, encoded, other = tie(
+        (near, crossed[0], mine_line, packed, own_piece(w_out, 0), encoded, other)
+    )
+
+    blocks = finish(near)
+    crossed[length // 2] = swap_pair(blocks[length // 2])
     other_near, other_finish = line_gather(other)
-    everything = lax.all_gather(
-        encoded.reshape(per_owner, span, width), "an", axis=0, tiled=True
-    )
-    mine_line, other_line = mine_finish(mine_near), other_finish(other_near)
+    packed = swap_pieces(packed, bits[0], 1)
     piece = swap_pair(piece)
-    packed = swap_pieces(packed, bits[0], 1)
-    mine_line, other_line, packed, piece = tie((mine_line, other_line, packed, piece))
+    blocks, crossed = tie((blocks, crossed))
+    for d in range(length):
+        everything = put(everything, blocks[d], d, 0)
+    for d in crossed:
+        everything = put(everything, crossed[d], d, 1)
+    late = [swap_pair(blocks[d]) for d in range(length) if d not in crossed]
+    other_near, piece, packed = tie((other_near, piece, packed))
+
+    other_line = other_finish(other_near)
     for bit in bits[1:]:
         packed = swap_pieces(packed, bit, 1)
     for bit in bits:
         piece = swap_pieces(piece, bit, 0)
+    late, everything = tie((late, everything))
+    for d, a in zip([d for d in range(length) if d not in crossed], late):
+        everything = put(everything, a, d, 1)
+    everything = everything.reshape(n * per_owner, span, width)
     order = (line + jnp.arange(length, dtype=jnp.int32)) % length
-    everything, piece = tie((everything, piece))
 
     chunks = []
     split = 1

time: 340 us -> 337 us (level)
  starting transfers between devices: 36.5 us -> 85.4 us
  waiting for transfers between devices: 202 us -> 158 us
  between operations: 16.5 us -> 3.1 us
  local copies, waits for them, and re-layouts: 12.7 us -> 18.5 us
  other arithmetic: 19.4 us -> 15.9 us
    ppermute x12 -> x16, starting transfers between devices: 30.3 us -> 73.6 us  [on_line(): lax.ppermute(a, 'an', [(i * 2 + y, j * 2 + y) for i, j in moves for y in...]
    ppermute x12 -> x16, waiting for transfers between devices: 150 us -> 118 us  [on_line(): lax.ppermute(a, 'an', [(i * 2 + y, j * 2 + y) for i, j in moves for y in...]
    all_gather x1 -> x0, waiting for transfers between devices: 10.8 us -> none  [shards(): lax.all_gather(encoded.reshape(per_owner, span, width), 'an', axis=0, til...]
    dynamic_update_slice x0 -> x8, local copies, waits for them, and re-layouts: none -> 9.15 us  [put(): lax.dynamic_update_slice_in_dim(everything, a, (d * 2 + over) * rows_each...]
    ppermute x4 -> x8, waiting for transfers between devices: 34.8 us -> 30.1 us  [swap_pair(): return lax.ppermute(a, 'an', [(i, i ^ 1) for i in range(n)])]
    concatenate x3, other arithmetic: 8.66 us -> 4.02 us  [swap_pieces(): return jnp.concatenate([pieces, swap_sa(pieces, bit)], axis=axis)]
    ppermute x4 -> x8, starting transfers between devices: 4.52 us -> 8.76 us  [swap_pair(): return lax.ppermute(a, 'an', [(i, i ^ 1) for i in range(n)])]
    unnamed x33 -> x43, local copies, waits for them, and re-layouts: 7.88 us -> 5.35 us
  transfers between devices with their start and end apart: 21 -> 28, of which waited for: 10 -> 14; matrix products, arithmetic and copies ran while one was open for 10% -> 11% of each run, Pallas kernels for 5% -> 5%
where the time goes in v3:
time: 337 us; the launch traced here: 335 us
  waiting for transfers between devices  158 us (47%)
  starting transfers between devices  85.4 us (25%)
  Pallas kernels  37.4 us (11%)
  local copies, waits for them, and re-layouts  18.5 us (5%)
  matrix products  16.9 us (5%)
  other arithmetic  15.9 us (5%)
    ppermute x16, waiting for transfers between devices, on_line(): lax.ppermute(a, 'an', [(i * 2 + y, j * 2 + y) for i, j in moves for y in...  118 us
    ppermute x16, starting transfers between devices, on_line(): lax.ppermute(a, 'an', [(i * 2 + y, j * 2 + y) for i, j in moves for y in...  73.6 us
    ppermute x8, waiting for transfers between devices, swap_pair(): return lax.ppermute(a, 'an', [(i, i ^ 1) for i in range(n)])  30.1 us
    dot_general x16, matrix products, shards(): total = total + jnp.dot(x, part, preferred_element_type=F32)  16.9 us
    pallas_call x1, Pallas kernels, encode(): pl.pallas_call(functools.partial(encode_kernel, count), grid_spec=pltpu.P...  16.2 us
    pallas_call x1, Pallas kernels, attend(): pl.pallas_call(functools.partial(attend_kernel, head_dim, count), grid_sp...  14.5 us
    ppermute x4, waiting for transfers between devices, swap_sa(): return lax.ppermute(a, 'sa', [(i, i ^ bit) for i in range(s_total)])  10 us
    dynamic_update_slice x8, local copies, waits for them, and re-layouts, put(): lax.dynamic_update_slice_in_dim(everything, a, (d * 2 + over) * rows_each...  9.15 us
  transfers between devices with their start and end apart: 28, of which 14 were waited for; matrix products, arithmetic and copies ran while one was open for 11% of the time, Pallas kernels for 5%

profile of v3, /device:TPU:0, one launch (start us, length us, event | category | flops | bytes accessed | tf_op | source)
XLA Modules:
  0.0 335.3 jit_solution(5197665095803700799)
XLA Ops:
  0.0 2.1 broadcast_select_fusion.11
  2.1 4.0 %collective-permute-start.1 = (bf16[512,512]{1,0:T(8,128)(2,1)S(1)}, bf16[512,512]{1,0:T(8,128)(2,1)S(1)}, u32[]{:S(2)}, u32[]{:S(2)}) collective-permute-start(bf16[512,512]{1,0:T(8,128)(2,1)S(1)} %get-tuple-element.57), channel_id=1, source_target_pairs={{4,0},{5,1},{6,2},{7,3},{0,4},{1,5},{2,6},{3,7},{12,8},{13,9},{14,... | collective-permute-start | bytes 1572872 | tf_op jit(solution)/shard_map/ppermute | solution.py:240
  7.4 5.4 %collective-permute-start.3 = (bf16[512,512]{1,0:T(8,128)(2,1)S(1)}, bf16[512,512]{1,0:T(8,128)(2,1)}, u32[]{:S(2)}, u32[]{:S(2)}) collective-permute-start(bf16[512,512]{1,0:T(8,128)(2,1)S(1)} %get-tuple-element.57), channel_id=1, source_target_pairs={{0,2},{1,3},{2,4},{3,5},{4,6},{5,7},{8,10},{9,11},{10,12},{11,13},... | collective-permute-start | bytes 1572872 | tf_op jit(solution)/shard_map/ppermute | solution.py:240
  12.8 1.5 collective-permute-start
  16.2 16.2 %encode.1 = bf16[512,1024]{1,0:T(8,128)(2,1)} custom-call(s32[4]{0:T(128)} %select_reduce_fusion.2.slots, bf16[8,128,1024]{2,1,0:T(8,128)(2,1)} %refs_3_.1, bf16[8,128,1024]{2,1,0:T(8,128)(2,1)} %refs_3_.1, bf16[8,128,1024]{2,1,0:T(8,128)(2,1)} %refs_3_.1, bf16[8,128,1024]{2,1,0:T(8,128)(2,1)} %refs_3_.1, bf16[1024,4096]{1,0:T(8,128)(2,1)} %refs_4_.1, ...), custom_call_target="tpu_custom_call" | custom-call | flops 8589934592 | bytes 18874368 | tf_op jit(solution)/shard_map/encode/pallas_call | solution.py:55
  36.9 11.3 %collective-permute-start.4 = (bf16[512,1024]{1,0:T(8,128)(2,1)}, bf16[512,1024]{1,0:T(8,128)(2,1)}, u32[]{:S(2)}, u32[]{:S(2)}) collective-permute-start(bf16[512,1024]{1,0:T(8,128)(2,1)} %encode.1), channel_id=1, source_target_pairs={{4,0},{5,1},{6,2},{7,3},{0,4},{1,5},{2,6},{3,7},{12,8},{13,9},{14,... | collective-permute-start | bytes 3145736 | tf_op jit(solution)/shard_map/ppermute | solution.py:240
  49.5 5.6 %collective-permute-start.6 = (bf16[512,1024]{1,0:T(8,128)(2,1)}, bf16[512,1024]{1,0:T(8,128)(2,1)}, u32[]{:S(2)}, u32[]{:S(2)}) collective-permute-start(bf16[512,1024]{1,0:T(8,128)(2,1)} %encode.1), channel_id=1, source_target_pairs={{0,2},{1,3},{2,4},{3,5},{4,6},{5,7},{8,10},{9,11},{10,12},{11,13},... | collective-permute-start | bytes 3145736 | tf_op jit(solution)/shard_map/ppermute | solution.py:240
  55.5 1.5 collective-permute-start.7
  60.3 1.4 constant_dynamic-slice_fusion
  61.7 1.4 broadcast_select_fusion.4
  63.1 31.1 %collective-permute-done.4 = bf16[512,1024]{1,0:T(8,128)(2,1)} collective-permute-done((bf16[512,1024]{1,0:T(8,128)(2,1)}, bf16[512,1024]{1,0:T(8,128)(2,1)}, u32[]{:S(2)}, u32[]{:S(2)}) %collective-permute-start.4) | collective-permute-done | bytes 1048608 | tf_op jit(solution)/shard_map/ppermute | solution.py:240
  94.2 5.5 %collective-permute-done.5 = bf16[512,1024]{1,0:T(8,128)(2,1)} collective-permute-done((bf16[512,1024]{1,0:T(8,128)(2,1)}, bf16[512,1024]{1,0:T(8,128)(2,1)}, u32[]{:S(2)}, u32[]{:S(2)}) %collective-permute-start.5) | collective-permute-done | bytes 1048608 | tf_op jit(solution)/shard_map/ppermute | solution.py:240
  99.7 1.6 collective-permute-start.18
  102.7 1.6 collective-permute-start.11
  104.3 15.5 %collective-permute-start.14 = (bf16[512,512]{1,0:T(8,128)(2,1)}, bf16[512,512]{1,0:T(8,128)(2,1)}, u32[]{:S(2)}, u32[]{:S(2)}) collective-permute-start(bf16[512,512]{1,0:T(8,128)(2,1)} %collective-permute-done), channel_id=1, source_target_pairs={{4,0},{5,1},{6,2},{7,3},{0,4},{1,5},{2,6},{3,7},{12,8},{13,9},{14,... | collective-permute-start | bytes 1572872 | tf_op jit(solution)/shard_map/ppermute | solution.py:240
  119.8 1.5 collective-permute-start.17
  121.3 2.5 fusion.41
  123.7 1.5 fusion.31
  125.2 1.4 fusion.35
  126.6 1.4 fusion.39
  128.0 14.9 %collective-permute-done.14 = bf16[512,512]{1,0:T(8,128)(2,1)} collective-permute-done((bf16[512,512]{1,0:T(8,128)(2,1)}, bf16[512,512]{1,0:T(8,128)(2,1)}, u32[]{:S(2)}, u32[]{:S(2)}) %collective-permute-start.14) | collective-permute-done | bytes 524320 | tf_op jit(solution)/shard_map/ppermute | solution.py:240
  144.2 11.3 %collective-permute-start.16 = (bf16[512,512]{1,0:T(8,128)(2,1)}, bf16[512,512]{1,0:T(8,128)(2,1)S(1)}, u32[]{:S(2)}, u32[]{:S(2)}) collective-permute-start(bf16[512,512]{1,0:T(8,128)(2,1)} %collective-permute-done), channel_id=1, source_target_pairs={{0,2},{1,3},{2,4},{3,5},{4,6},{5,7},{8,10},{9,11},{10,12},{11,13},... | collective-permute-start | bytes 1572872 | tf_op jit(solution)/shard_map/ppermute | solution.py:240
  155.6 3.5 %pad_maximum_fusion.1 = bf16[6144,256]{1,0:T(8,128)(2,1)} fusion(bf16[6144,128]{1,0:T(8,128)(2,1)S(1)} %collective-permute-done.18, bf16[6144,128]{1,0:T(8,128)(2,1)} %collective-permute-done.9), kind=kLoop, calls=%fused_computation.1 | loop fusion | flops 6291456 | bytes 6291456 | tf_op jit(solution)/shard_map/concatenate | solution.py:276
  159.1 6.1 %collective-permute-done.15 = bf16[512,512]{1,0:T(8,128)(2,1)S(1)} collective-permute-done((bf16[512,512]{1,0:T(8,128)(2,1)}, bf16[512,512]{1,0:T(8,128)(2,1)S(1)}, u32[]{:S(2)}, u32[]{:S(2)}) %collective-permute-start.15) | collective-permute-done | bytes 524320 | tf_op jit(solution)/shard_map/ppermute | solution.py:240
  166.3 1.5 collective-permute-start.21
  167.8 2.5 broadcast_select_fusion.1
  172.3 2.3 dynamic_update_slice.24
  174.6 1.4 constant_dynamic-update-slice_fusion.6
  178.9 1.5 collective-permute-start.19
  180.3 10.0 %collective-permute-done.21 = bf16[128,4096]{1,0:T(8,128)(2,1)S(1)} collective-permute-done((bf16[128,4096]{1,0:T(8,128)(2,1)S(1)}, bf16[128,4096]{1,0:T(8,128)(2,1)S(1)}, u32[]{:S(2)}, u32[]{:S(2)}) %collective-permute-start.21) | collective-permute-done | bytes 1048608 | tf_op jit(solution)/shard_map/ppermute | solution.py:237
  191.3 2.1 constant_dynamic-update-slice_fusion.8
  193.5 1.6 fusion.33
  195.0 1.7 collective-permute-done.12
  196.7 19.8 %collective-permute-done.13 = bf16[512,1024]{1,0:T(8,128)(2,1)} collective-permute-done((bf16[512,1024]{1,0:T(8,128)(2,1)S(1)}, bf16[512,1024]{1,0:T(8,128)(2,1)}, u32[]{:S(2)}, u32[]{:S(2)}) %collective-permute-start.13) | collective-permute-done | bytes 1048608 | tf_op jit(solution)/shard_map/ppermute | solution.py:234
  217.8 1.4 constant_dynamic-update-slice_fusion
  220.5 1.5 fusion.13
  224.9 1.5 fusion.18
  227.3 1.5 fusion.26
  230.9 14.5 %attend.1.a = bf16[512,1024]{1,0:T(8,128)(2,1)S(1)} custom-call(s32[16]{0:T(128)S(1)} %broadcast_select_fusion.17.where, bf16[32,128,1024]{2,1,0:T(8,128)(2,1)} %bitcast.17, bf16[32,128,1024]{2,1,0:T(8,128)(2,1)} %bitcast.18, bf16[32,128,1024]{2,1,0:T(8,128)(2,1)} %bitcast.19, bf16[32,128,1024]{2,1,0:T(8,128)(2,1)} %bitcast.20, ...), custom_call_target="tpu_custom_call" | custom-call | flops 9126805504 | bytes 10485760 | tf_op jit(solution)/shard_map/attend/pallas_call | solution.py:138
  245.4 6.7 %terms.1 = (f32[512,1024]{1,0:T(8,128)S(1)}, bf16[512,1024]{1,0:T(8,128)(2,1)S(1)}, bf16[512,1024]{1,0:T(8,128)(2,1)S(1)}, bf16[512,1024]{1,0:T(8,128)(2,1)S(1)}) custom-call(s32[4]{0:T(128)S(1)} %and_select_fusion.6.order, bf16[512,1024]{1,0:T(8,128)(2,1)S(1)} %attend.1.a, bf16[512,4096]{1,0:T(8,128)(2,1)S(1)} %copy-done.2, ...), custom_call_target="tpu_custom_call" | custom-call | flops 4294967296 | bytes 13631488 | tf_op jit(solution)/shard_map/terms/pallas_call | solution.py:192
  252.2 4.4 %collective-permute-start.25 = (bf16[512,1024]{1,0:T(8,128)(2,1)S(1)}, bf16[512,1024]{1,0:T(8,128)(2,1)S(1)}, u32[]{:S(2)}, u32[]{:S(2)}) collective-permute-start(bf16[512,1024]{1,0:T(8,128)(2,1)S(1)} %broadcast_select_fusion), channel_id=1, source_target_pairs={{0,2},{1,3},{6,4},{7,5},{8,10},{9,11},{14,12},{15,13},{16,18},{17,... | collective-permute-start | bytes 3145736 | tf_op jit(solution)/shard_map/ppermute | solution.py:240
  257.9 4.6 %collective-permute-start.23 = (bf16[512,1024]{1,0:T(8,128)(2,1)S(1)}, bf16[512,1024]{1,0:T(8,128)(2,1)S(1)}, u32[]{:S(2)}, u32[]{:S(2)}) collective-permute-start(bf16[512,1024]{1,0:T(8,128)(2,1)S(1)} %get-tuple-element.70), channel_id=1, source_target_pairs={{0,2},{1,3},{2,4},{3,5},{4,6},{5,7},{8,10},{9,11},{10,12},{11,13},... | collective-permute-start | bytes 3145736 | tf_op jit(solution)/shard_map/ppermute | solution.py:240
  262.5 17.6 %collective-permute-done.25 = bf16[512,1024]{1,0:T(8,128)(2,1)S(1)} collective-permute-done((bf16[512,1024]{1,0:T(8,128)(2,1)S(1)}, bf16[512,1024]{1,0:T(8,128)(2,1)S(1)}, u32[]{:S(2)}, u32[]{:S(2)}) %collective-permute-start.25) | collective-permute-done | bytes 1048608 | tf_op jit(solution)/shard_map/ppermute | solution.py:240
  280.5 2.3 collective-permute-start.26
  282.9 15.7 %collective-permute-done.24 = bf16[512,1024]{1,0:T(8,128)(2,1)S(1)} collective-permute-done((bf16[512,1024]{1,0:T(8,128)(2,1)S(1)}, bf16[512,1024]{1,0:T(8,128)(2,1)S(1)}, u32[]{:S(2)}, u32[]{:S(2)}) %collective-permute-start.24) | collective-permute-done | bytes 1048608 | tf_op jit(solution)/shard_map/ppermute | solution.py:240
  298.6 4.0 %collective-permute-done.23 = bf16[512,1024]{1,0:T(8,128)(2,1)S(1)} collective-permute-done((bf16[512,1024]{1,0:T(8,128)(2,1)S(1)}, bf16[512,1024]{1,0:T(8,128)(2,1)S(1)}, u32[]{:S(2)}, u32[]{:S(2)}) %collective-permute-start.23) | collective-permute-done | bytes 1048608 | tf_op jit(solution)/shard_map/ppermute | solution.py:240
  302.6 21.5 %collective-permute-done.26 = bf16[512,1024]{1,0:T(8,128)(2,1)S(1)} collective-permute-done((bf16[512,1024]{1,0:T(8,128)(2,1)S(1)}, bf16[512,1024]{1,0:T(8,128)(2,1)S(1)}, u32[]{:S(2)}, u32[]{:S(2)}) %collective-permute-start.26) | collective-permute-done | bytes 1048608 | tf_op jit(solution)/shard_map/ppermute | solution.py:240
  325.5 8.7 %collective-permute-done.27 = bf16[512,512]{1,0:T(8,128)(2,1)S(1)} collective-permute-done((bf16[512,512]{1,0:T(8,128)(2,1)S(1)}, bf16[512,512]{1,0:T(8,128)(2,1)S(1)}, u32[]{:S(2)}, u32[]{:S(2)}) %collective-permute-start.27) | collective-permute-done | bytes 524320 | tf_op jit(solution)/shard_map/ppermute | solution.py:234
  (111 shorter events, 32.3 us)
Async XLA Ops:
  2.1 31.7 %collective-permute-start.1 = (bf16[512,512]{1,0:T(8,128)(2,1)S(1)}, bf16[512,512]{1,0:T(8,128)(2,1)S(1)}, u32[]{:S(2)}, u32[]{:S(2)}) collective-permute-start(bf16[512,512]{1,0:T(8,128)(2,1)S(1)} %get-tuple-element.57), channel_id=1, source_target_pairs={{4,0},{5,1},{6,2},{7,3},{0,4},{1,5},{2,6},{3,7},{12,8},{13,9},{14,... | collective-permute-start | bytes 1572872 | tf_op jit(solution)/shard_map/ppermute | solution.py:240
  6.1 27.7 %collective-permute-start.2 = (bf16[512,512]{1,0:T(8,128)(2,1)S(1)}, bf16[512,512]{1,0:T(8,128)(2,1)}, u32[]{:S(2)}, u32[]{:S(2)}) collective-permute-start(bf16[512,512]{1,0:T(8,128)(2,1)S(1)} %get-tuple-element.57), channel_id=1, source_target_pairs={{2,0},{3,1},{4,2},{5,3},{6,4},{7,5},{10,8},{11,9},{12,10},{13,11},... | collective-permute-start | bytes 1572872 | tf_op jit(solution)/shard_map/ppermute | solution.py:240
  7.4 26.4 %collective-permute-start.3 = (bf16[512,512]{1,0:T(8,128)(2,1)S(1)}, bf16[512,512]{1,0:T(8,128)(2,1)}, u32[]{:S(2)}, u32[]{:S(2)}) collective-permute-start(bf16[512,512]{1,0:T(8,128)(2,1)S(1)} %get-tuple-element.57), channel_id=1, source_target_pairs={{0,2},{1,3},{2,4},{3,5},{4,6},{5,7},{8,10},{9,11},{10,12},{11,13},... | collective-permute-start | bytes 1572872 | tf_op jit(solution)/shard_map/ppermute | solution.py:240
  12.8 21.0 %collective-permute-start = (bf16[512,512]{1,0:T(8,128)(2,1)}, bf16[512,512]{1,0:T(8,128)(2,1)}, u32[]{:S(2)}, u32[]{:S(2)}) collective-permute-start(bf16[512,512]{1,0:T(8,128)(2,1)} %get-tuple-element.80), channel_id=1, source_target_pairs={{0,1},{1,0},{2,3},{3,2},{4,5},{5,4},{6,7},{7,6},{8,9},{9,8},{10,11... | collective-permute-start | bytes 1572872 | tf_op jit(solution)/shard_map/ppermute | solution.py:234
  16.2 16.2 %copy-start = (bf16[1024,512]{1,0:T(8,128)(2,1)S(1)}, bf16[1024,512]{1,0:T(8,128)(2,1)}, u32[]{:S(2)}) copy-start(bf16[1024,512]{1,0:T(8,128)(2,1)} %refs_11_.1) | copy-start | bytes 3145732
  16.2 16.2 %copy-start.1 = (bf16[1024,512]{1,0:T(8,128)(2,1)S(1)}, bf16[1024,512]{1,0:T(8,128)(2,1)}, u32[]{:S(2)}) copy-start(bf16[1024,512]{1,0:T(8,128)(2,1)} %refs_9_.1) | copy-start | bytes 3145732
  33.8 21.7 %collective-permute-start.8 = (bf16[512,512]{1,0:T(8,128)(2,1)S(1)}, bf16[512,512]{1,0:T(8,128)(2,1)}, u32[]{:S(2)}, u32[]{:S(2)}) collective-permute-start(bf16[512,512]{1,0:T(8,128)(2,1)S(1)} %collective-permute-done.1), channel_id=1, source_target_pairs={{4,6},{5,7},{2,0},{3,1},{12,14},{13,15},{10,8},{11,9},{20,22},{21,... | collective-permute-start | bytes 1572872 | tf_op jit(solution)/shard_map/ppermute | solution.py:240
  36.4 63.3 %collective-permute-start.9 = (bf16[6144,128]{1,0:T(8,128)(2,1)}, bf16[6144,128]{1,0:T(8,128)(2,1)}, u32[]{:S(2)}, u32[]{:S(2)}) collective-permute-start(bf16[6144,128]{1,0:T(8,128)(2,1)} %pad_maximum_fusion.3), channel_id=1, source_target_pairs={{0,1},{1,0},{2,3},{3,2},{4,5},{5,4},{6,7},{7,6},{8,9},{9,8},{10,11... | collective-permute-start | bytes 4718600 | tf_op jit(solution)/shard_map/ppermute | solution.py:234
  36.9 57.4 %collective-permute-start.4 = (bf16[512,1024]{1,0:T(8,128)(2,1)}, bf16[512,1024]{1,0:T(8,128)(2,1)}, u32[]{:S(2)}, u32[]{:S(2)}) collective-permute-start(bf16[512,1024]{1,0:T(8,128)(2,1)} %encode.1), channel_id=1, source_target_pairs={{4,0},{5,1},{6,2},{7,3},{0,4},{1,5},{2,6},{3,7},{12,8},{13,9},{14,... | collective-permute-start | bytes 3145736 | tf_op jit(solution)/shard_map/ppermute | solution.py:240
  48.2 51.5 %collective-permute-start.5 = (bf16[512,1024]{1,0:T(8,128)(2,1)}, bf16[512,1024]{1,0:T(8,128)(2,1)}, u32[]{:S(2)}, u32[]{:S(2)}) collective-permute-start(bf16[512,1024]{1,0:T(8,128)(2,1)} %encode.1), channel_id=1, source_target_pairs={{2,0},{3,1},{4,2},{5,3},{6,4},{7,5},{10,8},{11,9},{12,10},{13,11},... | collective-permute-start | bytes 3145736 | tf_op jit(solution)/shard_map/ppermute | solution.py:240
  49.5 50.2 %collective-permute-start.6 = (bf16[512,1024]{1,0:T(8,128)(2,1)}, bf16[512,1024]{1,0:T(8,128)(2,1)}, u32[]{:S(2)}, u32[]{:S(2)}) collective-permute-start(bf16[512,1024]{1,0:T(8,128)(2,1)} %encode.1), channel_id=1, source_target_pairs={{0,2},{1,3},{2,4},{3,5},{4,6},{5,7},{8,10},{9,11},{10,12},{11,13},... | collective-permute-start | bytes 3145736 | tf_op jit(solution)/shard_map/ppermute | solution.py:240
  55.5 44.2 %collective-permute-start.7 = (bf16[512,1024]{1,0:T(8,128)(2,1)}, bf16[512,1024]{1,0:T(8,128)(2,1)}, u32[]{:S(2)}, u32[]{:S(2)}) collective-permute-start(bf16[512,1024]{1,0:T(8,128)(2,1)} %encode.1), channel_id=1, source_target_pairs={{0,1},{1,0},{2,3},{3,2},{4,5},{5,4},{6,7},{7,6},{8,9},{9,8},{10,11... | collective-permute-start | bytes 3145736 | tf_op jit(solution)/shard_map/ppermute | solution.py:234
  60.2 61.0 %copy-start.4 = (bf16[4096,512]{1,0:T(8,128)(2,1)S(1)}, bf16[4096,512]{1,0:T(8,128)(2,1)}, u32[]{:S(2)}) copy-start(bf16[4096,512]{1,0:T(8,128)(2,1)} %param.10) | copy-start | bytes 12582916
  99.7 44.6 %collective-permute-start.18 = (bf16[6144,128]{1,0:T(8,128)(2,1)}, bf16[6144,128]{1,0:T(8,128)(2,1)S(1)}, u32[]{:S(2)}, u32[]{:S(2)}) collective-permute-start(bf16[6144,128]{1,0:T(8,128)(2,1)} %collective-permute-done.9), channel_id=1, source_target_pairs={{0,16},{8,24},{16,0},{24,8},{1,17},{9,25},{17,1},{25,9},{2,18},{10... | collective-permute-start | bytes 4718600 | tf_op jit(solution)/shard_map/ppermute | solution.py:237
  101.4 66.4 %collective-permute-start.10 = (bf16[512,1024]{1,0:T(8,128)(2,1)}, bf16[512,1024]{1,0:T(8,128)(2,1)S(1)}, u32[]{:S(2)}, u32[]{:S(2)}) collective-permute-start(bf16[512,1024]{1,0:T(8,128)(2,1)} %collective-permute-done.4), channel_id=1, source_target_pairs={{4,6},{5,7},{2,0},{3,1},{12,14},{13,15},{10,8},{11,9},{20,22},{21,... | collective-permute-start | bytes 3145736 | tf_op jit(solution)/shard_map/ppermute | solution.py:240
  102.7 67.6 %collective-permute-start.11 = (bf16[512,1024]{1,0:T(8,128)(2,1)}, bf16[512,1024]{1,0:T(8,128)(2,1)S(1)}, u32[]{:S(2)}, u32[]{:S(2)}) collective-permute-start(bf16[512,1024]{1,0:T(8,128)(2,1)} %collective-permute-done.4), channel_id=1, source_target_pairs={{0,1},{1,0},{2,3},{3,2},{4,5},{5,4},{6,7},{7,6},{8,9},{9,8},{10,11... | collective-permute-start | bytes 3145736 | tf_op jit(solution)/shard_map/ppermute | solution.py:234
  104.3 38.6 %collective-permute-start.14 = (bf16[512,512]{1,0:T(8,128)(2,1)}, bf16[512,512]{1,0:T(8,128)(2,1)}, u32[]{:S(2)}, u32[]{:S(2)}) collective-permute-start(bf16[512,512]{1,0:T(8,128)(2,1)} %collective-permute-done), channel_id=1, source_target_pairs={{4,0},{5,1},{6,2},{7,3},{0,4},{1,5},{2,6},{3,7},{12,8},{13,9},{14,... | collective-permute-start | bytes 1572872 | tf_op jit(solution)/shard_map/ppermute | solution.py:240
  119.8 46.5 %collective-permute-start.17 = (bf16[128,4096]{1,0:T(8,128)(2,1)S(1)}, bf16[128,4096]{1,0:T(8,128)(2,1)S(1)}, u32[]{:S(2)}, u32[]{:S(2)}) collective-permute-start(bf16[128,4096]{1,0:T(8,128)(2,1)S(1)} %constant_dynamic-slice_fusion), channel_id=1, source_target_pairs={{0,1},{1,0},{2,3},{3,2},{4,5},{5,4},{6,7},{7,6},{8,9},{9,8},{10,11... | collective-permute-start | bytes 3145736 | tf_op jit(solution)/shard_map/ppermute | solution.py:234
  143.0 22.2 %collective-permute-start.15 = (bf16[512,512]{1,0:T(8,128)(2,1)}, bf16[512,512]{1,0:T(8,128)(2,1)S(1)}, u32[]{:S(2)}, u32[]{:S(2)}) collective-permute-start(bf16[512,512]{1,0:T(8,128)(2,1)} %collective-permute-done), channel_id=1, source_target_pairs={{2,0},{3,1},{4,2},{5,3},{6,4},{7,5},{10,8},{11,9},{12,10},{13,11},... | collective-permute-start | bytes 1572872 | tf_op jit(solution)/shard_map/ppermute | solution.py:240
  144.2 22.0 %collective-permute-start.16 = (bf16[512,512]{1,0:T(8,128)(2,1)}, bf16[512,512]{1,0:T(8,128)(2,1)S(1)}, u32[]{:S(2)}, u32[]{:S(2)}) collective-permute-start(bf16[512,512]{1,0:T(8,128)(2,1)} %collective-permute-done), channel_id=1, source_target_pairs={{0,2},{1,3},{2,4},{3,5},{4,6},{5,7},{8,10},{9,11},{10,12},{11,13},... | collective-permute-start | bytes 1572872 | tf_op jit(solution)/shard_map/ppermute | solution.py:240
  165.2 2.6 copy-start.13
  166.3 1.5 copy-start.15
  166.3 24.1 %copy-start.9 = (bf16[128,4096]{1,0:T(8,128)(2,1)}, bf16[128,4096]{1,0:T(8,128)(2,1)S(1)}, u32[]{:S(2)}) copy-start(bf16[128,4096]{1,0:T(8,128)(2,1)S(1)} %collective-permute-done.17) | copy-start | bytes 3145732
  166.3 24.0 %collective-permute-start.21 = (bf16[128,4096]{1,0:T(8,128)(2,1)S(1)}, bf16[128,4096]{1,0:T(8,128)(2,1)S(1)}, u32[]{:S(2)}, u32[]{:S(2)}) collective-permute-start(bf16[128,4096]{1,0:T(8,128)(2,1)S(1)} %collective-permute-done.17), channel_id=1, source_target_pairs={{0,16},{8,24},{16,0},{24,8},{1,17},{9,25},{17,1},{25,9},{2,18},{10... | collective-permute-start | bytes 3145736 | tf_op jit(solution)/shard_map/ppermute | solution.py:237
  170.3 1.0 copy-start.19
  170.3 26.4 %collective-permute-start.12 = (bf16[512,1024]{1,0:T(8,128)(2,1)}, bf16[512,1024]{1,0:T(8,128)(2,1)}, u32[]{:S(2)}, u32[]{:S(2)}) collective-permute-start(bf16[512,1024]{1,0:T(8,128)(2,1)} %get-tuple-element.48), channel_id=1, source_target_pairs={{0,1},{1,0},{2,3},{3,2},{4,5},{5,4},{6,7},{7,6},{8,9},{9,8},{10,11... | collective-permute-start | bytes 3145736 | tf_op jit(solution)/shard_map/ppermute | solution.py:234
  171.3 45.2 %collective-permute-start.13 = (bf16[512,1024]{1,0:T(8,128)(2,1)S(1)}, bf16[512,1024]{1,0:T(8,128)(2,1)}, u32[]{:S(2)}, u32[]{:S(2)}) collective-permute-start(bf16[512,1024]{1,0:T(8,128)(2,1)S(1)} %get-tuple-element.49), channel_id=1, source_target_pairs={{0,1},{1,0},{2,3},{3,2},{4,5},{5,4},{6,7},{7,6},{8,9},{9,8},{10,11... | collective-permute-start | bytes 3145736 | tf_op jit(solution)/shard_map/ppermute | solution.py:234
  174.6 4.1 %copy-start.20 = (bf16[512,1024]{1,0:T(8,128)(2,1)S(1)}, bf16[512,1024]{1,0:T(8,128)(2,1)}, u32[]{:S(2)}) copy-start(bf16[512,1024]{1,0:T(8,128)(2,1)} %copy-done.19) | copy-start | bytes 3145732
  178.8 45.1 %collective-permute-start.20 = (bf16[6144,256]{1,0:T(8,128)(2,1)}, bf16[6144,256]{1,0:T(8,128)(2,1)S(1)}, u32[]{:S(2)}, u32[]{:S(2)}) collective-permute-start(bf16[6144,256]{1,0:T(8,128)(2,1)} %pad_maximum_fusion.1), channel_id=1, source_target_pairs={{0,8},{8,0},{16,24},{24,16},{1,9},{9,1},{17,25},{25,17},{2,10},{10... | collective-permute-start | bytes 9437192 | tf_op jit(solution)/shard_map/ppermute | solution.py:237
  178.9 40.4 %collective-permute-start.19 = (bf16[512,512]{1,0:T(8,128)(2,1)}, bf16[512,512]{1,0:T(8,128)(2,1)S(1)}, u32[]{:S(2)}, u32[]{:S(2)}) collective-permute-start(bf16[512,512]{1,0:T(8,128)(2,1)} %collective-permute-done.14), channel_id=1, source_target_pairs={{4,6},{5,7},{2,0},{3,1},{12,14},{13,15},{10,8},{11,9},{20,22},{21,... | collective-permute-start | bytes 1572872 | tf_op jit(solution)/shard_map/ppermute | solution.py:240
  191.3 31.8 %collective-permute-start.22 = (bf16[256,4096]{1,0:T(8,128)(2,1)S(1)}, bf16[256,4096]{1,0:T(8,128)(2,1)S(1)}, u32[]{:S(2)}, u32[]{:S(2)}) collective-permute-start(bf16[256,4096]{1,0:T(8,128)(2,1)S(1)} %pad_maximum_fusion.2), channel_id=1, source_target_pairs={{0,8},{8,0},{16,24},{24,16},{1,9},{9,1},{17,25},{25,17},{2,10},{10... | collective-permute-start | bytes 6291464 | tf_op jit(solution)/shard_map/ppermute | solution.py:237
  193.5 25.9 %copy-start.16 = (bf16[512,512]{1,0:T(8,128)(2,1)S(1)}, bf16[512,512]{1,0:T(8,128)(2,1)}, u32[]{:S(2)}) copy-start(bf16[512,512]{1,0:T(8,128)(2,1)} %copy-done.15) | copy-start | bytes 1572868
  193.5 26.3 %copy-start.14 = (bf16[512,512]{1,0:T(8,128)(2,1)S(1)}, bf16[512,512]{1,0:T(8,128)(2,1)}, u32[]{:S(2)}) copy-start(bf16[512,512]{1,0:T(8,128)(2,1)} %copy-done.13) | copy-start | bytes 1572868
  217.8 2.4 copy-start.5
  217.8 2.4 copy-start.6
  217.8 2.4 copy-start.7
  217.8 2.6 copy-start.8
  219.3 3.8 %copy-start.3 = (bf16[4096,1024]{1,0:T(8,128)(2,1)}, bf16[4096,1024]{1,0:T(8,128)(2,1)S(1)}, u32[]{:S(2)}) copy-start(bf16[4096,1024]{1,0:T(8,128)(2,1)S(1)} %constant_dynamic-update-slice_fusion) | copy-start | bytes 25165828
  220.5 2.6 copy-start.10
  220.5 3.1 copy-start.12
  224.9 3.9 %copy-start.17 = (bf16[512,512]{1,0:T(8,128)(2,1)S(1)}, bf16[512,512]{1,0:T(8,128)(2,1)}, u32[]{:S(2)}) copy-start(bf16[512,512]{1,0:T(8,128)(2,1)} %copy-done.15) | copy-start | bytes 1572868
  229.7 1.0 copy-start.18
  230.9 14.5 %copy-start.2 = (bf16[512,4096]{1,0:T(8,128)(2,1)S(1)}, bf16[512,4096]{1,0:T(8,128)(2,1)}, u32[]{:S(2)}) copy-start(bf16[512,4096]{1,0:T(8,128)(2,1)} %near.1) | copy-start | bytes 12582916
  252.2 27.9 %collective-permute-start.25 = (bf16[512,1024]{1,0:T(8,128)(2,1)S(1)}, bf16[512,1024]{1,0:T(8,128)(2,1)S(1)}, u32[]{:S(2)}, u32[]{:S(2)}) collective-permute-start(bf16[512,1024]{1,0:T(8,128)(2,1)S(1)} %broadcast_select_fusion), channel_id=1, source_target_pairs={{0,2},{1,3},{6,4},{7,5},{8,10},{9,11},{14,12},{15,13},{16,18},{17,... | collective-permute-start | bytes 3145736 | tf_op jit(solution)/shard_map/ppermute | solution.py:240
  256.6 42.0 %collective-permute-start.24 = (bf16[512,1024]{1,0:T(8,128)(2,1)S(1)}, bf16[512,1024]{1,0:T(8,128)(2,1)S(1)}, u32[]{:S(2)}, u32[]{:S(2)}) collective-permute-start(bf16[512,1024]{1,0:T(8,128)(2,1)S(1)} %get-tuple-element.71), channel_id=1, source_target_pairs={{2,0},{3,1},{4,2},{5,3},{6,4},{7,5},{10,8},{11,9},{12,10},{13,11},... | collective-permute-start | bytes 3145736 | tf_op jit(solution)/shard_map/ppermute | solution.py:240
  257.9 44.7 %collective-permute-start.23 = (bf16[512,1024]{1,0:T(8,128)(2,1)S(1)}, bf16[512,1024]{1,0:T(8,128)(2,1)S(1)}, u32[]{:S(2)}, u32[]{:S(2)}) collective-permute-start(bf16[512,1024]{1,0:T(8,128)(2,1)S(1)} %get-tuple-element.70), channel_id=1, source_target_pairs={{0,2},{1,3},{2,4},{3,5},{4,6},{5,7},{8,10},{9,11},{10,12},{11,13},... | collective-permute-start | bytes 3145736 | tf_op jit(solution)/shard_map/ppermute | solution.py:240
  280.5 43.5 %collective-permute-start.26 = (bf16[512,1024]{1,0:T(8,128)(2,1)S(1)}, bf16[512,1024]{1,0:T(8,128)(2,1)S(1)}, u32[]{:S(2)}, u32[]{:S(2)}) collective-permute-start(bf16[512,1024]{1,0:T(8,128)(2,1)S(1)} %add_convert_fusion.1), channel_id=1, source_target_pairs={{4,0},{5,1},{6,2},{7,3},{0,4},{1,5},{2,6},{3,7},{12,8},{13,9},{14,... | collective-permute-start | bytes 3145736 | tf_op jit(solution)/shard_map/ppermute | solution.py:240
  324.9 9.2 %collective-permute-start.27 = (bf16[512,512]{1,0:T(8,128)(2,1)S(1)}, bf16[512,512]{1,0:T(8,128)(2,1)S(1)}, u32[]{:S(2)}, u32[]{:S(2)}) collective-permute-start(bf16[512,512]{1,0:T(8,128)(2,1)S(1)} %broadcast_select_fusion.9), channel_id=1, source_target_pairs={{0,1},{1,0},{2,3},{3,2},{4,5},{5,4},{6,7},{7,6},{8,9},{9,8},{10,11... | collective-permute-start | bytes 1572872 | tf_op jit(solution)/shard_map/ppermute | solution.py:234
  (1 other events, 1.0 us)

commit v4 on v3

--- a/solution.py
+++ b/solution.py
@@ -258,19 +258,26 @@
 
         return [two, after, before], finish
 
+    def sides(a):
+        left, right = a[:, :local], a[:, local:]
+        return jnp.where(first, left, right), jnp.where(first, right, left)
+
     def line_sum(hold, send):
         if length == 4:
             one, two, three = send
             relay = on_line(jnp.where(line == 0, three, one), [(0, 1), (3, 2)])
             after = on_line(one, [(i, i + 1) for i in range(3)])
             before = on_line(three, [(i + 1, i) for i in range(3)])
-            two = from_place((two.astype(F32) + relay.astype(F32)).astype(BF16), 2)
-            got = [after, before, two]
-        else:
-            got = [from_place(a, length - 1 - i) for i, a in enumerate(send)]
-        for a in got:
-            hold = hold + a.astype(F32)
-        return hold
+            mine, given = sides((two.astype(F32) + relay.astype(F32)).astype(BF16))
+            mine = from_place(mine, 2)
+            given = lax.ppermute(given, "an", [(i, (i + 4) % 8 ^ 1) for i in range(n)])
+            keep, give = sides(hold + after.astype(F32) + before.astype(F32))
+            got = swap_pair(give.astype(BF16))
+            return keep + mine.astype(F32), got.astype(F32) + given.astype(F32)
+        for i, a in enumerate(send):
+            hold = hold + from_place(a, length - 1 - i).astype(F32)
+        keep, give = sides(hold)
+        return keep, swap_pair(give.astype(BF16))
 
     def swap_pieces(pieces, bit, axis):
         return jnp.concatenate([pieces, swap_sa(pieces, bit)], axis=axis)
@@ -377,9 +384,7 @@
             min(4, asked // NEIGH),
         )
         hold, *send = terms(order, attended, w_out, piece)
-        summed = line_sum(hold, send).astype(BF16)
-        left, right = summed[:, :local], summed[:, local:]
-        chunks.append((jnp.where(first, left, right), swap_pair(jnp.where(first, right, left))))
+        chunks.append([a.astype(BF16) for a in line_sum(hold, send)])
     keep = jnp.concatenate([c[0] for c in chunks], axis=0)
     got = jnp.concatenate([c[1] for c in chunks], axis=0)
     return jnp.concatenate([jnp.where(first, keep, got), jnp.where(first, got, keep)], axis=0)

time: 337 us -> 334 us (level)
  waiting for transfers between devices: 158 us -> 152 us
    ppermute x8, waiting for transfers between devices: 30.1 us -> 21.5 us  [swap_pair(): return lax.ppermute(a, 'an', [(i, i ^ 1) for i in range(n)])]
    ppermute x0 -> x1, waiting for transfers between devices: none -> 7.22 us  [line_sum(): given = lax.ppermute(given, 'an', [(i, (i + 4) % 8 ^ 1) for i in range(n)])]
    ppermute x16, waiting for transfers between devices: 118 us -> 114 us  [on_line(): lax.ppermute(a, 'an', [(i * 2 + y, j * 2 + y) for i, j in moves for y in...]
  transfers between devices with their start and end apart: 28 -> 29, of which waited for: 14 -> 14; matrix products, arithmetic and copies ran while one was open for 11% -> 11% of each run, Pallas kernels for 5% -> 5%
where the time goes in v4:
time: 334 us; the launch traced here: 333 us
  waiting for transfers between devices  152 us (46%)
  starting transfers between devices  88.7 us (27%)
  Pallas kernels  37.3 us (11%)
  local copies, waits for them, and re-layouts  18.5 us (6%)
  matrix products  16.9 us (5%)
  other arithmetic  16.2 us (5%)
    ppermute x16, waiting for transfers between devices, on_line(): lax.ppermute(a, 'an', [(i * 2 + y, j * 2 + y) for i, j in moves for y in...  114 us
    ppermute x16, starting transfers between devices, on_line(): lax.ppermute(a, 'an', [(i * 2 + y, j * 2 + y) for i, j in moves for y in...  73.8 us
    ppermute x8, waiting for transfers between devices, swap_pair(): return lax.ppermute(a, 'an', [(i, i ^ 1) for i in range(n)])  21.5 us
    dot_general x16, matrix products, shards(): total = total + jnp.dot(x, part, preferred_element_type=F32)  16.9 us
    pallas_call x1, Pallas kernels, encode(): pl.pallas_call(functools.partial(encode_kernel, count), grid_spec=pltpu.P...  16.2 us
    pallas_call x1, Pallas kernels, attend(): pl.pallas_call(functools.partial(attend_kernel, head_dim, count), grid_sp...  14.4 us
    ppermute x4, waiting for transfers between devices, swap_sa(): return lax.ppermute(a, 'sa', [(i, i ^ bit) for i in range(s_total)])  10 us
    dynamic_update_slice x8, local copies, waits for them, and re-layouts, put(): lax.dynamic_update_slice_in_dim(everything, a, (d * 2 + over) * rows_each...  9.15 us
  transfers between devices with their start and end apart: 29, of which 14 were waited for; matrix products, arithmetic and copies ran while one was open for 11% of the time, Pallas kernels for 5%

profile of v4, /device:TPU:0, one launch (start us, length us, event | category | flops | bytes accessed | tf_op | source)
XLA Modules:
  0.0 333.3 jit_solution(3783026248761143723)
XLA Ops:
  0.0 2.1 broadcast_select_fusion.11
  2.1 4.0 %collective-permute-start.1 = (bf16[512,512]{1,0:T(8,128)(2,1)S(1)}, bf16[512,512]{1,0:T(8,128)(2,1)S(1)}, u32[]{:S(2)}, u32[]{:S(2)}) collective-permute-start(bf16[512,512]{1,0:T(8,128)(2,1)S(1)} %get-tuple-element.57), channel_id=1, source_target_pairs={{4,0},{5,1},{6,2},{7,3},{0,4},{1,5},{2,6},{3,7},{12,8},{13,9},{14,... | collective-permute-start | bytes 1572872 | tf_op jit(solution)/shard_map/ppermute | solution.py:240
  7.4 5.4 %collective-permute-start.3 = (bf16[512,512]{1,0:T(8,128)(2,1)S(1)}, bf16[512,512]{1,0:T(8,128)(2,1)}, u32[]{:S(2)}, u32[]{:S(2)}) collective-permute-start(bf16[512,512]{1,0:T(8,128)(2,1)S(1)} %get-tuple-element.57), channel_id=1, source_target_pairs={{0,2},{1,3},{2,4},{3,5},{4,6},{5,7},{8,10},{9,11},{10,12},{11,13},... | collective-permute-start | bytes 1572872 | tf_op jit(solution)/shard_map/ppermute | solution.py:240
  12.8 1.5 collective-permute-start
  16.2 16.2 %encode.1 = bf16[512,1024]{1,0:T(8,128)(2,1)} custom-call(s32[4]{0:T(128)} %select_reduce_fusion.2.slots, bf16[8,128,1024]{2,1,0:T(8,128)(2,1)} %refs_3_.1, bf16[8,128,1024]{2,1,0:T(8,128)(2,1)} %refs_3_.1, bf16[8,128,1024]{2,1,0:T(8,128)(2,1)} %refs_3_.1, bf16[8,128,1024]{2,1,0:T(8,128)(2,1)} %refs_3_.1, bf16[1024,4096]{1,0:T(8,128)(2,1)} %refs_4_.1, ...), custom_call_target="tpu_custom_call" | custom-call | flops 8589934592 | bytes 18874368 | tf_op jit(solution)/shard_map/encode/pallas_call | solution.py:55
  36.9 11.3 %collective-permute-start.4 = (bf16[512,1024]{1,0:T(8,128)(2,1)}, bf16[512,1024]{1,0:T(8,128)(2,1)}, u32[]{:S(2)}, u32[]{:S(2)}) collective-permute-start(bf16[512,1024]{1,0:T(8,128)(2,1)} %encode.1), channel_id=1, source_target_pairs={{4,0},{5,1},{6,2},{7,3},{0,4},{1,5},{2,6},{3,7},{12,8},{13,9},{14,... | collective-permute-start | bytes 3145736 | tf_op jit(solution)/shard_map/ppermute | solution.py:240
  49.5 5.6 %collective-permute-start.6 = (bf16[512,1024]{1,0:T(8,128)(2,1)}, bf16[512,1024]{1,0:T(8,128)(2,1)}, u32[]{:S(2)}, u32[]{:S(2)}) collective-permute-start(bf16[512,1024]{1,0:T(8,128)(2,1)} %encode.1), channel_id=1, source_target_pairs={{0,2},{1,3},{2,4},{3,5},{4,6},{5,7},{8,10},{9,11},{10,12},{11,13},... | collective-permute-start | bytes 3145736 | tf_op jit(solution)/shard_map/ppermute | solution.py:240
  55.5 1.5 collective-permute-start.7
  60.3 1.4 constant_dynamic-slice_fusion
  61.8 1.4 broadcast_select_fusion.4
  63.2 31.1 %collective-permute-done.4 = bf16[512,1024]{1,0:T(8,128)(2,1)} collective-permute-done((bf16[512,1024]{1,0:T(8,128)(2,1)}, bf16[512,1024]{1,0:T(8,128)(2,1)}, u32[]{:S(2)}, u32[]{:S(2)}) %collective-permute-start.4) | collective-permute-done | bytes 1048608 | tf_op jit(solution)/shard_map/ppermute | solution.py:240
  94.2 5.4 %collective-permute-done.5 = bf16[512,1024]{1,0:T(8,128)(2,1)} collective-permute-done((bf16[512,1024]{1,0:T(8,128)(2,1)}, bf16[512,1024]{1,0:T(8,128)(2,1)}, u32[]{:S(2)}, u32[]{:S(2)}) %collective-permute-start.5) | collective-permute-done | bytes 1048608 | tf_op jit(solution)/shard_map/ppermute | solution.py:240
  99.7 1.6 collective-permute-start.18
  102.7 1.6 collective-permute-start.11
  104.3 15.5 %collective-permute-start.14 = (bf16[512,512]{1,0:T(8,128)(2,1)}, bf16[512,512]{1,0:T(8,128)(2,1)}, u32[]{:S(2)}, u32[]{:S(2)}) collective-permute-start(bf16[512,512]{1,0:T(8,128)(2,1)} %collective-permute-done), channel_id=1, source_target_pairs={{4,0},{5,1},{6,2},{7,3},{0,4},{1,5},{2,6},{3,7},{12,8},{13,9},{14,... | collective-permute-start | bytes 1572872 | tf_op jit(solution)/shard_map/ppermute | solution.py:240
  119.8 1.5 collective-permute-start.17
  121.3 2.5 fusion.41
  123.8 1.4 fusion.31
  125.2 1.4 fusion.35
  126.6 1.4 fusion.39
  128.0 14.9 %collective-permute-done.14 = bf16[512,512]{1,0:T(8,128)(2,1)} collective-permute-done((bf16[512,512]{1,0:T(8,128)(2,1)}, bf16[512,512]{1,0:T(8,128)(2,1)}, u32[]{:S(2)}, u32[]{:S(2)}) %collective-permute-start.14) | collective-permute-done | bytes 524320 | tf_op jit(solution)/shard_map/ppermute | solution.py:240
  144.3 11.3 %collective-permute-start.16 = (bf16[512,512]{1,0:T(8,128)(2,1)}, bf16[512,512]{1,0:T(8,128)(2,1)S(1)}, u32[]{:S(2)}, u32[]{:S(2)}) collective-permute-start(bf16[512,512]{1,0:T(8,128)(2,1)} %collective-permute-done), channel_id=1, source_target_pairs={{0,2},{1,3},{2,4},{3,5},{4,6},{5,7},{8,10},{9,11},{10,12},{11,13},... | collective-permute-start | bytes 1572872 | tf_op jit(solution)/shard_map/ppermute | solution.py:240
  155.6 3.5 %pad_maximum_fusion.1 = bf16[6144,256]{1,0:T(8,128)(2,1)} fusion(bf16[6144,128]{1,0:T(8,128)(2,1)S(1)} %collective-permute-done.18, bf16[6144,128]{1,0:T(8,128)(2,1)} %collective-permute-done.9), kind=kLoop, calls=%fused_computation.1 | loop fusion | flops 6291456 | bytes 6291456 | tf_op jit(solution)/shard_map/concatenate | solution.py:283
  159.1 6.1 %collective-permute-done.15 = bf16[512,512]{1,0:T(8,128)(2,1)S(1)} collective-permute-done((bf16[512,512]{1,0:T(8,128)(2,1)}, bf16[512,512]{1,0:T(8,128)(2,1)S(1)}, u32[]{:S(2)}, u32[]{:S(2)}) %collective-permute-start.15) | collective-permute-done | bytes 524320 | tf_op jit(solution)/shard_map/ppermute | solution.py:240
  166.3 1.5 collective-permute-start.21
  167.8 2.5 broadcast_select_fusion.1
  172.3 2.3 dynamic_update_slice.24
  178.9 1.5 collective-permute-start.19
  180.3 10.0 %collective-permute-done.21 = bf16[128,4096]{1,0:T(8,128)(2,1)S(1)} collective-permute-done((bf16[128,4096]{1,0:T(8,128)(2,1)S(1)}, bf16[128,4096]{1,0:T(8,128)(2,1)S(1)}, u32[]{:S(2)}, u32[]{:S(2)}) %collective-permute-start.21) | collective-permute-done | bytes 1048608 | tf_op jit(solution)/shard_map/ppermute | solution.py:237
  191.3 2.1 constant_dynamic-update-slice_fusion.8
  193.5 1.6 fusion.33
  195.1 1.7 collective-permute-done.12
  196.7 19.8 %collective-permute-done.13 = bf16[512,1024]{1,0:T(8,128)(2,1)} collective-permute-done((bf16[512,1024]{1,0:T(8,128)(2,1)S(1)}, bf16[512,1024]{1,0:T(8,128)(2,1)}, u32[]{:S(2)}, u32[]{:S(2)}) %collective-permute-start.13) | collective-permute-done | bytes 1048608 | tf_op jit(solution)/shard_map/ppermute | solution.py:234
  217.8 1.4 constant_dynamic-update-slice_fusion
  220.4 1.6 fusion.13
  224.9 1.5 fusion.18
  227.3 1.5 fusion.26
  230.9 14.4 %attend.1.a = bf16[512,1024]{1,0:T(8,128)(2,1)S(1)} custom-call(s32[16]{0:T(128)S(1)} %broadcast_select_fusion.17.where, bf16[32,128,1024]{2,1,0:T(8,128)(2,1)} %bitcast.17, bf16[32,128,1024]{2,1,0:T(8,128)(2,1)} %bitcast.18, bf16[32,128,1024]{2,1,0:T(8,128)(2,1)} %bitcast.19, bf16[32,128,1024]{2,1,0:T(8,128)(2,1)} %bitcast.20, ...), custom_call_target="tpu_custom_call" | custom-call | flops 9126805504 | bytes 10485760 | tf_op jit(solution)/shard_map/attend/pallas_call | solution.py:138
  245.3 6.7 %terms.1 = (f32[512,1024]{1,0:T(8,128)S(1)}, bf16[512,1024]{1,0:T(8,128)(2,1)S(1)}, bf16[512,1024]{1,0:T(8,128)(2,1)S(1)}, bf16[512,1024]{1,0:T(8,128)(2,1)S(1)}) custom-call(s32[4]{0:T(128)S(1)} %and_select_fusion.6.order, bf16[512,1024]{1,0:T(8,128)(2,1)S(1)} %attend.1.a, bf16[512,4096]{1,0:T(8,128)(2,1)S(1)} %copy-done.2, ...), custom_call_target="tpu_custom_call" | custom-call | flops 4294967296 | bytes 13631488 | tf_op jit(solution)/shard_map/terms/pallas_call | solution.py:192
  252.1 4.3 %collective-permute-start.25 = (bf16[512,1024]{1,0:T(8,128)(2,1)S(1)}, bf16[512,1024]{1,0:T(8,128)(2,1)S(1)}, u32[]{:S(2)}, u32[]{:S(2)}) collective-permute-start(bf16[512,1024]{1,0:T(8,128)(2,1)S(1)} %broadcast_select_fusion), channel_id=1, source_target_pairs={{0,2},{1,3},{6,4},{7,5},{8,10},{9,11},{14,12},{15,13},{16,18},{17,... | collective-permute-start | bytes 3145736 | tf_op jit(solution)/shard_map/ppermute | solution.py:240
  257.7 4.6 %collective-permute-start.23 = (bf16[512,1024]{1,0:T(8,128)(2,1)S(1)}, bf16[512,1024]{1,0:T(8,128)(2,1)S(1)}, u32[]{:S(2)}, u32[]{:S(2)}) collective-permute-start(bf16[512,1024]{1,0:T(8,128)(2,1)S(1)} %get-tuple-element.70), channel_id=1, source_target_pairs={{0,2},{1,3},{2,4},{3,5},{4,6},{5,7},{8,10},{9,11},{10,12},{11,13},... | collective-permute-start | bytes 3145736 | tf_op jit(solution)/shard_map/ppermute | solution.py:240
  262.3 17.6 %collective-permute-done.25 = bf16[512,1024]{1,0:T(8,128)(2,1)S(1)} collective-permute-done((bf16[512,1024]{1,0:T(8,128)(2,1)S(1)}, bf16[512,1024]{1,0:T(8,128)(2,1)S(1)}, u32[]{:S(2)}, u32[]{:S(2)}) %collective-permute-start.25) | collective-permute-done | bytes 1048608 | tf_op jit(solution)/shard_map/ppermute | solution.py:240
  280.4 2.8 collective-permute-start.28
  283.2 8.0 %collective-permute-done.24 = bf16[512,1024]{1,0:T(8,128)(2,1)S(1)} collective-permute-done((bf16[512,1024]{1,0:T(8,128)(2,1)S(1)}, bf16[512,1024]{1,0:T(8,128)(2,1)S(1)}, u32[]{:S(2)}, u32[]{:S(2)}) %collective-permute-start.24) | collective-permute-done | bytes 1048608 | tf_op jit(solution)/shard_map/ppermute | solution.py:240
  291.3 11.1 %collective-permute-done.23 = bf16[512,1024]{1,0:T(8,128)(2,1)S(1)} collective-permute-done((bf16[512,1024]{1,0:T(8,128)(2,1)S(1)}, bf16[512,1024]{1,0:T(8,128)(2,1)S(1)}, u32[]{:S(2)}, u32[]{:S(2)}) %collective-permute-start.23) | collective-permute-done | bytes 1048608 | tf_op jit(solution)/shard_map/ppermute | solution.py:240
  303.8 2.6 collective-permute-start.26
  306.4 7.2 %collective-permute-done.28 = bf16[512,512]{1,0:T(8,128)(2,1)S(1)} collective-permute-done((bf16[512,512]{1,0:T(8,128)(2,1)S(1)}, bf16[512,512]{1,0:T(8,128)(2,1)S(1)}, u32[]{:S(2)}, u32[]{:S(2)}) %collective-permute-start.28) | collective-permute-done | bytes 524320 | tf_op jit(solution)/shard_map/ppermute | solution.py:273
  313.6 18.0 %collective-permute-done.26 = bf16[512,512]{1,0:T(8,128)(2,1)S(1)} collective-permute-done((bf16[512,512]{1,0:T(8,128)(2,1)S(1)}, bf16[512,512]{1,0:T(8,128)(2,1)S(1)}, u32[]{:S(2)}, u32[]{:S(2)}) %collective-permute-start.26) | collective-permute-done | bytes 524320 | tf_op jit(solution)/shard_map/ppermute | solution.py:240
  (115 shorter events, 34.2 us)
Async XLA Ops:
  2.1 31.7 %collective-permute-start.1 = (bf16[512,512]{1,0:T(8,128)(2,1)S(1)}, bf16[512,512]{1,0:T(8,128)(2,1)S(1)}, u32[]{:S(2)}, u32[]{:S(2)}) collective-permute-start(bf16[512,512]{1,0:T(8,128)(2,1)S(1)} %get-tuple-element.57), channel_id=1, source_target_pairs={{4,0},{5,1},{6,2},{7,3},{0,4},{1,5},{2,6},{3,7},{12,8},{13,9},{14,... | collective-permute-start | bytes 1572872 | tf_op jit(solution)/shard_map/ppermute | solution.py:240
  6.1 27.7 %collective-permute-start.2 = (bf16[512,512]{1,0:T(8,128)(2,1)S(1)}, bf16[512,512]{1,0:T(8,128)(2,1)}, u32[]{:S(2)}, u32[]{:S(2)}) collective-permute-start(bf16[512,512]{1,0:T(8,128)(2,1)S(1)} %get-tuple-element.57), channel_id=1, source_target_pairs={{2,0},{3,1},{4,2},{5,3},{6,4},{7,5},{10,8},{11,9},{12,10},{13,11},... | collective-permute-start | bytes 1572872 | tf_op jit(solution)/shard_map/ppermute | solution.py:240
  7.4 26.4 %collective-permute-start.3 = (bf16[512,512]{1,0:T(8,128)(2,1)S(1)}, bf16[512,512]{1,0:T(8,128)(2,1)}, u32[]{:S(2)}, u32[]{:S(2)}) collective-permute-start(bf16[512,512]{1,0:T(8,128)(2,1)S(1)} %get-tuple-element.57), channel_id=1, source_target_pairs={{0,2},{1,3},{2,4},{3,5},{4,6},{5,7},{8,10},{9,11},{10,12},{11,13},... | collective-permute-start | bytes 1572872 | tf_op jit(solution)/shard_map/ppermute | solution.py:240
  12.8 21.0 %collective-permute-start = (bf16[512,512]{1,0:T(8,128)(2,1)}, bf16[512,512]{1,0:T(8,128)(2,1)}, u32[]{:S(2)}, u32[]{:S(2)}) collective-permute-start(bf16[512,512]{1,0:T(8,128)(2,1)} %get-tuple-element.82), channel_id=1, source_target_pairs={{0,1},{1,0},{2,3},{3,2},{4,5},{5,4},{6,7},{7,6},{8,9},{9,8},{10,11... | collective-permute-start | bytes 1572872 | tf_op jit(solution)/shard_map/ppermute | solution.py:234
  16.2 16.2 %copy-start = (bf16[1024,512]{1,0:T(8,128)(2,1)S(1)}, bf16[1024,512]{1,0:T(8,128)(2,1)}, u32[]{:S(2)}) copy-start(bf16[1024,512]{1,0:T(8,128)(2,1)} %refs_11_.1) | copy-start | bytes 3145732
  16.2 16.2 %copy-start.1 = (bf16[1024,512]{1,0:T(8,128)(2,1)S(1)}, bf16[1024,512]{1,0:T(8,128)(2,1)}, u32[]{:S(2)}) copy-start(bf16[1024,512]{1,0:T(8,128)(2,1)} %refs_9_.1) | copy-start | bytes 3145732
  33.8 21.7 %collective-permute-start.8 = (bf16[512,512]{1,0:T(8,128)(2,1)S(1)}, bf16[512,512]{1,0:T(8,128)(2,1)}, u32[]{:S(2)}, u32[]{:S(2)}) collective-permute-start(bf16[512,512]{1,0:T(8,128)(2,1)S(1)} %collective-permute-done.1), channel_id=1, source_target_pairs={{4,6},{5,7},{2,0},{3,1},{12,14},{13,15},{10,8},{11,9},{20,22},{21,... | collective-permute-start | bytes 1572872 | tf_op jit(solution)/shard_map/ppermute | solution.py:240
  36.4 63.3 %collective-permute-start.9 = (bf16[6144,128]{1,0:T(8,128)(2,1)}, bf16[6144,128]{1,0:T(8,128)(2,1)}, u32[]{:S(2)}, u32[]{:S(2)}) collective-permute-start(bf16[6144,128]{1,0:T(8,128)(2,1)} %pad_maximum_fusion.3), channel_id=1, source_target_pairs={{0,1},{1,0},{2,3},{3,2},{4,5},{5,4},{6,7},{7,6},{8,9},{9,8},{10,11... | collective-permute-start | bytes 4718600 | tf_op jit(solution)/shard_map/ppermute | solution.py:234
  36.9 57.4 %collective-permute-start.4 = (bf16[512,1024]{1,0:T(8,128)(2,1)}, bf16[512,1024]{1,0:T(8,128)(2,1)}, u32[]{:S(2)}, u32[]{:S(2)}) collective-permute-start(bf16[512,1024]{1,0:T(8,128)(2,1)} %encode.1), channel_id=1, source_target_pairs={{4,0},{5,1},{6,2},{7,3},{0,4},{1,5},{2,6},{3,7},{12,8},{13,9},{14,... | collective-permute-start | bytes 3145736 | tf_op jit(solution)/shard_map/ppermute | solution.py:240
  48.2 51.5 %collective-permute-start.5 = (bf16[512,1024]{1,0:T(8,128)(2,1)}, bf16[512,1024]{1,0:T(8,128)(2,1)}, u32[]{:S(2)}, u32[]{:S(2)}) collective-permute-start(bf16[512,1024]{1,0:T(8,128)(2,1)} %encode.1), channel_id=1, source_target_pairs={{2,0},{3,1},{4,2},{5,3},{6,4},{7,5},{10,8},{11,9},{12,10},{13,11},... | collective-permute-start | bytes 3145736 | tf_op jit(solution)/shard_map/ppermute | solution.py:240
  49.5 50.2 %collective-permute-start.6 = (bf16[512,1024]{1,0:T(8,128)(2,1)}, bf16[512,1024]{1,0:T(8,128)(2,1)}, u32[]{:S(2)}, u32[]{:S(2)}) collective-permute-start(bf16[512,1024]{1,0:T(8,128)(2,1)} %encode.1), channel_id=1, source_target_pairs={{0,2},{1,3},{2,4},{3,5},{4,6},{5,7},{8,10},{9,11},{10,12},{11,13},... | collective-permute-start | bytes 3145736 | tf_op jit(solution)/shard_map/ppermute | solution.py:240
  55.5 44.2 %collective-permute-start.7 = (bf16[512,1024]{1,0:T(8,128)(2,1)}, bf16[512,1024]{1,0:T(8,128)(2,1)}, u32[]{:S(2)}, u32[]{:S(2)}) collective-permute-start(bf16[512,1024]{1,0:T(8,128)(2,1)} %encode.1), channel_id=1, source_target_pairs={{0,1},{1,0},{2,3},{3,2},{4,5},{5,4},{6,7},{7,6},{8,9},{9,8},{10,11... | collective-permute-start | bytes 3145736 | tf_op jit(solution)/shard_map/ppermute | solution.py:234
  60.3 61.0 %copy-start.4 = (bf16[4096,512]{1,0:T(8,128)(2,1)S(1)}, bf16[4096,512]{1,0:T(8,128)(2,1)}, u32[]{:S(2)}) copy-start(bf16[4096,512]{1,0:T(8,128)(2,1)} %param.10) | copy-start | bytes 12582916
  99.7 44.6 %collective-permute-start.18 = (bf16[6144,128]{1,0:T(8,128)(2,1)}, bf16[6144,128]{1,0:T(8,128)(2,1)S(1)}, u32[]{:S(2)}, u32[]{:S(2)}) collective-permute-start(bf16[6144,128]{1,0:T(8,128)(2,1)} %collective-permute-done.9), channel_id=1, source_target_pairs={{0,16},{8,24},{16,0},{24,8},{1,17},{9,25},{17,1},{25,9},{2,18},{10... | collective-permute-start | bytes 4718600 | tf_op jit(solution)/shard_map/ppermute | solution.py:237
  101.4 66.4 %collective-permute-start.10 = (bf16[512,1024]{1,0:T(8,128)(2,1)}, bf16[512,1024]{1,0:T(8,128)(2,1)S(1)}, u32[]{:S(2)}, u32[]{:S(2)}) collective-permute-start(bf16[512,1024]{1,0:T(8,128)(2,1)} %collective-permute-done.4), channel_id=1, source_target_pairs={{4,6},{5,7},{2,0},{3,1},{12,14},{13,15},{10,8},{11,9},{20,22},{21,... | collective-permute-start | bytes 3145736 | tf_op jit(solution)/shard_map/ppermute | solution.py:240
  102.7 67.6 %collective-permute-start.11 = (bf16[512,1024]{1,0:T(8,128)(2,1)}, bf16[512,1024]{1,0:T(8,128)(2,1)S(1)}, u32[]{:S(2)}, u32[]{:S(2)}) collective-permute-start(bf16[512,1024]{1,0:T(8,128)(2,1)} %collective-permute-done.4), channel_id=1, source_target_pairs={{0,1},{1,0},{2,3},{3,2},{4,5},{5,4},{6,7},{7,6},{8,9},{9,8},{10,11... | collective-permute-start | bytes 3145736 | tf_op jit(solution)/shard_map/ppermute | solution.py:234
  104.3 38.6 %collective-permute-start.14 = (bf16[512,512]{1,0:T(8,128)(2,1)}, bf16[512,512]{1,0:T(8,128)(2,1)}, u32[]{:S(2)}, u32[]{:S(2)}) collective-permute-start(bf16[512,512]{1,0:T(8,128)(2,1)} %collective-permute-done), channel_id=1, source_target_pairs={{4,0},{5,1},{6,2},{7,3},{0,4},{1,5},{2,6},{3,7},{12,8},{13,9},{14,... | collective-permute-start | bytes 1572872 | tf_op jit(solution)/shard_map/ppermute | solution.py:240
  119.8 46.5 %collective-permute-start.17 = (bf16[128,4096]{1,0:T(8,128)(2,1)S(1)}, bf16[128,4096]{1,0:T(8,128)(2,1)S(1)}, u32[]{:S(2)}, u32[]{:S(2)}) collective-permute-start(bf16[128,4096]{1,0:T(8,128)(2,1)S(1)} %constant_dynamic-slice_fusion), channel_id=1, source_target_pairs={{0,1},{1,0},{2,3},{3,2},{4,5},{5,4},{6,7},{7,6},{8,9},{9,8},{10,11... | collective-permute-start | bytes 3145736 | tf_op jit(solution)/shard_map/ppermute | solution.py:234
  143.0 22.2 %collective-permute-start.15 = (bf16[512,512]{1,0:T(8,128)(2,1)}, bf16[512,512]{1,0:T(8,128)(2,1)S(1)}, u32[]{:S(2)}, u32[]{:S(2)}) collective-permute-start(bf16[512,512]{1,0:T(8,128)(2,1)} %collective-permute-done), channel_id=1, source_target_pairs={{2,0},{3,1},{4,2},{5,3},{6,4},{7,5},{10,8},{11,9},{12,10},{13,11},... | collective-permute-start | bytes 1572872 | tf_op jit(solution)/shard_map/ppermute | solution.py:240
  144.3 22.0 %collective-permute-start.16 = (bf16[512,512]{1,0:T(8,128)(2,1)}, bf16[512,512]{1,0:T(8,128)(2,1)S(1)}, u32[]{:S(2)}, u32[]{:S(2)}) collective-permute-start(bf16[512,512]{1,0:T(8,128)(2,1)} %collective-permute-done), channel_id=1, source_target_pairs={{0,2},{1,3},{2,4},{3,5},{4,6},{5,7},{8,10},{9,11},{10,12},{11,13},... | collective-permute-start | bytes 1572872 | tf_op jit(solution)/shard_map/ppermute | solution.py:240
  165.2 2.6 copy-start.13
  166.3 1.5 copy-start.15
  166.3 24.0 %copy-start.9 = (bf16[128,4096]{1,0:T(8,128)(2,1)}, bf16[128,4096]{1,0:T(8,128)(2,1)S(1)}, u32[]{:S(2)}) copy-start(bf16[128,4096]{1,0:T(8,128)(2,1)S(1)} %collective-permute-done.17) | copy-start | bytes 3145732
  166.3 24.0 %collective-permute-start.21 = (bf16[128,4096]{1,0:T(8,128)(2,1)S(1)}, bf16[128,4096]{1,0:T(8,128)(2,1)S(1)}, u32[]{:S(2)}, u32[]{:S(2)}) collective-permute-start(bf16[128,4096]{1,0:T(8,128)(2,1)S(1)} %collective-permute-done.17), channel_id=1, source_target_pairs={{0,16},{8,24},{16,0},{24,8},{1,17},{9,25},{17,1},{25,9},{2,18},{10... | collective-permute-start | bytes 3145736 | tf_op jit(solution)/shard_map/ppermute | solution.py:237
  170.3 26.4 %collective-permute-start.12 = (bf16[512,1024]{1,0:T(8,128)(2,1)}, bf16[512,1024]{1,0:T(8,128)(2,1)}, u32[]{:S(2)}, u32[]{:S(2)}) collective-permute-start(bf16[512,1024]{1,0:T(8,128)(2,1)} %get-tuple-element.48), channel_id=1, source_target_pairs={{0,1},{1,0},{2,3},{3,2},{4,5},{5,4},{6,7},{7,6},{8,9},{9,8},{10,11... | collective-permute-start | bytes 3145736 | tf_op jit(solution)/shard_map/ppermute | solution.py:234
  171.3 45.2 %collective-permute-start.13 = (bf16[512,1024]{1,0:T(8,128)(2,1)S(1)}, bf16[512,1024]{1,0:T(8,128)(2,1)}, u32[]{:S(2)}, u32[]{:S(2)}) collective-permute-start(bf16[512,1024]{1,0:T(8,128)(2,1)S(1)} %get-tuple-element.49), channel_id=1, source_target_pairs={{0,1},{1,0},{2,3},{3,2},{4,5},{5,4},{6,7},{7,6},{8,9},{9,8},{10,11... | collective-permute-start | bytes 3145736 | tf_op jit(solution)/shard_map/ppermute | solution.py:234
  174.6 4.1 %copy-start.20 = (bf16[512,1024]{1,0:T(8,128)(2,1)S(1)}, bf16[512,1024]{1,0:T(8,128)(2,1)}, u32[]{:S(2)}) copy-start(bf16[512,1024]{1,0:T(8,128)(2,1)} %copy-done.19) | copy-start | bytes 3145732
  178.8 45.1 %collective-permute-start.20 = (bf16[6144,256]{1,0:T(8,128)(2,1)}, bf16[6144,256]{1,0:T(8,128)(2,1)S(1)}, u32[]{:S(2)}, u32[]{:S(2)}) collective-permute-start(bf16[6144,256]{1,0:T(8,128)(2,1)} %pad_maximum_fusion.1), channel_id=1, source_target_pairs={{0,8},{8,0},{16,24},{24,16},{1,9},{9,1},{17,25},{25,17},{2,10},{10... | collective-permute-start | bytes 9437192 | tf_op jit(solution)/shard_map/ppermute | solution.py:237
  178.9 40.4 %collective-permute-start.19 = (bf16[512,512]{1,0:T(8,128)(2,1)}, bf16[512,512]{1,0:T(8,128)(2,1)S(1)}, u32[]{:S(2)}, u32[]{:S(2)}) collective-permute-start(bf16[512,512]{1,0:T(8,128)(2,1)} %collective-permute-done.14), channel_id=1, source_target_pairs={{4,6},{5,7},{2,0},{3,1},{12,14},{13,15},{10,8},{11,9},{20,22},{21,... | collective-permute-start | bytes 1572872 | tf_op jit(solution)/shard_map/ppermute | solution.py:240
  191.3 31.8 %collective-permute-start.22 = (bf16[256,4096]{1,0:T(8,128)(2,1)S(1)}, bf16[256,4096]{1,0:T(8,128)(2,1)S(1)}, u32[]{:S(2)}, u32[]{:S(2)}) collective-permute-start(bf16[256,4096]{1,0:T(8,128)(2,1)S(1)} %pad_maximum_fusion.2), channel_id=1, source_target_pairs={{0,8},{8,0},{16,24},{24,16},{1,9},{9,1},{17,25},{25,17},{2,10},{10... | collective-permute-start | bytes 6291464 | tf_op jit(solution)/shard_map/ppermute | solution.py:237
  193.5 25.8 %copy-start.16 = (bf16[512,512]{1,0:T(8,128)(2,1)S(1)}, bf16[512,512]{1,0:T(8,128)(2,1)}, u32[]{:S(2)}) copy-start(bf16[512,512]{1,0:T(8,128)(2,1)} %copy-done.15) | copy-start | bytes 1572868
  193.5 26.3 %copy-start.14 = (bf16[512,512]{1,0:T(8,128)(2,1)S(1)}, bf16[512,512]{1,0:T(8,128)(2,1)}, u32[]{:S(2)}) copy-start(bf16[512,512]{1,0:T(8,128)(2,1)} %copy-done.13) | copy-start | bytes 1572868
  217.8 2.4 copy-start.5
  217.8 2.4 copy-start.6
  217.8 2.4 copy-start.7
  217.8 2.6 copy-start.8
  219.3 3.8 %copy-start.3 = (bf16[4096,1024]{1,0:T(8,128)(2,1)}, bf16[4096,1024]{1,0:T(8,128)(2,1)S(1)}, u32[]{:S(2)}) copy-start(bf16[4096,1024]{1,0:T(8,128)(2,1)S(1)} %constant_dynamic-update-slice_fusion) | copy-start | bytes 25165828
  220.4 2.6 copy-start.10
  220.4 3.1 copy-start.12
  224.8 3.9 %copy-start.17 = (bf16[512,512]{1,0:T(8,128)(2,1)S(1)}, bf16[512,512]{1,0:T(8,128)(2,1)}, u32[]{:S(2)}) copy-start(bf16[512,512]{1,0:T(8,128)(2,1)} %copy-done.15) | copy-start | bytes 1572868
  229.7 1.0 copy-start.18
  230.9 14.4 %copy-start.2 = (bf16[512,4096]{1,0:T(8,128)(2,1)S(1)}, bf16[512,4096]{1,0:T(8,128)(2,1)}, u32[]{:S(2)}) copy-start(bf16[512,4096]{1,0:T(8,128)(2,1)} %near.1) | copy-start | bytes 12582916
  252.1 27.8 %collective-permute-start.25 = (bf16[512,1024]{1,0:T(8,128)(2,1)S(1)}, bf16[512,1024]{1,0:T(8,128)(2,1)S(1)}, u32[]{:S(2)}, u32[]{:S(2)}) collective-permute-start(bf16[512,1024]{1,0:T(8,128)(2,1)S(1)} %broadcast_select_fusion), channel_id=1, source_target_pairs={{0,2},{1,3},{6,4},{7,5},{8,10},{9,11},{14,12},{15,13},{16,18},{17,... | collective-permute-start | bytes 3145736 | tf_op jit(solution)/shard_map/ppermute | solution.py:240
  256.4 34.9 %collective-permute-start.24 = (bf16[512,1024]{1,0:T(8,128)(2,1)S(1)}, bf16[512,1024]{1,0:T(8,128)(2,1)S(1)}, u32[]{:S(2)}, u32[]{:S(2)}) collective-permute-start(bf16[512,1024]{1,0:T(8,128)(2,1)S(1)} %get-tuple-element.71), channel_id=1, source_target_pairs={{2,0},{3,1},{4,2},{5,3},{6,4},{7,5},{10,8},{11,9},{12,10},{13,11},... | collective-permute-start | bytes 3145736 | tf_op jit(solution)/shard_map/ppermute | solution.py:240
  257.7 44.7 %collective-permute-start.23 = (bf16[512,1024]{1,0:T(8,128)(2,1)S(1)}, bf16[512,1024]{1,0:T(8,128)(2,1)S(1)}, u32[]{:S(2)}, u32[]{:S(2)}) collective-permute-start(bf16[512,1024]{1,0:T(8,128)(2,1)S(1)} %get-tuple-element.70), channel_id=1, source_target_pairs={{0,2},{1,3},{2,4},{3,5},{4,6},{5,7},{8,10},{9,11},{10,12},{11,13},... | collective-permute-start | bytes 3145736 | tf_op jit(solution)/shard_map/ppermute | solution.py:240
  280.4 33.3 %collective-permute-start.28 = (bf16[512,512]{1,0:T(8,128)(2,1)S(1)}, bf16[512,512]{1,0:T(8,128)(2,1)S(1)}, u32[]{:S(2)}, u32[]{:S(2)}) collective-permute-start(bf16[512,512]{1,0:T(8,128)(2,1)S(1)} %get-tuple-element.78), channel_id=1, source_target_pairs={{0,5},{1,4},{2,7},{3,6},{4,1},{5,0},{6,3},{7,2},{8,13},{9,12},{10,... | collective-permute-start | bytes 1572872 | tf_op jit(solution)/shard_map/ppermute | solution.py:273
  303.0 10.6 %collective-permute-start.27 = (bf16[512,512]{1,0:T(8,128)(2,1)S(1)}, bf16[512,512]{1,0:T(8,128)(2,1)S(1)}, u32[]{:S(2)}, u32[]{:S(2)}) collective-permute-start(bf16[512,512]{1,0:T(8,128)(2,1)S(1)} %select_convert_fusion), channel_id=1, source_target_pairs={{0,1},{1,0},{2,3},{3,2},{4,5},{5,4},{6,7},{7,6},{8,9},{9,8},{10,11... | collective-permute-start | bytes 1572872 | tf_op jit(solution)/shard_map/ppermute | solution.py:234
  303.8 27.8 %collective-permute-start.26 = (bf16[512,512]{1,0:T(8,128)(2,1)S(1)}, bf16[512,512]{1,0:T(8,128)(2,1)S(1)}, u32[]{:S(2)}, u32[]{:S(2)}) collective-permute-start(bf16[512,512]{1,0:T(8,128)(2,1)S(1)} %get-tuple-element.77), channel_id=1, source_target_pairs={{4,0},{5,1},{6,2},{7,3},{0,4},{1,5},{2,6},{3,7},{12,8},{13,9},{14,... | collective-permute-start | bytes 1572872 | tf_op jit(solution)/shard_map/ppermute | solution.py:240
  (2 other events, 2.0 us)

commit v5 on v4

--- a/solution.py
+++ b/solution.py
@@ -282,6 +282,20 @@
     def swap_pieces(pieces, bit, axis):
         return jnp.concatenate([pieces, swap_sa(pieces, bit)], axis=axis)
 
+    def in_order(pieces, axis):
+        if (local // s_total) % head_dim == 0:
+            return pieces
+        came, size = [0], pieces.shape[axis] // s_total
+        for bit in bits:
+            came += [k ^ bit for k in came]
+        return jnp.concatenate(
+            [
+                lax.slice_in_dim(pieces, came.index(k) * size, (came.index(k) + 1) * size, axis=axis)
+                for k in range(s_total)
+            ],
+            axis=axis,
+        )
+
     def own_piece(a, axis):
         size = a.shape[axis] // s_total
         return lax.dynamic_slice_in_dim(a, lax.axis_index("sa") * size, size, axis)
@@ -352,6 +366,7 @@
         packed = swap_pieces(packed, bit, 1)
     for bit in bits:
         piece = swap_pieces(piece, bit, 0)
+    packed, piece = in_order(packed, 1), in_order(piece, 0)
     late, everything = tie((late, everything))
     for d, a in zip([d for d in range(length) if d not in crossed], late):
         everything = put(everything, a, d, 1)

time: 334 us -> 334 us (level)
  no operation moved by 1% of the time
where the time goes in v5:
time: 334 us; the launch traced here: 333 us
  waiting for transfers between devices  153 us (46%)
  starting transfers between devices  88.1 us (26%)
  Pallas kernels  37.2 us (11%)
  local copies, waits for them, and re-layouts  18.5 us (6%)
  matrix products  16.9 us (5%)
  other arithmetic  16.2 us (5%)
    ppermute x16, waiting for transfers between devices, on_line(): lax.ppermute(a, 'an', [(i * 2 + y, j * 2 + y) for i, j in moves for y in...  114 us
    ppermute x16, starting transfers between devices, on_line(): lax.ppermute(a, 'an', [(i * 2 + y, j * 2 + y) for i, j in moves for y in...  73.7 us
    ppermute x8, waiting for transfers between devices, swap_pair(): return lax.ppermute(a, 'an', [(i, i ^ 1) for i in range(n)])  21.5 us
    dot_general x16, matrix products, shards(): total = total + jnp.dot(x, part, preferred_element_type=F32)  16.9 us
    pallas_call x1, Pallas kernels, encode(): pl.pallas_call(functools.partial(encode_kernel, count), grid_spec=pltpu.P...  16.2 us
    pallas_call x1, Pallas kernels, attend(): pl.pallas_call(functools.partial(attend_kernel, head_dim, count), grid_sp...  14.4 us
    ppermute x4, waiting for transfers between devices, swap_sa(): return lax.ppermute(a, 'sa', [(i, i ^ bit) for i in range(s_total)])  10 us
    dynamic_update_slice x8, local copies, waits for them, and re-layouts, put(): lax.dynamic_update_slice_in_dim(everything, a, (d * 2 + over) * rows_each...  9.15 us
  transfers between devices with their start and end apart: 29, of which 14 were waited for; matrix products, arithmetic and copies ran while one was open for 11% of the time, Pallas kernels for 5%

profile of v5, /device:TPU:0, one launch (start us, length us, event | category | flops | bytes accessed | tf_op | source)
XLA Modules:
  0.0 333.3 jit_solution(3783026248761143723)
XLA Ops:
  0.0 2.1 broadcast_select_fusion.11
  2.1 4.0 %collective-permute-start.1 = (bf16[512,512]{1,0:T(8,128)(2,1)S(1)}, bf16[512,512]{1,0:T(8,128)(2,1)S(1)}, u32[]{:S(2)}, u32[]{:S(2)}) collective-permute-start(bf16[512,512]{1,0:T(8,128)(2,1)S(1)} %get-tuple-element.57), channel_id=1, source_target_pairs={{4,0},{5,1},{6,2},{7,3},{0,4},{1,5},{2,6},{3,7},{12,8},{13,9},{14,... | collective-permute-start | bytes 1572872 | tf_op jit(solution)/shard_map/ppermute | solution.py:240
  7.4 5.4 %collective-permute-start.3 = (bf16[512,512]{1,0:T(8,128)(2,1)S(1)}, bf16[512,512]{1,0:T(8,128)(2,1)}, u32[]{:S(2)}, u32[]{:S(2)}) collective-permute-start(bf16[512,512]{1,0:T(8,128)(2,1)S(1)} %get-tuple-element.57), channel_id=1, source_target_pairs={{0,2},{1,3},{2,4},{3,5},{4,6},{5,7},{8,10},{9,11},{10,12},{11,13},... | collective-permute-start | bytes 1572872 | tf_op jit(solution)/shard_map/ppermute | solution.py:240
  12.8 1.5 collective-permute-start
  16.2 16.2 %encode.1 = bf16[512,1024]{1,0:T(8,128)(2,1)} custom-call(s32[4]{0:T(128)} %select_reduce_fusion.2.slots, bf16[8,128,1024]{2,1,0:T(8,128)(2,1)} %refs_3_.1, bf16[8,128,1024]{2,1,0:T(8,128)(2,1)} %refs_3_.1, bf16[8,128,1024]{2,1,0:T(8,128)(2,1)} %refs_3_.1, bf16[8,128,1024]{2,1,0:T(8,128)(2,1)} %refs_3_.1, bf16[1024,4096]{1,0:T(8,128)(2,1)} %refs_4_.1, ...), custom_call_target="tpu_custom_call" | custom-call | flops 8589934592 | bytes 18874368 | tf_op jit(solution)/shard_map/encode/pallas_call | solution.py:55
  36.8 11.3 %collective-permute-start.4 = (bf16[512,1024]{1,0:T(8,128)(2,1)}, bf16[512,1024]{1,0:T(8,128)(2,1)}, u32[]{:S(2)}, u32[]{:S(2)}) collective-permute-start(bf16[512,1024]{1,0:T(8,128)(2,1)} %encode.1), channel_id=1, source_target_pairs={{4,0},{5,1},{6,2},{7,3},{0,4},{1,5},{2,6},{3,7},{12,8},{13,9},{14,... | collective-permute-start | bytes 3145736 | tf_op jit(solution)/shard_map/ppermute | solution.py:240
  49.5 5.6 %collective-permute-start.6 = (bf16[512,1024]{1,0:T(8,128)(2,1)}, bf16[512,1024]{1,0:T(8,128)(2,1)}, u32[]{:S(2)}, u32[]{:S(2)}) collective-permute-start(bf16[512,1024]{1,0:T(8,128)(2,1)} %encode.1), channel_id=1, source_target_pairs={{0,2},{1,3},{2,4},{3,5},{4,6},{5,7},{8,10},{9,11},{10,12},{11,13},... | collective-permute-start | bytes 3145736 | tf_op jit(solution)/shard_map/ppermute | solution.py:240
  55.5 1.5 collective-permute-start.7
  60.3 1.4 constant_dynamic-slice_fusion
  61.8 1.4 broadcast_select_fusion.4
  63.2 31.1 %collective-permute-done.4 = bf16[512,1024]{1,0:T(8,128)(2,1)} collective-permute-done((bf16[512,1024]{1,0:T(8,128)(2,1)}, bf16[512,1024]{1,0:T(8,128)(2,1)}, u32[]{:S(2)}, u32[]{:S(2)}) %collective-permute-start.4) | collective-permute-done | bytes 1048608 | tf_op jit(solution)/shard_map/ppermute | solution.py:240
  94.2 5.4 %collective-permute-done.5 = bf16[512,1024]{1,0:T(8,128)(2,1)} collective-permute-done((bf16[512,1024]{1,0:T(8,128)(2,1)}, bf16[512,1024]{1,0:T(8,128)(2,1)}, u32[]{:S(2)}, u32[]{:S(2)}) %collective-permute-start.5) | collective-permute-done | bytes 1048608 | tf_op jit(solution)/shard_map/ppermute | solution.py:240
  99.7 1.6 collective-permute-start.18
  102.7 1.6 collective-permute-start.11
  104.3 15.5 %collective-permute-start.14 = (bf16[512,512]{1,0:T(8,128)(2,1)}, bf16[512,512]{1,0:T(8,128)(2,1)}, u32[]{:S(2)}, u32[]{:S(2)}) collective-permute-start(bf16[512,512]{1,0:T(8,128)(2,1)} %collective-permute-done), channel_id=1, source_target_pairs={{4,0},{5,1},{6,2},{7,3},{0,4},{1,5},{2,6},{3,7},{12,8},{13,9},{14,... | collective-permute-start | bytes 1572872 | tf_op jit(solution)/shard_map/ppermute | solution.py:240
  119.8 1.5 collective-permute-start.17
  121.3 2.5 fusion.41
  123.8 1.4 fusion.31
  125.2 1.4 fusion.35
  126.6 1.4 fusion.39
  128.0 14.9 %collective-permute-done.14 = bf16[512,512]{1,0:T(8,128)(2,1)} collective-permute-done((bf16[512,512]{1,0:T(8,128)(2,1)}, bf16[512,512]{1,0:T(8,128)(2,1)}, u32[]{:S(2)}, u32[]{:S(2)}) %collective-permute-start.14) | collective-permute-done | bytes 524320 | tf_op jit(solution)/shard_map/ppermute | solution.py:240
  144.3 11.3 %collective-permute-start.16 = (bf16[512,512]{1,0:T(8,128)(2,1)}, bf16[512,512]{1,0:T(8,128)(2,1)S(1)}, u32[]{:S(2)}, u32[]{:S(2)}) collective-permute-start(bf16[512,512]{1,0:T(8,128)(2,1)} %collective-permute-done), channel_id=1, source_target_pairs={{0,2},{1,3},{2,4},{3,5},{4,6},{5,7},{8,10},{9,11},{10,12},{11,13},... | collective-permute-start | bytes 1572872 | tf_op jit(solution)/shard_map/ppermute | solution.py:240
  155.6 3.5 %pad_maximum_fusion.1 = bf16[6144,256]{1,0:T(8,128)(2,1)} fusion(bf16[6144,128]{1,0:T(8,128)(2,1)S(1)} %collective-permute-done.18, bf16[6144,128]{1,0:T(8,128)(2,1)} %collective-permute-done.9), kind=kLoop, calls=%fused_computation.1 | loop fusion | flops 6291456 | bytes 6291456 | tf_op jit(solution)/shard_map/concatenate | solution.py:283
  159.1 6.1 %collective-permute-done.15 = bf16[512,512]{1,0:T(8,128)(2,1)S(1)} collective-permute-done((bf16[512,512]{1,0:T(8,128)(2,1)}, bf16[512,512]{1,0:T(8,128)(2,1)S(1)}, u32[]{:S(2)}, u32[]{:S(2)}) %collective-permute-start.15) | collective-permute-done | bytes 524320 | tf_op jit(solution)/shard_map/ppermute | solution.py:240
  166.3 1.5 collective-permute-start.21
  167.8 2.5 broadcast_select_fusion.1
  172.3 2.3 dynamic_update_slice.24
  178.9 1.5 collective-permute-start.19
  180.3 10.0 %collective-permute-done.21 = bf16[128,4096]{1,0:T(8,128)(2,1)S(1)} collective-permute-done((bf16[128,4096]{1,0:T(8,128)(2,1)S(1)}, bf16[128,4096]{1,0:T(8,128)(2,1)S(1)}, u32[]{:S(2)}, u32[]{:S(2)}) %collective-permute-start.21) | collective-permute-done | bytes 1048608 | tf_op jit(solution)/shard_map/ppermute | solution.py:237
  191.3 2.1 constant_dynamic-update-slice_fusion.8
  193.5 1.6 fusion.33
  195.1 1.7 collective-permute-done.12
  196.7 19.8 %collective-permute-done.13 = bf16[512,1024]{1,0:T(8,128)(2,1)} collective-permute-done((bf16[512,1024]{1,0:T(8,128)(2,1)S(1)}, bf16[512,1024]{1,0:T(8,128)(2,1)}, u32[]{:S(2)}, u32[]{:S(2)}) %collective-permute-start.13) | collective-permute-done | bytes 1048608 | tf_op jit(solution)/shard_map/ppermute | solution.py:234
  217.8 1.4 constant_dynamic-update-slice_fusion
  220.4 1.6 fusion.13
  224.9 1.5 fusion.18
  227.3 1.5 fusion.26
  230.9 14.4 %attend.1.a = bf16[512,1024]{1,0:T(8,128)(2,1)S(1)} custom-call(s32[16]{0:T(128)S(1)} %broadcast_select_fusion.17.where, bf16[32,128,1024]{2,1,0:T(8,128)(2,1)} %bitcast.17, bf16[32,128,1024]{2,1,0:T(8,128)(2,1)} %bitcast.18, bf16[32,128,1024]{2,1,0:T(8,128)(2,1)} %bitcast.19, bf16[32,128,1024]{2,1,0:T(8,128)(2,1)} %bitcast.20, ...), custom_call_target="tpu_custom_call" | custom-call | flops 9126805504 | bytes 10485760 | tf_op jit(solution)/shard_map/attend/pallas_call | solution.py:138
  245.3 6.7 %terms.1 = (f32[512,1024]{1,0:T(8,128)S(1)}, bf16[512,1024]{1,0:T(8,128)(2,1)S(1)}, bf16[512,1024]{1,0:T(8,128)(2,1)S(1)}, bf16[512,1024]{1,0:T(8,128)(2,1)S(1)}) custom-call(s32[4]{0:T(128)S(1)} %and_select_fusion.6.order, bf16[512,1024]{1,0:T(8,128)(2,1)S(1)} %attend.1.a, bf16[512,4096]{1,0:T(8,128)(2,1)S(1)} %copy-done.2, ...), custom_call_target="tpu_custom_call" | custom-call | flops 4294967296 | bytes 13631488 | tf_op jit(solution)/shard_map/terms/pallas_call | solution.py:192
  252.1 4.3 %collective-permute-start.25 = (bf16[512,1024]{1,0:T(8,128)(2,1)S(1)}, bf16[512,1024]{1,0:T(8,128)(2,1)S(1)}, u32[]{:S(2)}, u32[]{:S(2)}) collective-permute-start(bf16[512,1024]{1,0:T(8,128)(2,1)S(1)} %broadcast_select_fusion), channel_id=1, source_target_pairs={{0,2},{1,3},{6,4},{7,5},{8,10},{9,11},{14,12},{15,13},{16,18},{17,... | collective-permute-start | bytes 3145736 | tf_op jit(solution)/shard_map/ppermute | solution.py:240
  257.7 4.6 %collective-permute-start.23 = (bf16[512,1024]{1,0:T(8,128)(2,1)S(1)}, bf16[512,1024]{1,0:T(8,128)(2,1)S(1)}, u32[]{:S(2)}, u32[]{:S(2)}) collective-permute-start(bf16[512,1024]{1,0:T(8,128)(2,1)S(1)} %get-tuple-element.70), channel_id=1, source_target_pairs={{0,2},{1,3},{2,4},{3,5},{4,6},{5,7},{8,10},{9,11},{10,12},{11,13},... | collective-permute-start | bytes 3145736 | tf_op jit(solution)/shard_map/ppermute | solution.py:240
  262.3 17.6 %collective-permute-done.25 = bf16[512,1024]{1,0:T(8,128)(2,1)S(1)} collective-permute-done((bf16[512,1024]{1,0:T(8,128)(2,1)S(1)}, bf16[512,1024]{1,0:T(8,128)(2,1)S(1)}, u32[]{:S(2)}, u32[]{:S(2)}) %collective-permute-start.25) | collective-permute-done | bytes 1048608 | tf_op jit(solution)/shard_map/ppermute | solution.py:240
  280.4 2.5 collective-permute-start.28
  282.9 8.4 %collective-permute-done.24 = bf16[512,1024]{1,0:T(8,128)(2,1)S(1)} collective-permute-done((bf16[512,1024]{1,0:T(8,128)(2,1)S(1)}, bf16[512,1024]{1,0:T(8,128)(2,1)S(1)}, u32[]{:S(2)}, u32[]{:S(2)}) %collective-permute-start.24) | collective-permute-done | bytes 1048608 | tf_op jit(solution)/shard_map/ppermute | solution.py:240
  291.3 11.1 %collective-permute-done.23 = bf16[512,1024]{1,0:T(8,128)(2,1)S(1)} collective-permute-done((bf16[512,1024]{1,0:T(8,128)(2,1)S(1)}, bf16[512,1024]{1,0:T(8,128)(2,1)S(1)}, u32[]{:S(2)}, u32[]{:S(2)}) %collective-permute-start.23) | collective-permute-done | bytes 1048608 | tf_op jit(solution)/shard_map/ppermute | solution.py:240
  303.6 2.5 collective-permute-start.26
  306.1 7.6 %collective-permute-done.28 = bf16[512,512]{1,0:T(8,128)(2,1)S(1)} collective-permute-done((bf16[512,512]{1,0:T(8,128)(2,1)S(1)}, bf16[512,512]{1,0:T(8,128)(2,1)S(1)}, u32[]{:S(2)}, u32[]{:S(2)}) %collective-permute-start.28) | collective-permute-done | bytes 524320 | tf_op jit(solution)/shard_map/ppermute | solution.py:273
  313.6 18.0 %collective-permute-done.26 = bf16[512,512]{1,0:T(8,128)(2,1)S(1)} collective-permute-done((bf16[512,512]{1,0:T(8,128)(2,1)S(1)}, bf16[512,512]{1,0:T(8,128)(2,1)S(1)}, u32[]{:S(2)}, u32[]{:S(2)}) %collective-permute-start.26) | collective-permute-done | bytes 524320 | tf_op jit(solution)/shard_map/ppermute | solution.py:240
  (115 shorter events, 34.0 us)
Async XLA Ops:
  2.1 31.7 %collective-permute-start.1 = (bf16[512,512]{1,0:T(8,128)(2,1)S(1)}, bf16[512,512]{1,0:T(8,128)(2,1)S(1)}, u32[]{:S(2)}, u32[]{:S(2)}) collective-permute-start(bf16[512,512]{1,0:T(8,128)(2,1)S(1)} %get-tuple-element.57), channel_id=1, source_target_pairs={{4,0},{5,1},{6,2},{7,3},{0,4},{1,5},{2,6},{3,7},{12,8},{13,9},{14,... | collective-permute-start | bytes 1572872 | tf_op jit(solution)/shard_map/ppermute | solution.py:240
  6.1 27.7 %collective-permute-start.2 = (bf16[512,512]{1,0:T(8,128)(2,1)S(1)}, bf16[512,512]{1,0:T(8,128)(2,1)}, u32[]{:S(2)}, u32[]{:S(2)}) collective-permute-start(bf16[512,512]{1,0:T(8,128)(2,1)S(1)} %get-tuple-element.57), channel_id=1, source_target_pairs={{2,0},{3,1},{4,2},{5,3},{6,4},{7,5},{10,8},{11,9},{12,10},{13,11},... | collective-permute-start | bytes 1572872 | tf_op jit(solution)/shard_map/ppermute | solution.py:240
  7.4 26.4 %collective-permute-start.3 = (bf16[512,512]{1,0:T(8,128)(2,1)S(1)}, bf16[512,512]{1,0:T(8,128)(2,1)}, u32[]{:S(2)}, u32[]{:S(2)}) collective-permute-start(bf16[512,512]{1,0:T(8,128)(2,1)S(1)} %get-tuple-element.57), channel_id=1, source_target_pairs={{0,2},{1,3},{2,4},{3,5},{4,6},{5,7},{8,10},{9,11},{10,12},{11,13},... | collective-permute-start | bytes 1572872 | tf_op jit(solution)/shard_map/ppermute | solution.py:240
  12.8 21.0 %collective-permute-start = (bf16[512,512]{1,0:T(8,128)(2,1)}, bf16[512,512]{1,0:T(8,128)(2,1)}, u32[]{:S(2)}, u32[]{:S(2)}) collective-permute-start(bf16[512,512]{1,0:T(8,128)(2,1)} %get-tuple-element.82), channel_id=1, source_target_pairs={{0,1},{1,0},{2,3},{3,2},{4,5},{5,4},{6,7},{7,6},{8,9},{9,8},{10,11... | collective-permute-start | bytes 1572872 | tf_op jit(solution)/shard_map/ppermute | solution.py:234
  16.2 16.2 %copy-start = (bf16[1024,512]{1,0:T(8,128)(2,1)S(1)}, bf16[1024,512]{1,0:T(8,128)(2,1)}, u32[]{:S(2)}) copy-start(bf16[1024,512]{1,0:T(8,128)(2,1)} %refs_11_.1) | copy-start | bytes 3145732
  16.2 16.2 %copy-start.1 = (bf16[1024,512]{1,0:T(8,128)(2,1)S(1)}, bf16[1024,512]{1,0:T(8,128)(2,1)}, u32[]{:S(2)}) copy-start(bf16[1024,512]{1,0:T(8,128)(2,1)} %refs_9_.1) | copy-start | bytes 3145732
  33.8 21.7 %collective-permute-start.8 = (bf16[512,512]{1,0:T(8,128)(2,1)S(1)}, bf16[512,512]{1,0:T(8,128)(2,1)}, u32[]{:S(2)}, u32[]{:S(2)}) collective-permute-start(bf16[512,512]{1,0:T(8,128)(2,1)S(1)} %collective-permute-done.1), channel_id=1, source_target_pairs={{4,6},{5,7},{2,0},{3,1},{12,14},{13,15},{10,8},{11,9},{20,22},{21,... | collective-permute-start | bytes 1572872 | tf_op jit(solution)/shard_map/ppermute | solution.py:240
  36.4 63.3 %collective-permute-start.9 = (bf16[6144,128]{1,0:T(8,128)(2,1)}, bf16[6144,128]{1,0:T(8,128)(2,1)}, u32[]{:S(2)}, u32[]{:S(2)}) collective-permute-start(bf16[6144,128]{1,0:T(8,128)(2,1)} %pad_maximum_fusion.3), channel_id=1, source_target_pairs={{0,1},{1,0},{2,3},{3,2},{4,5},{5,4},{6,7},{7,6},{8,9},{9,8},{10,11... | collective-permute-start | bytes 4718600 | tf_op jit(solution)/shard_map/ppermute | solution.py:234
  36.8 57.4 %collective-permute-start.4 = (bf16[512,1024]{1,0:T(8,128)(2,1)}, bf16[512,1024]{1,0:T(8,128)(2,1)}, u32[]{:S(2)}, u32[]{:S(2)}) collective-permute-start(bf16[512,1024]{1,0:T(8,128)(2,1)} %encode.1), channel_id=1, source_target_pairs={{4,0},{5,1},{6,2},{7,3},{0,4},{1,5},{2,6},{3,7},{12,8},{13,9},{14,... | collective-permute-start | bytes 3145736 | tf_op jit(solution)/shard_map/ppermute | solution.py:240
  48.2 51.5 %collective-permute-start.5 = (bf16[512,1024]{1,0:T(8,128)(2,1)}, bf16[512,1024]{1,0:T(8,128)(2,1)}, u32[]{:S(2)}, u32[]{:S(2)}) collective-permute-start(bf16[512,1024]{1,0:T(8,128)(2,1)} %encode.1), channel_id=1, source_target_pairs={{2,0},{3,1},{4,2},{5,3},{6,4},{7,5},{10,8},{11,9},{12,10},{13,11},... | collective-permute-start | bytes 3145736 | tf_op jit(solution)/shard_map/ppermute | solution.py:240
  49.5 50.2 %collective-permute-start.6 = (bf16[512,1024]{1,0:T(8,128)(2,1)}, bf16[512,1024]{1,0:T(8,128)(2,1)}, u32[]{:S(2)}, u32[]{:S(2)}) collective-permute-start(bf16[512,1024]{1,0:T(8,128)(2,1)} %encode.1), channel_id=1, source_target_pairs={{0,2},{1,3},{2,4},{3,5},{4,6},{5,7},{8,10},{9,11},{10,12},{11,13},... | collective-permute-start | bytes 3145736 | tf_op jit(solution)/shard_map/ppermute | solution.py:240
  55.5 44.2 %collective-permute-start.7 = (bf16[512,1024]{1,0:T(8,128)(2,1)}, bf16[512,1024]{1,0:T(8,128)(2,1)}, u32[]{:S(2)}, u32[]{:S(2)}) collective-permute-start(bf16[512,1024]{1,0:T(8,128)(2,1)} %encode.1), channel_id=1, source_target_pairs={{0,1},{1,0},{2,3},{3,2},{4,5},{5,4},{6,7},{7,6},{8,9},{9,8},{10,11... | collective-permute-start | bytes 3145736 | tf_op jit(solution)/shard_map/ppermute | solution.py:234
  60.3 61.0 %copy-start.4 = (bf16[4096,512]{1,0:T(8,128)(2,1)S(1)}, bf16[4096,512]{1,0:T(8,128)(2,1)}, u32[]{:S(2)}) copy-start(bf16[4096,512]{1,0:T(8,128)(2,1)} %param.10) | copy-start | bytes 12582916
  99.7 44.6 %collective-permute-start.18 = (bf16[6144,128]{1,0:T(8,128)(2,1)}, bf16[6144,128]{1,0:T(8,128)(2,1)S(1)}, u32[]{:S(2)}, u32[]{:S(2)}) collective-permute-start(bf16[6144,128]{1,0:T(8,128)(2,1)} %collective-permute-done.9), channel_id=1, source_target_pairs={{0,16},{8,24},{16,0},{24,8},{1,17},{9,25},{17,1},{25,9},{2,18},{10... | collective-permute-start | bytes 4718600 | tf_op jit(solution)/shard_map/ppermute | solution.py:237
  101.4 66.4 %collective-permute-start.10 = (bf16[512,1024]{1,0:T(8,128)(2,1)}, bf16[512,1024]{1,0:T(8,128)(2,1)S(1)}, u32[]{:S(2)}, u32[]{:S(2)}) collective-permute-start(bf16[512,1024]{1,0:T(8,128)(2,1)} %collective-permute-done.4), channel_id=1, source_target_pairs={{4,6},{5,7},{2,0},{3,1},{12,14},{13,15},{10,8},{11,9},{20,22},{21,... | collective-permute-start | bytes 3145736 | tf_op jit(solution)/shard_map/ppermute | solution.py:240
  102.7 67.6 %collective-permute-start.11 = (bf16[512,1024]{1,0:T(8,128)(2,1)}, bf16[512,1024]{1,0:T(8,128)(2,1)S(1)}, u32[]{:S(2)}, u32[]{:S(2)}) collective-permute-start(bf16[512,1024]{1,0:T(8,128)(2,1)} %collective-permute-done.4), channel_id=1, source_target_pairs={{0,1},{1,0},{2,3},{3,2},{4,5},{5,4},{6,7},{7,6},{8,9},{9,8},{10,11... | collective-permute-start | bytes 3145736 | tf_op jit(solution)/shard_map/ppermute | solution.py:234
  104.3 38.6 %collective-permute-start.14 = (bf16[512,512]{1,0:T(8,128)(2,1)}, bf16[512,512]{1,0:T(8,128)(2,1)}, u32[]{:S(2)}, u32[]{:S(2)}) collective-permute-start(bf16[512,512]{1,0:T(8,128)(2,1)} %collective-permute-done), channel_id=1, source_target_pairs={{4,0},{5,1},{6,2},{7,3},{0,4},{1,5},{2,6},{3,7},{12,8},{13,9},{14,... | collective-permute-start | bytes 1572872 | tf_op jit(solution)/shard_map/ppermute | solution.py:240
  119.8 46.5 %collective-permute-start.17 = (bf16[128,4096]{1,0:T(8,128)(2,1)S(1)}, bf16[128,4096]{1,0:T(8,128)(2,1)S(1)}, u32[]{:S(2)}, u32[]{:S(2)}) collective-permute-start(bf16[128,4096]{1,0:T(8,128)(2,1)S(1)} %constant_dynamic-slice_fusion), channel_id=1, source_target_pairs={{0,1},{1,0},{2,3},{3,2},{4,5},{5,4},{6,7},{7,6},{8,9},{9,8},{10,11... | collective-permute-start | bytes 3145736 | tf_op jit(solution)/shard_map/ppermute | solution.py:234
  143.0 22.2 %collective-permute-start.15 = (bf16[512,512]{1,0:T(8,128)(2,1)}, bf16[512,512]{1,0:T(8,128)(2,1)S(1)}, u32[]{:S(2)}, u32[]{:S(2)}) collective-permute-start(bf16[512,512]{1,0:T(8,128)(2,1)} %collective-permute-done), channel_id=1, source_target_pairs={{2,0},{3,1},{4,2},{5,3},{6,4},{7,5},{10,8},{11,9},{12,10},{13,11},... | collective-permute-start | bytes 1572872 | tf_op jit(solution)/shard_map/ppermute | solution.py:240
  144.3 22.0 %collective-permute-start.16 = (bf16[512,512]{1,0:T(8,128)(2,1)}, bf16[512,512]{1,0:T(8,128)(2,1)S(1)}, u32[]{:S(2)}, u32[]{:S(2)}) collective-permute-start(bf16[512,512]{1,0:T(8,128)(2,1)} %collective-permute-done), channel_id=1, source_target_pairs={{0,2},{1,3},{2,4},{3,5},{4,6},{5,7},{8,10},{9,11},{10,12},{11,13},... | collective-permute-start | bytes 1572872 | tf_op jit(solution)/shard_map/ppermute | solution.py:240
  165.2 2.6 copy-start.13
  166.3 1.5 copy-start.15
  166.3 24.0 %copy-start.9 = (bf16[128,4096]{1,0:T(8,128)(2,1)}, bf16[128,4096]{1,0:T(8,128)(2,1)S(1)}, u32[]{:S(2)}) copy-start(bf16[128,4096]{1,0:T(8,128)(2,1)S(1)} %collective-permute-done.17) | copy-start | bytes 3145732
  166.3 24.0 %collective-permute-start.21 = (bf16[128,4096]{1,0:T(8,128)(2,1)S(1)}, bf16[128,4096]{1,0:T(8,128)(2,1)S(1)}, u32[]{:S(2)}, u32[]{:S(2)}) collective-permute-start(bf16[128,4096]{1,0:T(8,128)(2,1)S(1)} %collective-permute-done.17), channel_id=1, source_target_pairs={{0,16},{8,24},{16,0},{24,8},{1,17},{9,25},{17,1},{25,9},{2,18},{10... | collective-permute-start | bytes 3145736 | tf_op jit(solution)/shard_map/ppermute | solution.py:237
  170.3 26.4 %collective-permute-start.12 = (bf16[512,1024]{1,0:T(8,128)(2,1)}, bf16[512,1024]{1,0:T(8,128)(2,1)}, u32[]{:S(2)}, u32[]{:S(2)}) collective-permute-start(bf16[512,1024]{1,0:T(8,128)(2,1)} %get-tuple-element.48), channel_id=1, source_target_pairs={{0,1},{1,0},{2,3},{3,2},{4,5},{5,4},{6,7},{7,6},{8,9},{9,8},{10,11... | collective-permute-start | bytes 3145736 | tf_op jit(solution)/shard_map/ppermute | solution.py:234
  171.3 45.2 %collective-permute-start.13 = (bf16[512,1024]{1,0:T(8,128)(2,1)S(1)}, bf16[512,1024]{1,0:T(8,128)(2,1)}, u32[]{:S(2)}, u32[]{:S(2)}) collective-permute-start(bf16[512,1024]{1,0:T(8,128)(2,1)S(1)} %get-tuple-element.49), channel_id=1, source_target_pairs={{0,1},{1,0},{2,3},{3,2},{4,5},{5,4},{6,7},{7,6},{8,9},{9,8},{10,11... | collective-permute-start | bytes 3145736 | tf_op jit(solution)/shard_map/ppermute | solution.py:234
  174.6 4.1 %copy-start.20 = (bf16[512,1024]{1,0:T(8,128)(2,1)S(1)}, bf16[512,1024]{1,0:T(8,128)(2,1)}, u32[]{:S(2)}) copy-start(bf16[512,1024]{1,0:T(8,128)(2,1)} %copy-done.19) | copy-start | bytes 3145732
  178.8 45.1 %collective-permute-start.20 = (bf16[6144,256]{1,0:T(8,128)(2,1)}, bf16[6144,256]{1,0:T(8,128)(2,1)S(1)}, u32[]{:S(2)}, u32[]{:S(2)}) collective-permute-start(bf16[6144,256]{1,0:T(8,128)(2,1)} %pad_maximum_fusion.1), channel_id=1, source_target_pairs={{0,8},{8,0},{16,24},{24,16},{1,9},{9,1},{17,25},{25,17},{2,10},{10... | collective-permute-start | bytes 9437192 | tf_op jit(solution)/shard_map/ppermute | solution.py:237
  178.9 40.4 %collective-permute-start.19 = (bf16[512,512]{1,0:T(8,128)(2,1)}, bf16[512,512]{1,0:T(8,128)(2,1)S(1)}, u32[]{:S(2)}, u32[]{:S(2)}) collective-permute-start(bf16[512,512]{1,0:T(8,128)(2,1)} %collective-permute-done.14), channel_id=1, source_target_pairs={{4,6},{5,7},{2,0},{3,1},{12,14},{13,15},{10,8},{11,9},{20,22},{21,... | collective-permute-start | bytes 1572872 | tf_op jit(solution)/shard_map/ppermute | solution.py:240
  191.3 31.8 %collective-permute-start.22 = (bf16[256,4096]{1,0:T(8,128)(2,1)S(1)}, bf16[256,4096]{1,0:T(8,128)(2,1)S(1)}, u32[]{:S(2)}, u32[]{:S(2)}) collective-permute-start(bf16[256,4096]{1,0:T(8,128)(2,1)S(1)} %pad_maximum_fusion.2), channel_id=1, source_target_pairs={{0,8},{8,0},{16,24},{24,16},{1,9},{9,1},{17,25},{25,17},{2,10},{10... | collective-permute-start | bytes 6291464 | tf_op jit(solution)/shard_map/ppermute | solution.py:237
  193.5 25.8 %copy-start.16 = (bf16[512,512]{1,0:T(8,128)(2,1)S(1)}, bf16[512,512]{1,0:T(8,128)(2,1)}, u32[]{:S(2)}) copy-start(bf16[512,512]{1,0:T(8,128)(2,1)} %copy-done.15) | copy-start | bytes 1572868
  193.5 26.3 %copy-start.14 = (bf16[512,512]{1,0:T(8,128)(2,1)S(1)}, bf16[512,512]{1,0:T(8,128)(2,1)}, u32[]{:S(2)}) copy-start(bf16[512,512]{1,0:T(8,128)(2,1)} %copy-done.13) | copy-start | bytes 1572868
  217.8 2.4 copy-start.5
  217.8 2.4 copy-start.6
  217.8 2.4 copy-start.7
  217.8 2.6 copy-start.8
  219.3 3.8 %copy-start.3 = (bf16[4096,1024]{1,0:T(8,128)(2,1)}, bf16[4096,1024]{1,0:T(8,128)(2,1)S(1)}, u32[]{:S(2)}) copy-start(bf16[4096,1024]{1,0:T(8,128)(2,1)S(1)} %constant_dynamic-update-slice_fusion) | copy-start | bytes 25165828
  220.4 2.6 copy-start.10
  220.4 3.1 copy-start.12
  224.8 3.9 %copy-start.17 = (bf16[512,512]{1,0:T(8,128)(2,1)S(1)}, bf16[512,512]{1,0:T(8,128)(2,1)}, u32[]{:S(2)}) copy-start(bf16[512,512]{1,0:T(8,128)(2,1)} %copy-done.15) | copy-start | bytes 1572868
  229.7 1.0 copy-start.18
  230.9 14.4 %copy-start.2 = (bf16[512,4096]{1,0:T(8,128)(2,1)S(1)}, bf16[512,4096]{1,0:T(8,128)(2,1)}, u32[]{:S(2)}) copy-start(bf16[512,4096]{1,0:T(8,128)(2,1)} %near.1) | copy-start | bytes 12582916
  252.1 27.8 %collective-permute-start.25 = (bf16[512,1024]{1,0:T(8,128)(2,1)S(1)}, bf16[512,1024]{1,0:T(8,128)(2,1)S(1)}, u32[]{:S(2)}, u32[]{:S(2)}) collective-permute-start(bf16[512,1024]{1,0:T(8,128)(2,1)S(1)} %broadcast_select_fusion), channel_id=1, source_target_pairs={{0,2},{1,3},{6,4},{7,5},{8,10},{9,11},{14,12},{15,13},{16,18},{17,... | collective-permute-start | bytes 3145736 | tf_op jit(solution)/shard_map/ppermute | solution.py:240
  256.4 34.9 %collective-permute-start.24 = (bf16[512,1024]{1,0:T(8,128)(2,1)S(1)}, bf16[512,1024]{1,0:T(8,128)(2,1)S(1)}, u32[]{:S(2)}, u32[]{:S(2)}) collective-permute-start(bf16[512,1024]{1,0:T(8,128)(2,1)S(1)} %get-tuple-element.71), channel_id=1, source_target_pairs={{2,0},{3,1},{4,2},{5,3},{6,4},{7,5},{10,8},{11,9},{12,10},{13,11},... | collective-permute-start | bytes 3145736 | tf_op jit(solution)/shard_map/ppermute | solution.py:240
  257.7 44.7 %collective-permute-start.23 = (bf16[512,1024]{1,0:T(8,128)(2,1)S(1)}, bf16[512,1024]{1,0:T(8,128)(2,1)S(1)}, u32[]{:S(2)}, u32[]{:S(2)}) collective-permute-start(bf16[512,1024]{1,0:T(8,128)(2,1)S(1)} %get-tuple-element.70), channel_id=1, source_target_pairs={{0,2},{1,3},{2,4},{3,5},{4,6},{5,7},{8,10},{9,11},{10,12},{11,13},... | collective-permute-start | bytes 3145736 | tf_op jit(solution)/shard_map/ppermute | solution.py:240
  280.4 33.3 %collective-permute-start.28 = (bf16[512,512]{1,0:T(8,128)(2,1)S(1)}, bf16[512,512]{1,0:T(8,128)(2,1)S(1)}, u32[]{:S(2)}, u32[]{:S(2)}) collective-permute-start(bf16[512,512]{1,0:T(8,128)(2,1)S(1)} %get-tuple-element.78), channel_id=1, source_target_pairs={{0,5},{1,4},{2,7},{3,6},{4,1},{5,0},{6,3},{7,2},{8,13},{9,12},{10,... | collective-permute-start | bytes 1572872 | tf_op jit(solution)/shard_map/ppermute | solution.py:273
  303.0 10.6 %collective-permute-start.27 = (bf16[512,512]{1,0:T(8,128)(2,1)S(1)}, bf16[512,512]{1,0:T(8,128)(2,1)S(1)}, u32[]{:S(2)}, u32[]{:S(2)}) collective-permute-start(bf16[512,512]{1,0:T(8,128)(2,1)S(1)} %select_convert_fusion), channel_id=1, source_target_pairs={{0,1},{1,0},{2,3},{3,2},{4,5},{5,4},{6,7},{7,6},{8,9},{9,8},{10,11... | collective-permute-start | bytes 1572872 | tf_op jit(solution)/shard_map/ppermute | solution.py:234
  303.6 28.1 %collective-permute-start.26 = (bf16[512,512]{1,0:T(8,128)(2,1)S(1)}, bf16[512,512]{1,0:T(8,128)(2,1)S(1)}, u32[]{:S(2)}, u32[]{:S(2)}) collective-permute-start(bf16[512,512]{1,0:T(8,128)(2,1)S(1)} %get-tuple-element.77), channel_id=1, source_target_pairs={{4,0},{5,1},{6,2},{7,3},{0,4},{1,5},{2,6},{3,7},{12,8},{13,9},{14,... | collective-permute-start | bytes 1572872 | tf_op jit(solution)/shard_map/ppermute | solution.py:240
  (2 other events, 2.0 us)
